TPU v7x, 32 devices: a whole 2x2x4 slice. The times are simulated.
32 devices in a mesh: sub: 8 (over y, x, core), alt: 4 (over z).
Axes of the slice: x: 2, y: 2, z: 4, core: 2. Of those that a mesh axis runs over, the one named last changes fastest.
Arguments:
- cotangent: bfloat16 [4096, 1024], P('alt', 'sub'), may hold values from -180 to 180, as said below
- amplitude: bfloat16 [1024, 1024], P('alt', 'sub'), may hold values from 0.19921875 to 1
- phase: float32 [1024, 1024], P('alt', 'sub'), may hold values from -6 to 6
- position: float32 [2, 1024], P(None, 'sub'), may hold values from -1 to 1
- profile: float32 [8], P('alt'), may hold values from 0.35 to 15, as said below
- alt_weight: float32 [8], P('alt'), may hold values from 0.3 to 3
Outputs:
- phase_grad: float32 [1024, 1024], P('alt', 'sub')
- profile_grad: float32 [8], P('alt')
Inputs may be any that keep to these rules, and one draw needn't show every extreme that they name: `cotangent`: cotangent values of varying scale per subaperture. `profile`: positive sodium densities.
All inputs are finite; a program needn't handle non-finite values.
Results may differ from a plain program's by a relative error of at most 0.0003.
Values may be sent and summed in bfloat16 or wider, within the bound.
No kernel may reach another device: no remote copies, remote signals or barrier semaphores. Data moves between devices by JAX's collectives and lax.ppermute only.
A program may use at most 64 MiB of HBM per device.

v0:
```python
import jax
import jax.numpy as jnp
from jax import lax
from jax.sharding import PartitionSpec as P

P_SIZE = 32
FIELD = 64


ELONG = 0.75


def dft_tables(size_pupil, size_field):
    rows = jnp.arange(size_field, dtype=jnp.int32)[:, None]
    cols = jnp.arange(size_pupil, dtype=jnp.int32)[None, :]
    angle = 2.0 * jnp.pi / size_field * (rows * cols % size_field).astype(jnp.float32)
    return (jnp.cos(angle), -jnp.sin(angle))


def spot_image(psi, ampl, table_re, table_im, size_pupil):
    high = lax.Precision.HIGHEST
    field_re = ampl * jnp.cos(psi)
    field_im = ampl * jnp.sin(psi)
    first_re = jnp.einsum("kj,ajs->aks", table_re, field_re, precision=high) - jnp.einsum(
        "kj,ajs->aks", table_im, field_im, precision=high
    )
    first_im = jnp.einsum("kj,ajs->aks", table_re, field_im, precision=high) + jnp.einsum(
        "kj,ajs->aks", table_im, field_re, precision=high
    )
    final_re = jnp.einsum("ka,ams->kms", table_re, first_re, precision=high) - jnp.einsum(
        "ka,ams->kms", table_im, first_im, precision=high
    )
    final_im = jnp.einsum("ka,ams->kms", table_re, first_im, precision=high) + jnp.einsum(
        "ka,ams->kms", table_im, first_re, precision=high
    )
    return (final_re * final_re + final_im * final_im) / (size_pupil * size_pupil)


def run_bins(
    grad_rows, ampl_rows, phase_rows, coords_xy, densities, weights, first_bin, nbins_all, group
):
    count = phase_rows.shape[1]
    total_bins = densities.shape[0]
    blocks = total_bins // group
    grad_img = grad_rows.astype(jnp.float32).reshape(FIELD, FIELD, count)
    ampl = ampl_rows.astype(jnp.float32).reshape(P_SIZE, P_SIZE, count)
    phases = phase_rows.reshape(P_SIZE, P_SIZE, count)
    table_re, table_im = dft_tables(P_SIZE, FIELD)
    coord = jnp.arange(P_SIZE, dtype=jnp.float32) - (P_SIZE - 1) / 2.0
    tilt = (
        coord[None, :, None] * coords_xy[0][None, None, :]
        + coord[:, None, None] * coords_xy[1][None, None, :]
    )
    wide = group * count
    phases_wide = phases[:, :, None, :].reshape(P_SIZE, P_SIZE, wide)
    tilt_wide = tilt[:, :, None, :].reshape(P_SIZE, P_SIZE, wide)
    ampl_wide = ampl[:, :, None, :].reshape(P_SIZE, P_SIZE, wide)
    dens_blocks = densities.reshape(blocks, group)
    weight_blocks = weights.reshape(blocks, group)

    def step(accum, block):
        offsets = block * group + jnp.arange(group, dtype=jnp.int32)
        global_bin = first_bin + offsets
        kappa = ELONG * (2.0 * global_bin.astype(jnp.float32) / (nbins_all - 1) - 1.0)
        kappa_wide = jnp.broadcast_to(kappa[:, None], (group, count)).reshape(wide)
        psi = phases_wide + kappa_wide[None, None, :] * tilt_wide
        intensity, pull = jax.vjp(
            lambda value: spot_image(value, ampl_wide, table_re, table_im, P_SIZE), psi
        )
        scale = dens_blocks[block] * weight_blocks[block]
        seed = (grad_img[:, :, None, :] * scale[None, None, :, None]).reshape(FIELD, FIELD, wide)
        (dpsi,) = pull(seed)
        stat = jnp.sum(
            grad_img[:, :, None, :] * intensity.reshape(FIELD, FIELD, group, count), axis=(0, 1, 3)
        )
        return (accum + jnp.sum(dpsi.reshape(P_SIZE, P_SIZE, group, count), axis=2), stat)

    accum, stats = lax.scan(
        step, jnp.zeros((P_SIZE, P_SIZE, count), jnp.float32), jnp.arange(blocks, dtype=jnp.int32)
    )
    return (accum.reshape(P_SIZE * P_SIZE, count), stats.reshape(total_bins))


def local(cotangent, amplitude, phase, position, profile, alt_weight):
    n_alt = lax.axis_size("alt")
    nsub_all = lax.axis_size("sub") * phase.shape[1]
    local_bins = profile.shape[0]
    nbins_all = n_alt * local_bins
    first_bin = lax.axis_index("alt") * local_bins
    grad_rows, ampl_rows = (
        lax.all_gather(cotangent, "alt", axis=0, tiled=True),
        lax.all_gather(amplitude, "alt", axis=0, tiled=True),
    )
    phase_rows = lax.all_gather(phase, "alt", axis=0, tiled=True)
    accum, stats = run_bins(
        grad_rows, ampl_rows, phase_rows, position, profile, alt_weight, first_bin, nbins_all, 1
    )
    partial_value = lax.psum_scatter(accum, "alt", scatter_dimension=0, tiled=True)
    total = lax.psum(jnp.sum(profile), "alt")
    mine = lax.psum(stats, "sub")
    centre = lax.psum(jnp.sum(profile * alt_weight * mine), "alt")
    phase_grad = partial_value / total
    profile_grad = (alt_weight * mine / total - centre / (total * total)) / nsub_all
    return (phase_grad, profile_grad)


def solution(mesh):
    placed = (P("alt", "sub"), P("alt", "sub"), P("alt", "sub"), P(None, "sub"), P("alt"), P("alt"))
    return jax.shard_map(
        local, mesh=mesh, in_specs=placed, out_specs=(P("alt", "sub"), P("alt")), check_vma=False
    )
```

profile of v0, /device:TPU:0, one launch (start us, length us, event | category | flops | bytes accessed | tf_op | source)
XLA Modules:
  0.0 202.0 jit_solution(5432399782633211105)
XLA Ops:
  7.2 0.0 all-gather.2.cloned.1.call-start
  7.2 0.7 all-gather.2.cloned.1.call-update
  7.9 0.0 reduce-scatter.2.cloned.1.call-start
  8.0 16.5 %all_gather.10 = bf16[1024,128]{1,0:T(8,128)(2,1)S(1)} all-gather(bf16[256,128]{1,0:T(8,128)(2,1)} %param.9), channel_id=1, replica_groups=mesh['sub'=8,'alt'=4] {'alt'}, dimensions={0}, use_global_device_ids=true | all-gather | bytes 327680 | tf_op jit(solution)/shard_map/all_gather | solution.py:92
  24.5 0.0 copy-start.5
  24.5 0.0 copy-start.6
  24.5 23.3 %all_gather.9 = f32[1024,128]{1,0:T(8,128)S(1)} all-gather(f32[256,128]{1,0:T(8,128)} %param.10), channel_id=1, replica_groups=mesh['sub'=8,'alt'=4] {'alt'}, dimensions={0}, use_global_device_ids=true | all-gather | bytes 655360 | tf_op jit(solution)/shard_map/all_gather | solution.py:94
  47.8 0.8 slice_bitcast_fusion.1
  48.6 0.1 broadcast_multiply_fusion.1
  48.6 1.0 all-gather.2.cloned.1.call-done
  49.6 1.4 convert_element_type.44
  51.0 0.0 copy-done.5
  51.0 0.0 copy-done.6
  51.0 113.2 %while.16 = (s32[]{:T(128)}, f32[32,32,128]{2,1,0:T(8,128)}, f32[2,1]{0,1:T(1,128)S(1)}, s32[]{:T(128)}, s32[2]{0:T(128)S(1)}, /*index=5*/f32[32,32,128]{2,1,0:T...) while((s32[]{:T(128)}, f32[32,32,128]{2,1,0:T(8,128)}, ...), condition=%wide.region_2.3_spmd.clone.clone, body=%wide.region_0.2_spmd.clone.clone.sunk | while | flops 2435006464 | bytes 95617512 | solution.py:78
  51.3 0.7 dynamic_slice.30
  54.5 0.6 constant_dynamic-slice_fusion.3
  55.1 1.2 fusion.228
  56.3 2.7 %fusion.224 = f32[32,128,64]{1,2,0:T(8,128)S(1)} fusion(f32[32,32,128]{2,1,0:T(8,128)S(1)} %get-tuple-element.460, f32[32,32,128]{2,1,0:T(8,128)S(1)} %get-tuple-element.459, f32[32,128]{1,0:T(8,128)S(1)} %get-tuple-element.464, f32[32,128]{1,0:T(8,128)S(1)} %get-tuple-element.465, f32[]{:T(128)} %bitcast.156), kind=kOutput, calls=%fused_computation.52.clone.1 | convolution fusion | flops 101216256 | bytes 2129924 | tf_op jit(solution)/shard_map/while/body/eval_jaxpr/jvp(kj,ajs->aks)/dot_general | solution.py:27
  59.1 2.7 %fusion.225 = f32[32,64,128]{2,1,0:T(8,128)S(1)} fusion(f32[32,128,64]{1,2,0:T(8,128)S(1)} %fusion.224, f32[32,32,128]{2,1,0:T(8,128)S(1)} %get-tuple-element.460, f32[32,32,128]{2,1,0:T(8,128)S(1)} %get-tuple-element.459, f32[32,128]{1,0:T(8,128)S(1)} %get-tuple-element.464, f32[32,128]{1,0:T(8,128)S(1)} %get-tuple-element.465, f32[]{:T(128)} %bitcast.156), kind=kOutput, calls=%fused_computation.19.clone.1 | convolution fusion | flops 101480448 | bytes 3178500 | tf_op jit(solution)/shard_map/while/body/eval_jaxpr/jvp(kj,ajs->aks)/dot_general | solution.py:27
  61.8 2.7 %fusion.221 = f32[32,128,64]{1,2,0:T(8,128)S(1)} fusion(f32[32,32,128]{2,1,0:T(8,128)S(1)} %get-tuple-element.460, f32[32,32,128]{2,1,0:T(8,128)S(1)} %get-tuple-element.459, f32[32,128]{1,0:T(8,128)S(1)} %get-tuple-element.464, f32[32,128]{1,0:T(8,128)S(1)} %get-tuple-element.465, f32[]{:T(128)} %bitcast.156), kind=kOutput, calls=%fused_computation.51.clone.1 | convolution fusion | flops 101216256 | bytes 2129924 | tf_op jit(solution)/shard_map/while/body/eval_jaxpr/jvp(kj,ajs->aks)/dot_general | solution.py:24
  64.5 2.8 %fusion.222 = f32[32,64,128]{2,1,0:T(8,128)S(1)} fusion(f32[32,128,64]{1,2,0:T(8,128)S(1)} %fusion.221, f32[32,32,128]{2,1,0:T(8,128)S(1)} %get-tuple-element.460, f32[32,32,128]{2,1,0:T(8,128)S(1)} %get-tuple-element.459, f32[32,128]{1,0:T(8,128)S(1)} %get-tuple-element.464, f32[32,128]{1,0:T(8,128)S(1)} %get-tuple-element.465, f32[]{:T(128)} %bitcast.156), kind=kOutput, calls=%fused_computation.17.clone.1 | convolution fusion | flops 101480448 | bytes 3178500 | tf_op jit(solution)/shard_map/while/body/eval_jaxpr/jvp(kj,ajs->aks)/dot_general | solution.py:24
  67.3 3.1 %fusion.223 = f32[64,128,64]{1,2,0:T(8,128)S(1)} fusion(f32[32,64,128]{2,1,0:T(8,128)S(1)} %fusion.222), kind=kOutput, calls=%fused_computation.37.clone.1 | convolution fusion | flops 201355264 | bytes 3145728 | tf_op jit(solution)/shard_map/while/body/eval_jaxpr/jvp(ka,ams->kms)/dot_general | solution.py:30
  70.4 2.6 %convolution_subtract_fusion.3 = f32[64,128,64]{1,2,0:T(8,128)S(1)} fusion(f32[64,128,64]{1,2,0:T(8,128)S(1)} %fusion.223, f32[32,64,128]{2,1,0:T(8,128)S(1)} %fusion.225), kind=kOutput, calls=%fused_computation.10.clone.1 | convolution fusion | flops 201881600 | bytes 5242880 | tf_op jit(solution)/shard_map/while/body/eval_jaxpr/jvp(ka,ams->kms)/dot_general | solution.py:30
  73.0 0.0 copy-start
  73.0 2.5 %fusion.226 = f32[64,128,64]{1,2,0:T(8,128)S(1)} fusion(f32[32,64,128]{2,1,0:T(8,128)S(1)} %fusion.225), kind=kOutput, calls=%fused_computation.41.clone.1 | convolution fusion | flops 201355264 | bytes 3145728 | tf_op jit(solution)/shard_map/while/body/eval_jaxpr/jvp(ka,ams->kms)/dot_general | solution.py:33
  75.6 5.7 %fusion.227 = (f32[]{:T(128)}, f32[64,128,64]{1,2,0:T(8,128)}) fusion(f32[64,128,64]{1,2,0:T(8,128)S(1)} %convolution_subtract_fusion.3, f32[64,64,128]{2,1,0:T(8,128)S(1)} %bitcast.161, f32[64,128,64]{1,2,0:T(8,128)S(1)} %fusion.226, f32[32,64,128]{2,1,0:T(8,128)S(1)} %fusion.222), kind=kOutput, calls=%fused_computation.4.clone.1 | convolution fusion | flops 205027328 | bytes 9437188 | tf_op jit(solution)/shard_map/while/body/eval_jaxpr/jvp(ka,ams->kms)/dot_general | solution.py:33
  81.3 0.8 dynamic_update_slice.10
  82.1 5.0 %fusion.232 = f32[64,128,32]{1,2,0:T(8,128)S(1)} fusion(f32[64,128,64]{1,2,0:T(8,128)} %get-tuple-element.414, f32[64,64,128]{2,1,0:T(8,128)S(1)} %bitcast.162, f32[]{:T(128)} %bitcast.159), kind=kOutput, calls=%fused_computation.47.clone.1 | convolution fusion | flops 203454464 | bytes 5242884 | tf_op jit(solution)/shard_map/while/body/eval_jaxpr/transpose(jvp(ka,ams->kms))/dot_general | solution.py:33
  87.1 3.5 %fusion.229 = f32[64,128,32]{1,2,0:T(8,128)S(1)} fusion(f32[64,128,64]{1,2,0:T(8,128)S(1)} %copy-done.2, f32[64,64,128]{2,1,0:T(8,128)S(1)} %bitcast.163, f32[]{:T(128)} %bitcast.159), kind=kOutput, calls=%fused_computation.48.clone.1 | convolution fusion | flops 203452416 | bytes 5242884 | tf_op jit(solution)/shard_map/while/body/eval_jaxpr/transpose(jvp(ka,ams->kms))/dot_general | solution.py:33
  90.6 3.3 %fusion.230 = f32[32,128,64]{1,0,2:T(8,128)S(1)} fusion(f32[64,128,32]{1,2,0:T(8,128)S(1)} %fusion.229, f32[64,128,64]{1,2,0:T(8,128)S(1)} %copy-done.1, f32[64,64,128]{2,1,0:T(8,128)S(1)} %bitcast.164, f32[]{:T(128)} %bitcast.159), kind=kOutput, calls=%fused_computation.13.clone.1 | convolution fusion | flops 204240896 | bytes 6291460 | tf_op jit(solution)/shard_map/while/body/eval_jaxpr/transpose(jvp(ka,ams->kms))/dot_general | solution.py:30
  93.9 3.4 %fusion.233 = (f32[32,128,64]{1,0,2:T(8,128)S(1)}, f32[32,128,64]{1,0,2:T(8,128)S(1)}) fusion(f32[64,128,32]{1,2,0:T(8,128)S(1)} %fusion.232, f32[64,128,64]{1,2,0:T(8,128)S(1)} %copy-done.1, f32[64,64,128]{2,1,0:T(8,128)S(1)} %bitcast.165, f32[]{:T(128)} %bitcast.159), kind=kOutput, calls=%fused_computation.159.clone.1 | convolution fusion | flops 203976704 | bytes 7340036 | tf_op jit(solution)/shard_map/while/body/eval_jaxpr/transpose(jvp(ka,ams->kms))/dot_general | solution.py:30
  97.3 1.5 fusion.235
  98.8 1.3 fusion.231
  100.2 3.0 %fusion.234 = f32[32,32,128]{2,1,0:T(8,128)S(1)} fusion(f32[32,32,128]{2,1,0:T(8,128)S(1)} %get-tuple-element.460, f32[32,128,32]{1,2,0:T(8,128)S(1)} %fusion.231, f32[32,128,64]{1,0,2:T(8,128)S(1)} %get-tuple-element.415, f32[32,32,128]{2,1,0:T(8,128)S(1)} %get-tuple-element.459, f32[32,128]{1,0:T(8,128)S(1)} %get-tuple-element.464, ...), kind=kOutput, calls=%fused_computation.24.clone.1 | convolution fusion | flops 101609472 | bytes 3178500 | tf_op jit(solution)/shard_map/while/body/eval_jaxpr/transpose(jvp(kj,ajs->aks))/dot_general | solution.py:24
  103.2 3.0 %fusion.236 = f32[32,32,128]{2,1,0:T(8,128)S(1)} fusion(f32[32,32,128]{2,1,0:T(8,128)S(1)} %fusion.234, f32[32,32,128]{2,1,0:T(8,128)S(1)} %get-tuple-element.460, f32[32,128,32]{1,2,0:T(8,128)S(1)} %fusion.235, f32[32,128,64]{1,0,2:T(8,128)S(1)} %get-tuple-element.416, f32[32,32,128]{2,1,0:T(8,128)S(1)} %copy-done.3, ...), kind=kOutput, calls=%fused_computation.30.clone.1 | convolution fusion | flops 101873664 | bytes 4227077 | tf_op jit(solution)/shard_map/while/body/eval_jaxpr/transpose(jvp(kj,ajs->aks))/dot_general | solution.py:24
  106.2 0.8 copy-done.4
  107.4 0.7 dynamic_slice.30
  110.6 0.6 constant_dynamic-slice_fusion.3
  111.2 1.2 fusion.228
  112.4 2.7 %fusion.224 = f32[32,128,64]{1,2,0:T(8,128)S(1)} fusion(f32[32,32,128]{2,1,0:T(8,128)S(1)} %get-tuple-element.460, f32[32,32,128]{2,1,0:T(8,128)S(1)} %get-tuple-element.459, f32[32,128]{1,0:T(8,128)S(1)} %get-tuple-element.464, f32[32,128]{1,0:T(8,128)S(1)} %get-tuple-element.465, f32[]{:T(128)} %bitcast.156), kind=kOutput, calls=%fused_computation.52.clone.1 | convolution fusion | flops 101216256 | bytes 2129924 | tf_op jit(solution)/shard_map/while/body/eval_jaxpr/jvp(kj,ajs->aks)/dot_general | solution.py:27
  115.2 2.7 %fusion.225 = f32[32,64,128]{2,1,0:T(8,128)S(1)} fusion(f32[32,128,64]{1,2,0:T(8,128)S(1)} %fusion.224, f32[32,32,128]{2,1,0:T(8,128)S(1)} %get-tuple-element.460, f32[32,32,128]{2,1,0:T(8,128)S(1)} %get-tuple-element.459, f32[32,128]{1,0:T(8,128)S(1)} %get-tuple-element.464, f32[32,128]{1,0:T(8,128)S(1)} %get-tuple-element.465, f32[]{:T(128)} %bitcast.156), kind=kOutput, calls=%fused_computation.19.clone.1 | convolution fusion | flops 101480448 | bytes 3178500 | tf_op jit(solution)/shard_map/while/body/eval_jaxpr/jvp(kj,ajs->aks)/dot_general | solution.py:27
  117.9 2.7 %fusion.221 = f32[32,128,64]{1,2,0:T(8,128)S(1)} fusion(f32[32,32,128]{2,1,0:T(8,128)S(1)} %get-tuple-element.460, f32[32,32,128]{2,1,0:T(8,128)S(1)} %get-tuple-element.459, f32[32,128]{1,0:T(8,128)S(1)} %get-tuple-element.464, f32[32,128]{1,0:T(8,128)S(1)} %get-tuple-element.465, f32[]{:T(128)} %bitcast.156), kind=kOutput, calls=%fused_computation.51.clone.1 | convolution fusion | flops 101216256 | bytes 2129924 | tf_op jit(solution)/shard_map/while/body/eval_jaxpr/jvp(kj,ajs->aks)/dot_general | solution.py:24
  120.6 2.8 %fusion.222 = f32[32,64,128]{2,1,0:T(8,128)S(1)} fusion(f32[32,128,64]{1,2,0:T(8,128)S(1)} %fusion.221, f32[32,32,128]{2,1,0:T(8,128)S(1)} %get-tuple-element.460, f32[32,32,128]{2,1,0:T(8,128)S(1)} %get-tuple-element.459, f32[32,128]{1,0:T(8,128)S(1)} %get-tuple-element.464, f32[32,128]{1,0:T(8,128)S(1)} %get-tuple-element.465, f32[]{:T(128)} %bitcast.156), kind=kOutput, calls=%fused_computation.17.clone.1 | convolution fusion | flops 101480448 | bytes 3178500 | tf_op jit(solution)/shard_map/while/body/eval_jaxpr/jvp(kj,ajs->aks)/dot_general | solution.py:24
  123.4 2.7 %fusion.223 = f32[64,128,64]{1,2,0:T(8,128)S(1)} fusion(f32[32,64,128]{2,1,0:T(8,128)S(1)} %fusion.222), kind=kOutput, calls=%fused_computation.37.clone.1 | convolution fusion | flops 201355264 | bytes 3145728 | tf_op jit(solution)/shard_map/while/body/eval_jaxpr/jvp(ka,ams->kms)/dot_general | solution.py:30
  126.1 2.6 %convolution_subtract_fusion.3 = f32[64,128,64]{1,2,0:T(8,128)S(1)} fusion(f32[64,128,64]{1,2,0:T(8,128)S(1)} %fusion.223, f32[32,64,128]{2,1,0:T(8,128)S(1)} %fusion.225), kind=kOutput, calls=%fused_computation.10.clone.1 | convolution fusion | flops 201881600 | bytes 5242880 | tf_op jit(solution)/shard_map/while/body/eval_jaxpr/jvp(ka,ams->kms)/dot_general | solution.py:30
  128.7 2.5 %fusion.226 = f32[64,128,64]{1,2,0:T(8,128)S(1)} fusion(f32[32,64,128]{2,1,0:T(8,128)S(1)} %fusion.225), kind=kOutput, calls=%fused_computation.41.clone.1 | convolution fusion | flops 201355264 | bytes 3145728 | tf_op jit(solution)/shard_map/while/body/eval_jaxpr/jvp(ka,ams->kms)/dot_general | solution.py:33
  131.2 5.7 %fusion.227 = (f32[]{:T(128)}, f32[64,128,64]{1,2,0:T(8,128)}) fusion(f32[64,128,64]{1,2,0:T(8,128)S(1)} %convolution_subtract_fusion.3, f32[64,64,128]{2,1,0:T(8,128)S(1)} %bitcast.161, f32[64,128,64]{1,2,0:T(8,128)S(1)} %fusion.226, f32[32,64,128]{2,1,0:T(8,128)S(1)} %fusion.222), kind=kOutput, calls=%fused_computation.4.clone.1 | convolution fusion | flops 205027328 | bytes 9437188 | tf_op jit(solution)/shard_map/while/body/eval_jaxpr/jvp(ka,ams->kms)/dot_general | solution.py:33
  137.0 0.9 dynamic_update_slice.10
  137.9 5.0 %fusion.232 = f32[64,128,32]{1,2,0:T(8,128)S(1)} fusion(f32[64,128,64]{1,2,0:T(8,128)} %get-tuple-element.414, f32[64,64,128]{2,1,0:T(8,128)S(1)} %bitcast.162, f32[]{:T(128)} %bitcast.159), kind=kOutput, calls=%fused_computation.47.clone.1 | convolution fusion | flops 203454464 | bytes 5242884 | tf_op jit(solution)/shard_map/while/body/eval_jaxpr/transpose(jvp(ka,ams->kms))/dot_general | solution.py:33
  142.9 3.5 %fusion.229 = f32[64,128,32]{1,2,0:T(8,128)S(1)} fusion(f32[64,128,64]{1,2,0:T(8,128)S(1)} %copy-done.2, f32[64,64,128]{2,1,0:T(8,128)S(1)} %bitcast.163, f32[]{:T(128)} %bitcast.159), kind=kOutput, calls=%fused_computation.48.clone.1 | convolution fusion | flops 203452416 | bytes 5242884 | tf_op jit(solution)/shard_map/while/body/eval_jaxpr/transpose(jvp(ka,ams->kms))/dot_general | solution.py:33
  146.4 3.3 %fusion.230 = f32[32,128,64]{1,0,2:T(8,128)S(1)} fusion(f32[64,128,32]{1,2,0:T(8,128)S(1)} %fusion.229, f32[64,128,64]{1,2,0:T(8,128)S(1)} %copy-done.1, f32[64,64,128]{2,1,0:T(8,128)S(1)} %bitcast.164, f32[]{:T(128)} %bitcast.159), kind=kOutput, calls=%fused_computation.13.clone.1 | convolution fusion | flops 204240896 | bytes 6291460 | tf_op jit(solution)/shard_map/while/body/eval_jaxpr/transpose(jvp(ka,ams->kms))/dot_general | solution.py:30
  149.7 3.4 %fusion.233 = (f32[32,128,64]{1,0,2:T(8,128)S(1)}, f32[32,128,64]{1,0,2:T(8,128)S(1)}) fusion(f32[64,128,32]{1,2,0:T(8,128)S(1)} %fusion.232, f32[64,128,64]{1,2,0:T(8,128)S(1)} %copy-done.1, f32[64,64,128]{2,1,0:T(8,128)S(1)} %bitcast.165, f32[]{:T(128)} %bitcast.159), kind=kOutput, calls=%fused_computation.159.clone.1 | convolution fusion | flops 203976704 | bytes 7340036 | tf_op jit(solution)/shard_map/while/body/eval_jaxpr/transpose(jvp(ka,ams->kms))/dot_general | solution.py:30
  153.1 1.7 fusion.235
  154.8 1.3 fusion.231
  156.1 3.0 %fusion.234 = f32[32,32,128]{2,1,0:T(8,128)S(1)} fusion(f32[32,32,128]{2,1,0:T(8,128)S(1)} %get-tuple-element.460, f32[32,128,32]{1,2,0:T(8,128)S(1)} %fusion.231, f32[32,128,64]{1,0,2:T(8,128)S(1)} %get-tuple-element.415, f32[32,32,128]{2,1,0:T(8,128)S(1)} %get-tuple-element.459, f32[32,128]{1,0:T(8,128)S(1)} %get-tuple-element.464, ...), kind=kOutput, calls=%fused_computation.24.clone.1 | convolution fusion | flops 101609472 | bytes 3178500 | tf_op jit(solution)/shard_map/while/body/eval_jaxpr/transpose(jvp(kj,ajs->aks))/dot_general | solution.py:24
  159.1 0.0 copy-done.3
  159.1 3.0 %fusion.236 = f32[32,32,128]{2,1,0:T(8,128)S(1)} fusion(f32[32,32,128]{2,1,0:T(8,128)S(1)} %fusion.234, f32[32,32,128]{2,1,0:T(8,128)S(1)} %get-tuple-element.460, f32[32,128,32]{1,2,0:T(8,128)S(1)} %fusion.235, f32[32,128,64]{1,0,2:T(8,128)S(1)} %get-tuple-element.416, f32[32,32,128]{2,1,0:T(8,128)S(1)} %copy-done.3, ...), kind=kOutput, calls=%fused_computation.30.clone.1 | convolution fusion | flops 101873664 | bytes 4227077 | tf_op jit(solution)/shard_map/while/body/eval_jaxpr/transpose(jvp(kj,ajs->aks))/dot_general | solution.py:24
  162.2 0.8 copy-done.4
  164.2 0.0 reduce-scatter.2.cloned.1.call-update
  164.3 14.2 %psum.22 = f32[2]{0:T(128)S(1)} all-reduce(f32[2]{0:T(128)S(1)} %bitcast.174), channel_id=1, replica_groups=mesh['sub'=8,'alt'=4] {'sub'}, use_global_device_ids=true, to_apply=%region_6.7 | all-reduce | flops 2 | bytes 16 | tf_op jit(solution)/shard_map/psum | solution.py:100
  178.5 0.6 multiply_reduce_fusion
  179.1 10.5 %all-reduce = (f32[]{:T(128)}, f32[]{:T(128)}) all-reduce(f32[]{:T(128)} %get-tuple-element.302, f32[]{:T(128)} %get-tuple-element.301), channel_id=1, replica_groups=mesh['sub'=8,'alt'=4] {'alt'}, use_global_device_ids=true, to_apply=%region_5.6 | all-reduce | flops 2 | bytes 16 | tf_op jit(solution)/shard_map/psum | solution.py:99
  191.5 1.2 subtract_multiply_fusion
  192.7 2.2 %broadcast_divide_fusion = f32[256,128]{1,0:T(8,128)} fusion(f32[256,128]{1,0:T(8,128)} %reduce-scatter.2.cloned.1.call-done, f32[]{:T(128)} %get-tuple-element.327), kind=kLoop, calls=%fused_computation.150 | loop fusion | flops 32768 | bytes 262148 | tf_op jit(solution)/shard_map/div | solution.py:102
  (22 shorter events, 0.1 us)
Async XLA Ops:
  7.2 42.5 %all-gather.2.cloned.1.call-start = ((), (), s32[]{:S(2)}) async-start(), calls=%async_computation.1 | async-start | bytes 1310720 | tf_op jit(solution)/shard_map/all_gather | solution.py:91
  7.9 184.8 %reduce-scatter.2.cloned.1.call-start = ((), (), s32[]{:S(2)}) async-start(), calls=%async_computation.2 | async-start | bytes 655360 | tf_op jit(solution)/shard_map/reduce_scatter | solution.py:98
  24.5 26.5 %copy-start.5 = (f32[2]{0:T(128)S(1)}, f32[2]{0:T(128)}, u32[]{:S(2)}) copy-start(f32[2]{0:T(128)} %param.12) | copy-start | bytes 28
  24.5 26.5 %copy-start.6 = (f32[2]{0:T(128)S(1)}, f32[2]{0:T(128)}, u32[]{:S(2)}) copy-start(f32[2]{0:T(128)} %param.13) | copy-start | bytes 28
  73.0 8.2 %copy-start = (f32[64,128,64]{1,2,0:T(8,128)}, f32[64,128,64]{1,2,0:T(8,128)S(1)}, u32[]{:S(2)}) copy-start(f32[64,128,64]{1,2,0:T(8,128)S(1)} %convolution_subtract_fusion.3) | copy-start | bytes 6291460 | tf_op jit(solution)/shard_map/while
  82.1 5.0 %copy-start.2 = (f32[64,128,64]{1,2,0:T(8,128)S(1)}, f32[64,128,64]{1,2,0:T(8,128)}, u32[]{:S(2)}) copy-start(f32[64,128,64]{1,2,0:T(8,128)} %get-tuple-element.414) | copy-start | bytes 6291460 | tf_op jit(solution)/shard_map/while
  87.1 3.5 %copy-start.1 = (f32[64,128,64]{1,2,0:T(8,128)S(1)}, f32[64,128,64]{1,2,0:T(8,128)}, u32[]{:S(2)}) copy-start(f32[64,128,64]{1,2,0:T(8,128)} %copy-done) | copy-start | bytes 6291460 | tf_op jit(solution)/shard_map/while
  98.8 4.3 %copy-start.3 = (f32[32,32,128]{2,1,0:T(8,128)S(1)}, f32[32,32,128]{2,1,0:T(8,128)}, u32[]{:S(2)}) copy-start(f32[32,32,128]{2,1,0:T(8,128)} %get-tuple-element.437) | copy-start | bytes 1572868 | tf_op jit(solution)/shard_map/while
  106.2 0.8 copy-start.4
  128.7 8.2 %copy-start = (f32[64,128,64]{1,2,0:T(8,128)}, f32[64,128,64]{1,2,0:T(8,128)S(1)}, u32[]{:S(2)}) copy-start(f32[64,128,64]{1,2,0:T(8,128)S(1)} %convolution_subtract_fusion.3) | copy-start | bytes 6291460 | tf_op jit(solution)/shard_map/while
  137.9 5.0 %copy-start.2 = (f32[64,128,64]{1,2,0:T(8,128)S(1)}, f32[64,128,64]{1,2,0:T(8,128)}, u32[]{:S(2)}) copy-start(f32[64,128,64]{1,2,0:T(8,128)} %get-tuple-element.414) | copy-start | bytes 6291460 | tf_op jit(solution)/shard_map/while
  142.9 3.5 %copy-start.1 = (f32[64,128,64]{1,2,0:T(8,128)S(1)}, f32[64,128,64]{1,2,0:T(8,128)}, u32[]{:S(2)}) copy-start(f32[64,128,64]{1,2,0:T(8,128)} %copy-done) | copy-start | bytes 6291460 | tf_op jit(solution)/shard_map/while
  154.8 4.3 %copy-start.3 = (f32[32,32,128]{2,1,0:T(8,128)S(1)}, f32[32,32,128]{2,1,0:T(8,128)}, u32[]{:S(2)}) copy-start(f32[32,32,128]{2,1,0:T(8,128)} %get-tuple-element.437) | copy-start | bytes 1572868 | tf_op jit(solution)/shard_map/while
  162.2 0.8 copy-start.4
Sparse Core Ops, SparseCore 0:
  9.6 40.0 all-gather.1
  164.4 20.8 reduce-scatter.1
where the time goes:
time: 204 us; the launch traced here: 202 us
  matrix products  97.4 us (48%)
  blocking collectives  64.5 us (32%)
  between operations  16.3 us (8%)
  other arithmetic  7.9 us (4%)
  loops' own time  7.44 us (4%)
  local copies, waits for them, and re-layouts  6.64 us (3%)
    all_gather x1, blocking collectives, local(): phase_rows = lax.all_gather(phase, 'alt', axis=0, tiled=True)  23.3 us
    dot_general x4, matrix products, spot_image(): jnp.einsum('ka,ams->kms', table_im, first_re, precision=high)  21.3 us
    all_gather x1, blocking collectives, local(): lax.all_gather(amplitude, 'alt', axis=0, tiled=True)  16.5 us
    psum x1, blocking collectives, local(): mine = lax.psum(stats, 'sub')  14.2 us
    dot_general x4, matrix products, spot_image(): jnp.einsum('ka,ams->kms', table_re, first_re, precision=high)  12.5 us
    dot_general x4, matrix products, spot_image(): jnp.einsum('ka,ams->kms', table_re, first_im, precision=high)  12 us
    dot_general x4, matrix products, spot_image(): jnp.einsum('ka,ams->kms', table_im, first_im, precision=high)  11.8 us
    dot_general x4, matrix products, spot_image(): jnp.einsum('kj,ajs->aks', table_im, field_im, precision=high)  11.6 us
  transfers between devices with their start and end apart: 2, of which 1 were waited for; matrix products, arithmetic and copies ran while one was open for 1% of the time, Pallas kernels for 0%

commit v1 on v0

v1 whole, which is shorter than its diff:
```python
import functools
import math

import jax
import jax.numpy as jnp
import ml_dtypes
import numpy as np
from jax import lax
from jax.experimental import pallas as pl
from jax.experimental.pallas import tpu as pltpu
from jax.sharding import PartitionSpec as P

ELONG = 0.75
LANES = 128
VMEM_LIMIT = 48 * 1024 * 1024
F32 = jnp.float32
BF16 = jnp.bfloat16


def dft_matrix(pupil, field):
    angle = 2.0 * np.pi / field * (np.outer(np.arange(field), np.arange(pupil)) % field)
    c, s = np.cos(angle), np.sin(angle)
    return np.block([[c, s], [-s, c]])


def table_three(matrix):
    hi = matrix.astype(np.float32).astype(ml_dtypes.bfloat16)
    lo = (matrix - hi.astype(np.float64)).astype(np.float32).astype(ml_dtypes.bfloat16)
    return np.concatenate([hi, lo, hi], axis=1)


def split_three(x):
    hi = x.astype(BF16)
    lo = (x - hi.astype(F32)).astype(BF16)
    return jnp.concatenate([hi, hi, lo], axis=0)


def dot(a, b):
    return jnp.dot(a, b, preferred_element_type=F32)


def lane_group(shape, width):
    return lax.broadcasted_iota(jnp.int32, shape, len(shape) - 1) // width


def roll(x, shift):
    return pltpu.roll(x, shift % LANES, x.ndim - 1)


def swap_groups(blocks, width):
    n = len(blocks)
    blocks = list(blocks)
    group = lane_group(blocks[0].shape, width)
    step = 1
    while step < n:
        low = (group & step) == 0
        for i in range(n):
            if i & step:
                continue
            j = i + step
            a, b = blocks[i], blocks[j]
            blocks[i] = jnp.where(low, a, roll(b, step * width))
            blocks[j] = jnp.where(low, roll(a, -step * width), b)
        step *= 2
    return blocks


def spread_groups(x, n, width):
    group = lane_group(x.shape, width)
    out = [x]
    step = n // 2
    while step >= 1:
        low = (group & step) == 0
        made = []
        for y in out:
            up, down = roll(y, step * width), roll(y, -step * width)
            made.append(jnp.where(low, y, up))
            made.append(jnp.where(low, down, y))
        out = made
        step //= 2
    return out


def pack_kernel(n, nb, profile_ref, weight_ref, cot_ref, amp_ref, phase_ref, early_ref, late_ref):
    width = LANES // n
    qp = phase_ref.shape[0] // n
    qc = cot_ref.shape[0] // n
    blocks = swap_groups([phase_ref[a * qp : (a + 1) * qp, :] for a in range(n)], width)
    for d in range(n):
        hi = blocks[d].astype(BF16)
        early_ref[d, 0:qp, :] = hi
        early_ref[d, qp : 2 * qp, :] = (blocks[d] - hi.astype(F32)).astype(BF16)
    blocks = swap_groups([amp_ref[a * qp : (a + 1) * qp, :].astype(F32) for a in range(n)], width)
    for d in range(n):
        early_ref[d, 2 * qp : 3 * qp, :] = blocks[d].astype(BF16)
    rows = early_ref.shape[1] - 3 * qp
    row = lax.broadcasted_iota(jnp.int32, (rows, LANES), 0)
    extra = jnp.zeros((rows, LANES), F32)
    for j in range(nb):
        for k, ref in enumerate((profile_ref, weight_ref)):
            value = jnp.full((rows, LANES), ref[j], F32)
            for part in range(3):
                piece = value.astype(BF16).astype(F32)
                extra = jnp.where(row == (2 * j + k) * 3 + part, piece, extra)
                value = value - piece
    for d in range(n):
        early_ref[d, 3 * qp :, :] = extra.astype(BF16)

    def step(i, carry):
        at = pl.multiple_of(i * 16, 16)
        parts = [cot_ref[pl.ds(a * qc + at, 16), :].astype(F32) for a in range(n)]
        for d, block in enumerate(swap_groups(parts, width)):
            late_ref[d, pl.ds(at, 16), :] = block.astype(BF16)
        return carry

    lax.fori_loop(0, qc // 16, step, 0, unroll=2)


def sincos(x):
    turns = jnp.round(x * (2.0 / math.pi))
    r = x - turns * 1.5703125
    r = r - turns * 4.838267948966e-4
    r2 = r * r
    s = r + r * r2 * (-1.6666654611e-1 + r2 * (8.3321608736e-3 + r2 * -1.9515295891e-4))
    c = (1.0 - 0.5 * r2) + r2 * r2 * (
        4.166664568298827e-2 + r2 * (-1.388731625493765e-3 + r2 * 2.443315711809948e-5)
    )
    quad = turns.astype(jnp.int32)
    odd = (quad & 1) != 0
    sin_v = jnp.where(odd, c, s)
    cos_v = jnp.where(odd, s, c)
    sin_v = jnp.where((quad & 2) != 0, -sin_v, sin_v)
    cos_v = jnp.where(((quad + 1) & 2) != 0, -cos_v, cos_v)
    return sin_v, cos_v


def main_kernel(
    n,
    nb,
    pupil,
    field,
    me_ref,
    pos_ref,
    early_ref,
    late_ref,
    fwd_ref,
    bwd_ref,
    grad_ref,
    aux_ref,
    phase_s,
    amp_s,
    e_s,
    f_s,
    g_s,
    pg_s,
):
    width = LANES // n
    nbins = n * nb
    qp = pupil * pupil // (n * n)
    qc = field * field // (n * n)
    group1 = lane_group((1, LANES), width)

    pos = pos_ref[...]
    me = me_ref[0]
    near = jnp.zeros_like(pos)
    for d in range(n):
        near = jnp.where(me == d, spread_groups(pos, n, width)[d], near)

    prof, wgt = [], []
    for t in range(nb):
        p_row, w_row = jnp.zeros((1, LANES), F32), jnp.zeros((1, LANES), F32)
        for d in range(n):
            extra = early_ref[d, 3 * qp :, :].astype(F32)
            p_d = sum(extra[(2 * t) * 3 + part : (2 * t) * 3 + part + 1, :] for part in (0, 1, 2))
            w_d = sum(
                extra[(2 * t + 1) * 3 + part : (2 * t + 1) * 3 + part + 1, :] for part in (0, 1, 2)
            )
            p_row = jnp.where(group1 == d, p_d, p_row)
            w_row = jnp.where(group1 == d, w_d, w_row)
        prof.append(p_row)
        wgt.append(w_row)
    total = sum(prof)
    step = n // 2
    while step >= 1:
        total = total + roll(total, step * width)
        step //= 2
    coef = [2.0 / (pupil * pupil) * prof[t] * wgt[t] / total for t in range(nb)]
    kappa = [
        ELONG * (2.0 * (group1 * nb + t).astype(F32) / (nbins - 1) - 1.0) for t in range(nb)
    ]
    tilt_x = [kappa[t] * near[0:1, :] for t in range(nb)]
    tilt_y = [kappa[t] * near[1:2, :] for t in range(nb)]

    def unpack(d, carry):
        for q in range(0, qp, 16):
            hi = early_ref[d, q : q + 16, :].astype(F32)
            lo = early_ref[d, qp + q : qp + q + 16, :].astype(F32)
            am = early_ref[d, 2 * qp + q : 2 * qp + q + 16, :].astype(F32)
            for a, (one, two) in enumerate(
                zip(spread_groups(hi + lo, n, width), spread_groups(am, n, width))
            ):
                at = pl.multiple_of((d * n + a) * qp + q, 16)
                phase_s[pl.ds(at, 16), :] = one
                amp_s[pl.ds(at, 16), :] = two
        return carry

    lax.fori_loop(0, n, unpack, 0)

    v_rows = lax.broadcasted_iota(jnp.int32, (pupil, LANES), 0).astype(F32) - (pupil - 1) / 2.0
    swing = [v_rows * tilt_y[t] for t in range(nb)]
    fwd = fwd_ref[...]
    bwd = bwd_ref[...]

    def first(i, carry):
        for k in range(4):
            c = i * 4 + k
            u = c.astype(F32) - (pupil - 1) / 2.0
            ph = phase_s[pl.ds(c, pupil, stride=pupil), :]
            am = amp_s[pl.ds(c, pupil, stride=pupil), :]
            fields = []
            for t in range(nb):
                sin_v, cos_v = sincos(ph + (u * tilt_x[t] + swing[t]))
                e = jnp.concatenate([am * cos_v, am * sin_v], axis=0)
                e_s[t, pl.ds(pl.multiple_of(c * 2 * pupil, 2 * pupil), 2 * pupil), :] = e
                fields.append(split_three(e))
            out = dot(fwd, jnp.concatenate(fields, axis=1))
            for t in range(nb):
                f_s[t, pl.ds(pl.multiple_of(c * 2 * field, 2 * field), 2 * field), :] = out[
                    :, t * LANES : (t + 1) * LANES
                ]
        return carry

    lax.fori_loop(0, pupil // 4, first, 0)

    per = qc // field

    def middle(i, carry):
        d, j = i // per, i % per
        raw = late_ref[d, pl.ds(pl.multiple_of(j * field, field), field), :].astype(F32)
        for a, cot in enumerate(spread_groups(raw, n, width)):
            k1 = (d * n + a) * per + j
            parts = []
            for t in range(nb):
                re = f_s[t, pl.ds(k1, pupil, stride=2 * field), :]
                im = f_s[t, pl.ds(k1 + field, pupil, stride=2 * field), :]
                parts.append(split_three(jnp.concatenate([re, im], axis=0)))
            image = dot(fwd, jnp.concatenate(parts, axis=1))
            both = jnp.concatenate([cot, cot], axis=0)
            parts = [
                split_three(image[:, t * LANES : (t + 1) * LANES] * both) for t in range(nb)
            ]
            back = dot(bwd, jnp.concatenate(parts, axis=1))
            for t in range(nb):
                g_s[t, pl.ds(pl.multiple_of(k1 * 2 * pupil, 2 * pupil), 2 * pupil), :] = back[
                    :, t * LANES : (t + 1) * LANES
                ]
        return carry

    lax.fori_loop(0, n * per, middle, 0)

    def last(i, stats):
        stats = list(stats)
        for k in range(4):
            c = i * 4 + k
            parts = []
            for t in range(nb):
                re = g_s[t, pl.ds(c, field, stride=2 * pupil), :]
                im = g_s[t, pl.ds(c + pupil, field, stride=2 * pupil), :]
                parts.append(split_three(jnp.concatenate([re, im], axis=0)))
            out = dot(bwd, jnp.concatenate(parts, axis=1))
            grad = jnp.zeros((pupil, LANES), F32)
            for t in range(nb):
                g = out[:, t * LANES : (t + 1) * LANES]
                e = e_s[t, pl.ds(pl.multiple_of(c * 2 * pupil, 2 * pupil), 2 * pupil), :]
                g_re, g_im = g[:pupil], g[pupil:]
                e_re, e_im = e[:pupil], e[pupil:]
                stats[t] = stats[t] + (e_re * g_re + e_im * g_im)
                grad = grad + coef[t] * (e_re * g_im - e_im * g_re)
            step = n // 2
            while step >= 1:
                grad = grad + roll(grad, step * width)
                step //= 2
            pg_s[pl.ds(c, pupil, stride=pupil), :] = grad
        return tuple(stats)

    stats = lax.fori_loop(
        0, pupil // 4, last, tuple(jnp.zeros((pupil, LANES), F32) for _ in range(nb))
    )

    aux = jnp.zeros(aux_ref.shape, F32)
    row = lax.broadcasted_iota(jnp.int32, aux_ref.shape, 0)
    for t in range(nb):
        stat = jnp.sum(stats[t], axis=0, keepdims=True) * (1.0 / (pupil * pupil))
        aux = jnp.where(row == t, stat, aux)
        aux = jnp.where(row == nb + t, prof[t], aux)
        aux = jnp.where(row == 2 * nb + t, wgt[t], aux)
    aux_ref[...] = jnp.where(row == 3 * nb, total, aux)

    def repack(d, carry):
        for q in range(0, qp, 8):
            out = jnp.zeros((8, LANES), F32)
            group = lane_group((8, LANES), width)
            for a in range(n):
                at = pl.multiple_of((d * n + a) * qp + q, 8)
                out = jnp.where(group == a, pg_s[pl.ds(at, 8), :], out)
            grad_ref[d, q : q + 8, :] = out
        return carry

    lax.fori_loop(0, n, repack, 0)


def final_kernel(n, nb, nsub_all, me_ref, grad_ref, stat_ref, aux_ref, out_ref, prof_ref):
    width = LANES // n
    qp = grad_ref.shape[1]
    for a, block in enumerate(swap_groups([grad_ref[d] for d in range(n)], width)):
        out_ref[a * qp : (a + 1) * qp, :] = block
    group = lane_group((1, LANES), width)
    mine = group == me_ref[0]
    stat = stat_ref[...]
    aux = aux_ref[...]
    total = jnp.max(aux[3 * nb : 3 * nb + 1, :])
    centre = jnp.float32(0.0)
    for t in range(nb):
        centre += jnp.sum(
            stat[t : t + 1] * aux[nb + t : nb + t + 1] * aux[2 * nb + t : 2 * nb + t + 1]
        )
    for t in range(nb):
        own = jnp.sum(
            jnp.where(mine, stat[t : t + 1] * aux[2 * nb + t : 2 * nb + t + 1], 0.0)
        )
        prof_ref[t] = (own / total - centre / (total * total)) / nsub_all


def local(cotangent, amplitude, phase, position, profile, alt_weight):
    n = lax.axis_size("alt")
    count = phase.shape[1]
    nsub_all = lax.axis_size("sub") * count
    nb = profile.shape[0]
    pupil = math.isqrt(n * phase.shape[0])
    field = math.isqrt(n * cotangent.shape[0])
    qp = phase.shape[0] // n
    qc = cotangent.shape[0] // n
    extra = -(-6 * nb // 16) * 16
    me = lax.axis_index("alt").astype(jnp.int32).reshape(1)
    smem = pl.BlockSpec(memory_space=pltpu.SMEM)
    vmem = pl.BlockSpec(memory_space=pltpu.VMEM)
    params = pltpu.CompilerParams(vmem_limit_bytes=VMEM_LIMIT)

    early, late = pl.pallas_call(
        functools.partial(pack_kernel, n, nb),
        out_shape=(
            jax.ShapeDtypeStruct((n, 3 * qp + extra, LANES), BF16),
            jax.ShapeDtypeStruct((n, qc, LANES), BF16),
        ),
        in_specs=[smem, smem, vmem, vmem, vmem],
        out_specs=(vmem, vmem),
        compiler_params=params,
        name="pack",
    )(profile, alt_weight, cotangent, amplitude, phase)
    early = lax.all_to_all(early, "alt", 0, 0)
    late = lax.all_to_all(late, "alt", 0, 0)

    base = dft_matrix(pupil, field)
    fwd = jnp.asarray(table_three(base))
    bwd = jnp.asarray(table_three(base.T))
    aux_rows = -(-(3 * nb + 1) // 8) * 8
    grad, aux = pl.pallas_call(
        functools.partial(main_kernel, n, nb, pupil, field),
        out_shape=(
            jax.ShapeDtypeStruct((n, qp, LANES), F32),
            jax.ShapeDtypeStruct((aux_rows, LANES), F32),
        ),
        in_specs=[smem, vmem, vmem, vmem, vmem, vmem],
        out_specs=(vmem, vmem),
        scratch_shapes=[
            pltpu.VMEM((pupil * pupil, LANES), F32),
            pltpu.VMEM((pupil * pupil, LANES), F32),
            pltpu.VMEM((nb, 2 * pupil * pupil, LANES), F32),
            pltpu.VMEM((nb, 2 * pupil * field, LANES), F32),
            pltpu.VMEM((nb, 2 * pupil * field, LANES), F32),
            pltpu.VMEM((pupil * pupil, LANES), F32),
        ],
        compiler_params=params,
        name="spots",
    )(me, position, early, late, fwd, bwd)
    grad = lax.all_to_all(grad, "alt", 0, 0)
    stat = lax.psum(aux[:nb], ("sub", "alt"))
    phase_grad, profile_grad = pl.pallas_call(
        functools.partial(final_kernel, n, nb, nsub_all),
        out_shape=(
            jax.ShapeDtypeStruct(phase.shape, F32),
            jax.ShapeDtypeStruct(profile.shape, F32),
        ),
        in_specs=[smem, vmem, vmem, vmem],
        out_specs=(vmem, smem),
        compiler_params=params,
        name="unpack",
    )(me, grad, stat, aux)
    return phase_grad, profile_grad


def solution(mesh):
    placed = (P("alt", "sub"), P("alt", "sub"), P("alt", "sub"), P(None, "sub"), P("alt"), P("alt"))
    return jax.shard_map(
        local, mesh=mesh, in_specs=placed, out_specs=(P("alt", "sub"), P("alt")), check_vma=False
    )
```

time: 204 us -> 101 us (0.50)
  matrix products: 97.4 us -> 0 us
  Pallas kernels: 0 us -> 26.4 us
  between operations: 16.3 us -> 0.69 us
  blocking collectives: 64.5 us -> 54.6 us
  other arithmetic: 7.9 us -> 0 us
  loops' own time: 7.44 us -> 0 us
  starting transfers between devices: 0.08 us -> 6.86 us
  waiting for transfers between devices: 1.7 us -> 8.03 us
  local copies, waits for them, and re-layouts: 6.64 us -> 4.01 us
    dot_general x32 -> x0, matrix products: 97.4 us -> none  [the longest x4 21.3 us: spot_image(): jnp.einsum('ka,ams->kms', table_im, first_re, precision=high)]
    all_gather x2 -> x0, blocking collectives: 39.7 us -> none  [the longest x1 23.3 us: local(): phase_rows = lax.all_gather(phase, 'alt', axis=0, tiled=True)]
    pallas_call x0 -> x3, Pallas kernels: none -> 26.4 us  [the longest x1 22.8 us: local(): pl.pallas_call(functools.partial(main_kernel, n, nb, pupil, field), out_s...]
    psum x2 -> x1, blocking collectives: 24.7 us -> 40.7 us  [local(): stat = lax.psum(aux[:nb], ('sub', 'alt'))]
    all_to_all x0 -> x1, blocking collectives: none -> 13.9 us  [local(): early = lax.all_to_all(early, 'alt', 0, 0)]
    all_to_all x0 -> x2, waiting for transfers between devices: none -> 8.03 us  [the longest x1 8.03 us: local(): late = lax.all_to_all(late, 'alt', 0, 0)]
    another operation x1 -> x0, loops' own time: 7.44 us -> none  [run_bins(): lax.scan(step, jnp.zeros((P_SIZE, P_SIZE, count), jnp.float32), jnp.arang...]
    all_to_all x0 -> x2, starting transfers between devices: none -> 6.86 us  [the longest x1 3.54 us: local(): late = lax.all_to_all(late, 'alt', 0, 0)]
  transfers between devices with their start and end apart: 2 -> 2, of which waited for: 1 -> 1; matrix products, arithmetic and copies ran while one was open for 1% -> 0% of each run, Pallas kernels for 0% -> 0%
where the time goes in v1:
time: 101 us
  blocking collectives  54.6 us (54%)
  Pallas kernels  26.4 us (26%)
  waiting for transfers between devices  8.03 us (8%)
  starting transfers between devices  6.86 us (7%)
  local copies, waits for them, and re-layouts  4.01 us (4%)
    psum x1, blocking collectives, local(): stat = lax.psum(aux[:nb], ('sub', 'alt'))  40.7 us
    pallas_call x1, Pallas kernels, local(): pl.pallas_call(functools.partial(main_kernel, n, nb, pupil, field), out_s...  22.8 us
    all_to_all x1, blocking collectives, local(): early = lax.all_to_all(early, 'alt', 0, 0)  13.9 us
    all_to_all x1, waiting for transfers between devices, local(): late = lax.all_to_all(late, 'alt', 0, 0)  8.03 us
    unnamed x16, local copies, waits for them, and re-layouts  4.01 us
    all_to_all x1, starting transfers between devices, local(): late = lax.all_to_all(late, 'alt', 0, 0)  3.54 us
    all_to_all x1, starting transfers between devices, local(): grad = lax.all_to_all(grad, 'alt', 0, 0)  3.33 us
    pallas_call x1, Pallas kernels, local(): pl.pallas_call(functools.partial(pack_kernel, n, nb), out_shape=(jax.Shap...  2.74 us
  transfers between devices with their start and end apart: 2, of which 1 were waited for; matrix products, arithmetic and copies ran while one was open for 0% of the time, Pallas kernels for 0%

profile of v1, /device:TPU:0, one launch (start us, length us, event | category | flops | bytes accessed | tf_op | source)
XLA Modules:
  0.0 100.7 jit_solution(4586418188271045154)
XLA Ops:
  0.6 0.0 copy-start
  0.6 0.9 copy-done
  1.6 0.0 copy-start.1
  1.6 0.9 copy-done.1
  2.5 0.0 copy-start.2
  2.5 0.8 copy-done.2
  3.3 0.0 copy-start.6
  3.3 0.7 copy-done.6
  4.0 0.0 copy-start.7
  4.0 0.7 copy-done.7
  4.6 2.7 %pack.1 = (bf16[4,208,128]{2,1,0:T(8,128)(2,1)S(1)}, bf16[4,256,128]{2,1,0:T(8,128)(2,1)}) custom-call(f32[2]{0:T(128)S(1)} %copy-done.6, f32[2]{0:T(128)S(1)} %copy-done.7, bf16[1024,128]{1,0:T(8,128)(2,1)S(1)} %copy-done, bf16[256,128]{1,0:T(8,128)(2,1)S(1)} %copy-done.2, f32[256,128]{1,0:T(8,128)S(1)} %copy-done.1), custom_call_target="tpu_custom_call" | custom-call | tf_op jit(solution)/shard_map/pack/pallas_call | solution.py:349
  7.4 13.9 %all_to_all.15.early_ref = bf16[4,208,128]{2,1,0:T(8,128)(2,1)S(1)} all-to-all(bf16[4,208,128]{2,1,0:T(8,128)(2,1)S(1)} %get-tuple-element.6), channel_id=1, replica_groups=mesh['sub'=8,'alt'=4] {'alt'}, dimensions={0} | all-to-all | bytes 425984 | tf_op jit(solution)/shard_map/all_to_all | solution.py:360
  21.3 0.0 copy-start.3
  21.3 0.0 copy-start.4
  21.3 3.5 %all-to-all-start.1 = ((bf16[4,256,128]{2,1,0:T(8,128)(2,1)}), bf16[4,256,128]{2,1,0:T(8,128)(2,1)S(1)}, u32[]{:S(2)}, u32[]{:S(2)}) async-start(bf16[4,256,128]{2,1,0:T(8,128)(2,1)} %get-tuple-element.7), calls=%async_computation.1 | async-start | bytes 524288 | tf_op jit(solution)/shard_map/all_to_all | solution.py:361
  24.9 0.0 copy-start.5
  24.9 8.0 %all-to-all-done.1.late_ref = bf16[4,256,128]{2,1,0:T(8,128)(2,1)S(1)} async-done(((bf16[4,256,128]{2,1,0:T(8,128)(2,1)}), bf16[4,256,128]{2,1,0:T(8,128)(2,1)S(1)}, u32[]{:S(2)}, u32[]{:S(2)}) %all-to-all-start.1) | async-done | bytes 262176 | tf_op jit(solution)/shard_map/all_to_all | solution.py:361
  32.9 0.0 copy-done.3
  32.9 0.0 copy-done.4
  32.9 0.0 copy-done.5
  32.9 22.8 %spots.1 = (f32[4,64,128]{2,1,0:T(8,128)}, f32[8,128]{1,0:T(8,128)S(1)}) custom-call(s32[1]{0:T(128)} %bitcast.me_ref, f32[2,128]{1,0:T(2,128)S(1)} %copy-done.5, bf16[4,208,128]{2,1,0:T(8,128)(2,1)S(1)} %all_to_all.15.early_ref, bf16[4,256,128]{2,1,0:T(8,128)(2,1)S(1)} %all-to-all-done.1.late_ref, bf16[128,192]{1,0:T(8,128)(2,1)S(1)} %copy-done.3, ...), custom_call_target="tpu_custom_call" | custom-call | tf_op jit(solution)/shard_map/spots/pallas_call | solution.py:367
  55.7 3.3 %all-to-all-start.2 = ((f32[4,64,128]{2,1,0:T(8,128)}), f32[4,64,128]{2,1,0:T(8,128)S(1)}, u32[]{:S(2)}, u32[]{:S(2)}) async-start(f32[4,64,128]{2,1,0:T(8,128)} %get-tuple-element.8), calls=%async_computation.2 | async-start | bytes 262144 | tf_op jit(solution)/shard_map/all_to_all | solution.py:386
  59.1 40.7 %psum.7.stat_ref = f32[2,128]{1,0:T(2,128)S(1)} all-reduce(f32[2,128]{1,0:T(2,128)S(1)} %slice.3), channel_id=1, replica_groups=mesh['sub'=8,'alt'=4] {'sub','alt'}, use_global_device_ids=true, to_apply=%region_0.0 | all-reduce | flops 256 | bytes 2048 | tf_op jit(solution)/shard_map/psum | solution.py:387
  99.8 0.0 all-to-all-done.2.grad_ref
  99.8 0.9 unpack.1
  (1 shorter events, 0.0 us)
Async XLA Ops:
  0.6 1.0 copy-start
  1.6 0.9 copy-start.1
  2.5 0.8 copy-start.2
  3.3 0.7 copy-start.6
  4.0 0.7 copy-start.7
  21.3 11.6 %copy-start.3 = (bf16[128,192]{1,0:T(8,128)(2,1)S(1)}, bf16[128,192]{1,0:T(8,128)(2,1)}, u32[]{:S(2)}) copy-start(bf16[128,192]{1,0:T(8,128)(2,1)} %constant.8.clone.fwd_ref) | copy-start | bytes 147460
  21.3 11.6 %copy-start.4 = (bf16[64,384]{1,0:T(8,128)(2,1)S(1)}, bf16[64,384]{1,0:T(8,128)(2,1)}, u32[]{:S(2)}) copy-start(bf16[64,384]{1,0:T(8,128)(2,1)} %constant.9.clone.bwd_ref) | copy-start | bytes 147460
  21.3 11.6 %all-to-all-start.1 = ((bf16[4,256,128]{2,1,0:T(8,128)(2,1)}), bf16[4,256,128]{2,1,0:T(8,128)(2,1)S(1)}, u32[]{:S(2)}, u32[]{:S(2)}) async-start(bf16[4,256,128]{2,1,0:T(8,128)(2,1)} %get-tuple-element.7), calls=%async_computation.1 | async-start | bytes 524288 | tf_op jit(solution)/shard_map/all_to_all | solution.py:361
  24.9 8.1 %copy-start.5 = (f32[2,128]{1,0:T(2,128)S(1)}, f32[2,128]{1,0:T(2,128)}, u32[]{:S(2)}) copy-start(f32[2,128]{1,0:T(2,128)} %pos_ref.1) | copy-start | bytes 3076
  55.7 44.1 %all-to-all-start.2 = ((f32[4,64,128]{2,1,0:T(8,128)}), f32[4,64,128]{2,1,0:T(8,128)S(1)}, u32[]{:S(2)}, u32[]{:S(2)}) async-start(f32[4,64,128]{2,1,0:T(8,128)} %get-tuple-element.8), calls=%async_computation.2 | async-start | bytes 262144 | tf_op jit(solution)/shard_map/all_to_all | solution.py:386

commit v2 on v1

--- a/solution.py
+++ b/solution.py
@@ -12,7 +12,7 @@
 
 ELONG = 0.75
 LANES = 128
-VMEM_LIMIT = 48 * 1024 * 1024
+VMEM_LIMIT = 24 * 1024 * 1024
 F32 = jnp.float32
 BF16 = jnp.bfloat16
 
@@ -81,19 +81,23 @@
     return out
 
 
-def pack_kernel(n, nb, profile_ref, weight_ref, cot_ref, amp_ref, phase_ref, early_ref, late_ref):
+def pack_kernel(n, nb, me_ref, profile_ref, weight_ref, cot_hbm, amp_hbm, phase_hbm, *refs):
+    early_refs, late_ref = refs[:n], refs[n]
+    cot_ref, amp_ref, phase_ref, sems = refs[n + 1 :]
+    copies = [
+        pltpu.make_async_copy(src, dst, sems.at[i])
+        for i, (src, dst) in enumerate(
+            ((phase_hbm, phase_ref), (amp_hbm, amp_ref), (cot_hbm, cot_ref))
+        )
+    ]
+    for copy in copies:
+        copy.start()
     width = LANES // n
     qp = phase_ref.shape[0] // n
     qc = cot_ref.shape[0] // n
-    blocks = swap_groups([phase_ref[a * qp : (a + 1) * qp, :] for a in range(n)], width)
-    for d in range(n):
-        hi = blocks[d].astype(BF16)
-        early_ref[d, 0:qp, :] = hi
-        early_ref[d, qp : 2 * qp, :] = (blocks[d] - hi.astype(F32)).astype(BF16)
-    blocks = swap_groups([amp_ref[a * qp : (a + 1) * qp, :].astype(F32) for a in range(n)], width)
-    for d in range(n):
-        early_ref[d, 2 * qp : 3 * qp, :] = blocks[d].astype(BF16)
-    rows = early_ref.shape[1] - 3 * qp
+    me = me_ref[0]
+    turn = lax.rem(n - me, n) * width
+    rows = early_refs[0].shape[0] - 3 * qp
     row = lax.broadcasted_iota(jnp.int32, (rows, LANES), 0)
     extra = jnp.zeros((rows, LANES), F32)
     for j in range(nb):
@@ -103,8 +107,24 @@
                 piece = value.astype(BF16).astype(F32)
                 extra = jnp.where(row == (2 * j + k) * 3 + part, piece, extra)
                 value = value - piece
-    for d in range(n):
-        early_ref[d, 3 * qp :, :] = extra.astype(BF16)
+    for j in range(n):
+        early_refs[j][3 * qp :, :] = extra.astype(BF16)
+    copies[0].wait()
+    for q in range(0, qp, 16):
+        parts = [pltpu.roll(phase_ref[a * qp + q : a * qp + q + 16, :], turn, 1) for a in range(n)]
+        for j, block in enumerate(swap_groups(parts, width)):
+            hi = block.astype(BF16)
+            early_refs[j][q : q + 16, :] = hi
+            early_refs[j][qp + q : qp + q + 16, :] = (block - hi.astype(F32)).astype(BF16)
+    copies[1].wait()
+    for q in range(0, qp, 16):
+        parts = [
+            pltpu.roll(amp_ref[a * qp + q : a * qp + q + 16, :].astype(F32), turn, 1)
+            for a in range(n)
+        ]
+        for j, block in enumerate(swap_groups(parts, width)):
+            early_refs[j][2 * qp + q : 2 * qp + q + 16, :] = block.astype(BF16)
+    copies[2].wait()
 
     def step(i, carry):
         at = pl.multiple_of(i * 16, 16)
@@ -113,7 +133,7 @@
             late_ref[d, pl.ds(at, 16), :] = block.astype(BF16)
         return carry
 
-    lax.fori_loop(0, qc // 16, step, 0, unroll=2)
+    lax.fori_loop(0, qc // 16, step, 0, unroll=4)
 
 
 def sincos(x):
@@ -134,30 +154,12 @@
     return sin_v, cos_v
 
 
-def main_kernel(
-    n,
-    nb,
-    pupil,
-    field,
-    me_ref,
-    pos_ref,
-    early_ref,
-    late_ref,
-    fwd_ref,
-    bwd_ref,
-    grad_ref,
-    aux_ref,
-    phase_s,
-    amp_s,
-    e_s,
-    f_s,
-    g_s,
-    pg_s,
-):
+def first_kernel(n, nb, pupil, field, me_ref, pos_ref, *refs):
+    early_refs = refs[:n]
+    fwd_ref, e_s, f_s, aux_ref, phase_s, amp_s = refs[n:]
     width = LANES // n
     nbins = n * nb
     qp = pupil * pupil // (n * n)
-    qc = field * field // (n * n)
     group1 = lane_group((1, LANES), width)
 
     pos = pos_ref[...]
@@ -169,8 +171,9 @@
     prof, wgt = [], []
     for t in range(nb):
         p_row, w_row = jnp.zeros((1, LANES), F32), jnp.zeros((1, LANES), F32)
-        for d in range(n):
-            extra = early_ref[d, 3 * qp :, :].astype(F32)
+        for j in range(n):
+            d = lax.rem(me + n - j, n)
+            extra = early_refs[j][3 * qp :, :].astype(F32)
             p_d = sum(extra[(2 * t) * 3 + part : (2 * t) * 3 + part + 1, :] for part in (0, 1, 2))
             w_d = sum(
                 extra[(2 * t + 1) * 3 + part : (2 * t + 1) * 3 + part + 1, :] for part in (0, 1, 2)
@@ -184,32 +187,35 @@
     while step >= 1:
         total = total + roll(total, step * width)
         step //= 2
-    coef = [2.0 / (pupil * pupil) * prof[t] * wgt[t] / total for t in range(nb)]
+    aux = jnp.zeros(aux_ref.shape, F32)
+    row = lax.broadcasted_iota(jnp.int32, aux_ref.shape, 0)
+    for t in range(nb):
+        aux = jnp.where(row == t, 2.0 / (pupil * pupil) * prof[t] * wgt[t] / total, aux)
+        aux = jnp.where(row == nb + t, prof[t], aux)
+        aux = jnp.where(row == 2 * nb + t, wgt[t], aux)
+    aux_ref[...] = jnp.where(row == 3 * nb, total, aux)
     kappa = [
         ELONG * (2.0 * (group1 * nb + t).astype(F32) / (nbins - 1) - 1.0) for t in range(nb)
     ]
     tilt_x = [kappa[t] * near[0:1, :] for t in range(nb)]
     tilt_y = [kappa[t] * near[1:2, :] for t in range(nb)]
 
-    def unpack(d, carry):
+    for j in range(n):
+        d = lax.rem(me + n - j, n)
         for q in range(0, qp, 16):
-            hi = early_ref[d, q : q + 16, :].astype(F32)
-            lo = early_ref[d, qp + q : qp + q + 16, :].astype(F32)
-            am = early_ref[d, 2 * qp + q : 2 * qp + q + 16, :].astype(F32)
+            hi = early_refs[j][q : q + 16, :].astype(F32)
+            lo = early_refs[j][qp + q : qp + q + 16, :].astype(F32)
+            am = early_refs[j][2 * qp + q : 2 * qp + q + 16, :].astype(F32)
             for a, (one, two) in enumerate(
                 zip(spread_groups(hi + lo, n, width), spread_groups(am, n, width))
             ):
                 at = pl.multiple_of((d * n + a) * qp + q, 16)
                 phase_s[pl.ds(at, 16), :] = one
                 amp_s[pl.ds(at, 16), :] = two
-        return carry
-
-    lax.fori_loop(0, n, unpack, 0)
 
     v_rows = lax.broadcasted_iota(jnp.int32, (pupil, LANES), 0).astype(F32) - (pupil - 1) / 2.0
     swing = [v_rows * tilt_y[t] for t in range(nb)]
     fwd = fwd_ref[...]
-    bwd = bwd_ref[...]
 
     def first(i, carry):
         for k in range(4):
@@ -231,6 +237,17 @@
         return carry
 
     lax.fori_loop(0, pupil // 4, first, 0)
+
+
+def second_kernel(
+    n, nb, pupil, field, e_s, f_s, aux_in, late_ref, fwd_ref, bwd_ref, grad_ref, stat_ref, g_s, pg_s
+):
+    width = LANES // n
+    qp = pupil * pupil // (n * n)
+    qc = field * field // (n * n)
+    fwd = fwd_ref[...]
+    bwd = bwd_ref[...]
+    coef = [aux_in[t : t + 1, :] for t in range(nb)]
 
     per = qc // field
 
@@ -287,14 +304,17 @@
         0, pupil // 4, last, tuple(jnp.zeros((pupil, LANES), F32) for _ in range(nb))
     )
 
-    aux = jnp.zeros(aux_ref.shape, F32)
-    row = lax.broadcasted_iota(jnp.int32, aux_ref.shape, 0)
+    lane = lax.broadcasted_iota(jnp.int32, (1, LANES), 1)
+    sums = jnp.zeros((1, LANES), F32)
     for t in range(nb):
         stat = jnp.sum(stats[t], axis=0, keepdims=True) * (1.0 / (pupil * pupil))
-        aux = jnp.where(row == t, stat, aux)
-        aux = jnp.where(row == nb + t, prof[t], aux)
-        aux = jnp.where(row == 2 * nb + t, wgt[t], aux)
-    aux_ref[...] = jnp.where(row == 3 * nb, total, aux)
+        step = 1
+        while step < width:
+            stat = stat + roll(stat, step)
+            step *= 2
+        sums = jnp.where(lane % width == width - 1 - t, roll(stat, -t), sums)
+    for i in range(stat_ref.shape[0]):
+        stat_ref[i] = sums
 
     def repack(d, carry):
         for q in range(0, qp, 8):
@@ -314,21 +334,20 @@
     qp = grad_ref.shape[1]
     for a, block in enumerate(swap_groups([grad_ref[d] for d in range(n)], width)):
         out_ref[a * qp : (a + 1) * qp, :] = block
-    group = lane_group((1, LANES), width)
-    mine = group == me_ref[0]
-    stat = stat_ref[...]
+    lane = lax.broadcasted_iota(jnp.int32, (1, LANES), 1)
+    stat = jnp.sum(stat_ref[...], axis=0)
     aux = aux_ref[...]
     total = jnp.max(aux[3 * nb : 3 * nb + 1, :])
-    centre = jnp.float32(0.0)
+    centre = jnp.zeros((1, LANES), F32)
+    own = []
     for t in range(nb):
-        centre += jnp.sum(
-            stat[t : t + 1] * aux[nb + t : nb + t + 1] * aux[2 * nb + t : 2 * nb + t + 1]
-        )
+        prof, wgt = aux[nb + t : nb + t + 1], aux[2 * nb + t : 2 * nb + t + 1]
+        term = stat * wgt
+        centre += jnp.where(lane % width == width - 1 - t, term * prof, 0.0)
+        own.append(jnp.sum(jnp.where(lane == (me_ref[0] + 1) * width - 1 - t, term, 0.0)))
+    centre = jnp.sum(centre)
     for t in range(nb):
-        own = jnp.sum(
-            jnp.where(mine, stat[t : t + 1] * aux[2 * nb + t : 2 * nb + t + 1], 0.0)
-        )
-        prof_ref[t] = (own / total - centre / (total * total)) / nsub_all
+        prof_ref[t] = (own[t] / total - centre / (total * total)) / nsub_all
 
 
 def local(cotangent, amplitude, phase, position, profile, alt_weight):
@@ -346,45 +365,66 @@
     vmem = pl.BlockSpec(memory_space=pltpu.VMEM)
     params = pltpu.CompilerParams(vmem_limit_bytes=VMEM_LIMIT)
 
-    early, late = pl.pallas_call(
+    any_space = pl.BlockSpec(memory_space=pl.ANY)
+    early_shape = (3 * qp + extra, LANES)
+    *early, late = pl.pallas_call(
         functools.partial(pack_kernel, n, nb),
-        out_shape=(
-            jax.ShapeDtypeStruct((n, 3 * qp + extra, LANES), BF16),
-            jax.ShapeDtypeStruct((n, qc, LANES), BF16),
-        ),
-        in_specs=[smem, smem, vmem, vmem, vmem],
-        out_specs=(vmem, vmem),
+        out_shape=[jax.ShapeDtypeStruct(early_shape, BF16)] * n
+        + [jax.ShapeDtypeStruct((n, qc, LANES), BF16)],
+        in_specs=[smem, smem, smem, any_space, any_space, any_space],
+        out_specs=[vmem] * (n + 1),
+        scratch_shapes=[
+            pltpu.VMEM(cotangent.shape, BF16),
+            pltpu.VMEM(amplitude.shape, BF16),
+            pltpu.VMEM(phase.shape, F32),
+            pltpu.SemaphoreType.DMA((3,)),
+        ],
         compiler_params=params,
         name="pack",
-    )(profile, alt_weight, cotangent, amplitude, phase)
-    early = lax.all_to_all(early, "alt", 0, 0)
+    )(me, profile, alt_weight, cotangent, amplitude, phase)
+    early = early[:1] + [
+        lax.ppermute(early[j], "alt", [(i, (i + j) % n) for i in range(n)]) for j in range(1, n)
+    ]
     late = lax.all_to_all(late, "alt", 0, 0)
 
     base = dft_matrix(pupil, field)
     fwd = jnp.asarray(table_three(base))
     bwd = jnp.asarray(table_three(base.T))
     aux_rows = -(-(3 * nb + 1) // 8) * 8
-    grad, aux = pl.pallas_call(
-        functools.partial(main_kernel, n, nb, pupil, field),
+    e, f, aux = pl.pallas_call(
+        functools.partial(first_kernel, n, nb, pupil, field),
         out_shape=(
-            jax.ShapeDtypeStruct((n, qp, LANES), F32),
+            jax.ShapeDtypeStruct((nb, 2 * pupil * pupil, LANES), F32),
+            jax.ShapeDtypeStruct((nb, 2 * pupil * field, LANES), F32),
             jax.ShapeDtypeStruct((aux_rows, LANES), F32),
         ),
-        in_specs=[smem, vmem, vmem, vmem, vmem, vmem],
-        out_specs=(vmem, vmem),
+        in_specs=[smem, vmem] + [vmem] * n + [vmem],
+        out_specs=(vmem, vmem, vmem),
         scratch_shapes=[
             pltpu.VMEM((pupil * pupil, LANES), F32),
             pltpu.VMEM((pupil * pupil, LANES), F32),
-            pltpu.VMEM((nb, 2 * pupil * pupil, LANES), F32),
-            pltpu.VMEM((nb, 2 * pupil * field, LANES), F32),
+        ],
+        compiler_params=params,
+        name="fields",
+    )(me, position, *early, fwd)
+    devices = lax.axis_size("sub") * n
+    grad, stat = pl.pallas_call(
+        functools.partial(second_kernel, n, nb, pupil, field),
+        out_shape=(
+            jax.ShapeDtypeStruct((n, qp, LANES), F32),
+            jax.ShapeDtypeStruct((devices, 1, LANES), F32),
+        ),
+        in_specs=[vmem] * 6,
+        out_specs=(vmem, vmem),
+        scratch_shapes=[
             pltpu.VMEM((nb, 2 * pupil * field, LANES), F32),
             pltpu.VMEM((pupil * pupil, LANES), F32),
         ],
         compiler_params=params,
-        name="spots",
-    )(me, position, early, late, fwd, bwd)
+        name="images",
+    )(e, f, aux, late, fwd, bwd)
     grad = lax.all_to_all(grad, "alt", 0, 0)
-    stat = lax.psum(aux[:nb], ("sub", "alt"))
+    stat = lax.all_to_all(stat, ("sub", "alt"), 0, 0)
     phase_grad, profile_grad = pl.pallas_call(
         functools.partial(final_kernel, n, nb, nsub_all),
         out_shape=(

time: 101 us -> 78.2 us (0.77)
  blocking collectives: 54.6 us -> 19.7 us
  local copies, waits for them, and re-layouts: 4.01 us -> 11.3 us
  starting transfers between devices: 6.86 us -> 12.2 us
    psum x1 -> x0, blocking collectives: 40.7 us -> none  [local(): stat = lax.psum(aux[:nb], ('sub', 'alt'))]
    all_to_all x1, waiting for transfers between devices: 8.03 us -> 0.01 us  [local(): late = lax.all_to_all(late, 'alt', 0, 0)]
    unnamed x16 -> x22, local copies, waits for them, and re-layouts: 4.01 us -> 11.3 us
    ppermute x0 -> x3, waiting for transfers between devices: none -> 7.06 us  [local(): lax.ppermute(early[j], 'alt', [(i, (i + j) % n) for i in range(n)])]
    ppermute x0 -> x3, starting transfers between devices: none -> 5.85 us  [local(): lax.ppermute(early[j], 'alt', [(i, (i + j) % n) for i in range(n)])]
    all_to_all x1 -> x2, blocking collectives: 13.9 us -> 19.7 us  [the longest x1 11.2 us: local(): stat = lax.all_to_all(stat, ('sub', 'alt'), 0, 0)]
    all_to_all x1 -> x0, starting transfers between devices: 3.33 us -> none  [local(): grad = lax.all_to_all(grad, 'alt', 0, 0)]
    all_to_all x1, starting transfers between devices: 3.54 us -> 6.33 us  [local(): late = lax.all_to_all(late, 'alt', 0, 0)]
  transfers between devices with their start and end apart: 2 -> 4, of which waited for: 1 -> 2; matrix products, arithmetic and copies ran while one was open for 0% -> 0% of each run, Pallas kernels for 0% -> 6%
where the time goes in v2:
time: 78.2 us; the launch traced here: 77.6 us
  Pallas kernels  26.6 us (34%)
  blocking collectives  19.7 us (25%)
  starting transfers between devices  12.2 us (16%)
  local copies, waits for them, and re-layouts  11.3 us (14%)
  waiting for transfers between devices  7.07 us (9%)
    pallas_call x1, Pallas kernels, local(): pl.pallas_call(functools.partial(second_kernel, n, nb, pupil, field), out...  18.1 us
    unnamed x22, local copies, waits for them, and re-layouts  11.3 us
    all_to_all x1, blocking collectives, local(): stat = lax.all_to_all(stat, ('sub', 'alt'), 0, 0)  11.2 us
    all_to_all x1, blocking collectives, local(): grad = lax.all_to_all(grad, 'alt', 0, 0)  8.5 us
    ppermute x3, waiting for transfers between devices, local(): lax.ppermute(early[j], 'alt', [(i, (i + j) % n) for i in range(n)])  7.06 us
    all_to_all x1, starting transfers between devices, local(): late = lax.all_to_all(late, 'alt', 0, 0)  6.33 us
    ppermute x3, starting transfers between devices, local(): lax.ppermute(early[j], 'alt', [(i, (i + j) % n) for i in range(n)])  5.85 us
    pallas_call x1, Pallas kernels, local(): pl.pallas_call(functools.partial(first_kernel, n, nb, pupil, field), out_...  5 us
  transfers between devices with their start and end apart: 4, of which 2 were waited for; matrix products, arithmetic and copies ran while one was open for 0% of the time, Pallas kernels for 6%

profile of v2, /device:TPU:0, one launch (start us, length us, event | category | flops | bytes accessed | tf_op | source)
XLA Modules:
  0.0 77.6 jit_solution(9733154895684546415)
XLA Ops:
  0.6 0.0 copy-start.4
  0.6 0.9 %copy-done.4 = bf16[1024,128]{1,0:T(8,128)(2,1)S(1)} copy-done((bf16[1024,128]{1,0:T(8,128)(2,1)S(1)}, bf16[1024,128]{1,0:T(8,128)(2,1)}, u32[]{:S(2)}) %copy-start.4) | copy-done | bytes 262168
  1.6 0.0 copy-start.5
  1.6 0.9 %copy-done.5 = f32[256,128]{1,0:T(8,128)S(1)} copy-done((f32[256,128]{1,0:T(8,128)S(1)}, f32[256,128]{1,0:T(8,128)}, u32[]{:S(2)}) %copy-start.5) | copy-done | bytes 131096
  2.5 0.0 copy-start.6
  2.5 0.8 %copy-done.6 = bf16[256,128]{1,0:T(8,128)(2,1)S(1)} copy-done((bf16[256,128]{1,0:T(8,128)(2,1)S(1)}, bf16[256,128]{1,0:T(8,128)(2,1)}, u32[]{:S(2)}) %copy-start.6) | copy-done | bytes 65560
  3.3 0.0 copy-start.9
  3.3 0.7 copy-done.9
  4.0 0.0 copy-start.10
  4.0 0.7 copy-done.10
  4.6 2.7 %pack.1 = (bf16[208,128]{1,0:T(8,128)(2,1)S(1)}, bf16[208,128]{1,0:T(8,128)(2,1)S(1)}, bf16[208,128]{1,0:T(8,128)(2,1)S(1)}, bf16[208,128]{1,0:T(8,128)(2,1)S(1)}, bf16[4,256,128]{2,1,0:T(8,128)(2,1)}) custom-call(s32[1]{0:T(128)} %bitcast.me_ref, f32[2]{0:T(128)S(1)} %copy-done.9, f32[2]{0:T(128)S(1)} %copy-done.10, bf16[1024,128]{1,0:T(8,128)(2,1)S(1)} %copy-done.4, ...), custom_call_target="tpu_custom_call" | custom-call | tf_op jit(solution)/shard_map/pack/pallas_call | solution.py:370
  7.3 6.3 %all-to-all-start = ((bf16[4,256,128]{2,1,0:T(8,128)(2,1)}), bf16[4,256,128]{2,1,0:T(8,128)(2,1)S(1)}, u32[]{:S(2)}, u32[]{:S(2)}) async-start(bf16[4,256,128]{2,1,0:T(8,128)(2,1)} %get-tuple-element.19), calls=%async_computation | async-start | bytes 524288 | tf_op jit(solution)/shard_map/all_to_all | solution.py:388
  13.7 2.0 %collective-permute-start = (bf16[208,128]{1,0:T(8,128)(2,1)S(1)}, bf16[208,128]{1,0:T(8,128)(2,1)S(1)}, u32[]{:S(2)}, u32[]{:S(2)}) collective-permute-start(bf16[208,128]{1,0:T(8,128)(2,1)S(1)} %get-tuple-element.13), channel_id=1, source_target_pairs={{0,1},{1,2},{2,3},{3,0},{4,5},{5,6},{6,7},{7,4},{8,9},{9,10},{10,1... | collective-permute-start | bytes 159752 | tf_op jit(solution)/shard_map/ppermute | solution.py:386
  15.7 2.4 %collective-permute-start.1 = (bf16[208,128]{1,0:T(8,128)(2,1)S(1)}, bf16[208,128]{1,0:T(8,128)(2,1)S(1)}, u32[]{:S(2)}, u32[]{:S(2)}) collective-permute-start(bf16[208,128]{1,0:T(8,128)(2,1)S(1)} %get-tuple-element.14), channel_id=1, source_target_pairs={{0,2},{1,3},{2,0},{3,1},{4,6},{5,7},{6,4},{7,5},{8,10},{9,11},{10,... | collective-permute-start | bytes 159752 | tf_op jit(solution)/shard_map/ppermute | solution.py:386
  18.1 1.5 %collective-permute-start.2 = (bf16[208,128]{1,0:T(8,128)(2,1)S(1)}, bf16[208,128]{1,0:T(8,128)(2,1)S(1)}, u32[]{:S(2)}, u32[]{:S(2)}) collective-permute-start(bf16[208,128]{1,0:T(8,128)(2,1)S(1)} %get-tuple-element.15), channel_id=1, source_target_pairs={{0,3},{1,0},{2,1},{3,2},{4,7},{5,4},{6,5},{7,6},{8,11},{9,8},{10,9... | collective-permute-start | bytes 159752 | tf_op jit(solution)/shard_map/ppermute | solution.py:386
  19.5 4.8 %collective-permute-done.refs_1_ = bf16[208,128]{1,0:T(8,128)(2,1)S(1)} collective-permute-done((bf16[208,128]{1,0:T(8,128)(2,1)S(1)}, bf16[208,128]{1,0:T(8,128)(2,1)S(1)}, u32[]{:S(2)}, u32[]{:S(2)}) %collective-permute-start) | collective-permute-done | bytes 53280 | tf_op jit(solution)/shard_map/ppermute | solution.py:386
  24.4 2.2 %collective-permute-done.1.refs_2_ = bf16[208,128]{1,0:T(8,128)(2,1)S(1)} collective-permute-done((bf16[208,128]{1,0:T(8,128)(2,1)S(1)}, bf16[208,128]{1,0:T(8,128)(2,1)S(1)}, u32[]{:S(2)}, u32[]{:S(2)}) %collective-permute-start.1) | collective-permute-done | bytes 53280 | tf_op jit(solution)/shard_map/ppermute | solution.py:386
  26.6 0.0 collective-permute-done.2.refs_3_
  26.6 0.0 copy-start.2
  26.6 0.8 %copy-done.2 = bf16[128,192]{1,0:T(8,128)(2,1)S(1)} copy-done((bf16[128,192]{1,0:T(8,128)(2,1)S(1)}, bf16[128,192]{1,0:T(8,128)(2,1)}, u32[]{:S(2)}) %copy-start.2) | copy-done | bytes 49176
  27.4 0.0 copy-start.8
  27.4 0.7 copy-done.8
  28.1 5.0 %fields.1 = (f32[2,2048,128]{2,1,0:T(8,128)S(1)}, f32[2,4096,128]{2,1,0:T(8,128)S(1)}, f32[8,128]{1,0:T(8,128)S(1)}) custom-call(s32[1]{0:T(128)} %bitcast.me_ref, f32[2,128]{1,0:T(2,128)S(1)} %copy-done.8, bf16[208,128]{1,0:T(8,128)(2,1)S(1)} %get-tuple-element.12.refs_0_, bf16[208,128]{1,0:T(8,128)(2,1)S(1)} %collective-permute-done.refs_1_, ...), custom_call_target="tpu_custom_call" | custom-call | tf_op jit(solution)/shard_map/fields/pallas_call | solution.py:394
  33.1 0.0 copy-start
  33.1 1.9 %copy-done = f32[2,4096,128]{2,1,0:T(8,128)} copy-done((f32[2,4096,128]{2,1,0:T(8,128)}, f32[2,4096,128]{2,1,0:T(8,128)S(1)}, u32[]{:S(2)}) %copy-start) | copy-done | bytes 4194328
  35.1 0.0 all-to-all-done.late_ref
  35.1 0.0 copy-start.1
  35.1 2.2 %copy-done.1 = f32[2,4096,128]{2,1,0:T(8,128)S(1)} copy-done((f32[2,4096,128]{2,1,0:T(8,128)S(1)}, f32[2,4096,128]{2,1,0:T(8,128)}, u32[]{:S(2)}) %copy-start.1) | copy-done | bytes 4194328
  37.3 0.0 copy-start.3
  37.3 0.8 %copy-done.3 = bf16[128,192]{1,0:T(8,128)(2,1)S(1)} copy-done((bf16[128,192]{1,0:T(8,128)(2,1)S(1)}, bf16[128,192]{1,0:T(8,128)(2,1)}, u32[]{:S(2)}) %copy-start.3) | copy-done | bytes 49176
  38.1 0.0 copy-start.7
  38.1 0.8 %copy-done.7 = bf16[64,384]{1,0:T(8,128)(2,1)S(1)} copy-done((bf16[64,384]{1,0:T(8,128)(2,1)S(1)}, bf16[64,384]{1,0:T(8,128)(2,1)}, u32[]{:S(2)}) %copy-start.7) | copy-done | bytes 49176
  38.9 18.1 %images.1 = (f32[4,64,128]{2,1,0:T(8,128)S(1)}, f32[32,1,128]{2,1,0:T(1,128)S(1)}) custom-call(f32[2,2048,128]{2,1,0:T(8,128)S(1)} %get-tuple-element.16.e_s, f32[2,4096,128]{2,1,0:T(8,128)S(1)} %copy-done.1, f32[8,128]{1,0:T(8,128)S(1)} %get-tuple-element.18.aux_in.aux_ref, bf16[4,256,128]{2,1,0:T(8,128)(2,1)S(1)} %all-to-all-done.late_ref, ...), custom_call_target="tpu_custom_call" | custom-call | tf_op jit(solution)/shard_map/images/pallas_call | solution.py:411
  57.0 11.2 %all_to_all.15.stat_ref = f32[32,1,128]{2,1,0:T(1,128)S(1)} all-to-all(f32[32,1,128]{2,1,0:T(1,128)S(1)} %get-tuple-element.21), channel_id=1, replica_groups=mesh['sub'=8,'alt'=4] {'sub','alt'}, dimensions={0} | all-to-all | bytes 32768 | tf_op jit(solution)/shard_map/all_to_all | solution.py:427
  68.2 8.5 %all_to_all.16.grad_ref = f32[4,64,128]{2,1,0:T(8,128)S(1)} all-to-all(f32[4,64,128]{2,1,0:T(8,128)S(1)} %get-tuple-element.20), channel_id=1, replica_groups=mesh['sub'=8,'alt'=4] {'alt'}, dimensions={0} | all-to-all | bytes 262144 | tf_op jit(solution)/shard_map/all_to_all | solution.py:426
  76.7 0.9 %unpack.1 = (f32[256,128]{1,0:T(8,128)}, f32[2]{0:T(128)}) custom-call(s32[1]{0:T(128)} %bitcast.me_ref, f32[4,64,128]{2,1,0:T(8,128)S(1)} %all_to_all.16.grad_ref, f32[32,1,128]{2,1,0:T(1,128)S(1)} %all_to_all.15.stat_ref, f32[8,128]{1,0:T(8,128)S(1)} %get-tuple-element.18.aux_in.aux_ref), custom_call_target="tpu_custom_call" | custom-call | tf_op jit(solution)/shard_map/unpack/pallas_call | solution.py:428
Async XLA Ops:
  0.6 1.0 %copy-start.4 = (bf16[1024,128]{1,0:T(8,128)(2,1)S(1)}, bf16[1024,128]{1,0:T(8,128)(2,1)}, u32[]{:S(2)}) copy-start(bf16[1024,128]{1,0:T(8,128)(2,1)} %cot_hbm.1) | copy-start | bytes 786436
  1.6 0.9 %copy-start.5 = (f32[256,128]{1,0:T(8,128)S(1)}, f32[256,128]{1,0:T(8,128)}, u32[]{:S(2)}) copy-start(f32[256,128]{1,0:T(8,128)} %phase_hbm.1) | copy-start | bytes 393220
  2.5 0.8 %copy-start.6 = (bf16[256,128]{1,0:T(8,128)(2,1)S(1)}, bf16[256,128]{1,0:T(8,128)(2,1)}, u32[]{:S(2)}) copy-start(bf16[256,128]{1,0:T(8,128)(2,1)} %amp_hbm.1) | copy-start | bytes 196612
  3.3 0.7 copy-start.9
  4.0 0.7 copy-start.10
  7.3 27.7 %all-to-all-start = ((bf16[4,256,128]{2,1,0:T(8,128)(2,1)}), bf16[4,256,128]{2,1,0:T(8,128)(2,1)S(1)}, u32[]{:S(2)}, u32[]{:S(2)}) async-start(bf16[4,256,128]{2,1,0:T(8,128)(2,1)} %get-tuple-element.19), calls=%async_computation | async-start | bytes 524288 | tf_op jit(solution)/shard_map/all_to_all | solution.py:388
  13.7 10.7 %collective-permute-start = (bf16[208,128]{1,0:T(8,128)(2,1)S(1)}, bf16[208,128]{1,0:T(8,128)(2,1)S(1)}, u32[]{:S(2)}, u32[]{:S(2)}) collective-permute-start(bf16[208,128]{1,0:T(8,128)(2,1)S(1)} %get-tuple-element.13), channel_id=1, source_target_pairs={{0,1},{1,2},{2,3},{3,0},{4,5},{5,6},{6,7},{7,4},{8,9},{9,10},{10,1... | collective-permute-start | bytes 159752 | tf_op jit(solution)/shard_map/ppermute | solution.py:386
  15.7 10.9 %collective-permute-start.1 = (bf16[208,128]{1,0:T(8,128)(2,1)S(1)}, bf16[208,128]{1,0:T(8,128)(2,1)S(1)}, u32[]{:S(2)}, u32[]{:S(2)}) collective-permute-start(bf16[208,128]{1,0:T(8,128)(2,1)S(1)} %get-tuple-element.14), channel_id=1, source_target_pairs={{0,2},{1,3},{2,0},{3,1},{4,6},{5,7},{6,4},{7,5},{8,10},{9,11},{10,... | collective-permute-start | bytes 159752 | tf_op jit(solution)/shard_map/ppermute | solution.py:386
  18.1 8.5 %collective-permute-start.2 = (bf16[208,128]{1,0:T(8,128)(2,1)S(1)}, bf16[208,128]{1,0:T(8,128)(2,1)S(1)}, u32[]{:S(2)}, u32[]{:S(2)}) collective-permute-start(bf16[208,128]{1,0:T(8,128)(2,1)S(1)} %get-tuple-element.15), channel_id=1, source_target_pairs={{0,3},{1,0},{2,1},{3,2},{4,7},{5,4},{6,5},{7,6},{8,11},{9,8},{10,9... | collective-permute-start | bytes 159752 | tf_op jit(solution)/shard_map/ppermute | solution.py:386
  26.6 0.8 %copy-start.2 = (bf16[128,192]{1,0:T(8,128)(2,1)S(1)}, bf16[128,192]{1,0:T(8,128)(2,1)}, u32[]{:S(2)}) copy-start(bf16[128,192]{1,0:T(8,128)(2,1)} %constant.8.clone.refs_4_.fwd_ref) | copy-start | bytes 147460
  27.4 0.7 copy-start.8
  33.1 2.0 %copy-start = (f32[2,4096,128]{2,1,0:T(8,128)}, f32[2,4096,128]{2,1,0:T(8,128)S(1)}, u32[]{:S(2)}) copy-start(f32[2,4096,128]{2,1,0:T(8,128)S(1)} %get-tuple-element.17.f_s) | copy-start | bytes 12582916
  35.1 2.2 %copy-start.1 = (f32[2,4096,128]{2,1,0:T(8,128)S(1)}, f32[2,4096,128]{2,1,0:T(8,128)}, u32[]{:S(2)}) copy-start(f32[2,4096,128]{2,1,0:T(8,128)} %copy-done) | copy-start | bytes 12582916
  37.3 0.8 %copy-start.3 = (bf16[128,192]{1,0:T(8,128)(2,1)S(1)}, bf16[128,192]{1,0:T(8,128)(2,1)}, u32[]{:S(2)}) copy-start(bf16[128,192]{1,0:T(8,128)(2,1)} %constant.8.clone.refs_4_.fwd_ref) | copy-start | bytes 147460
  38.1 0.8 %copy-start.7 = (bf16[64,384]{1,0:T(8,128)(2,1)S(1)}, bf16[64,384]{1,0:T(8,128)(2,1)}, u32[]{:S(2)}) copy-start(bf16[64,384]{1,0:T(8,128)(2,1)} %constant.9.clone.bwd_ref) | copy-start | bytes 147460

commit v3 on v2

--- a/solution.py
+++ b/solution.py
@@ -81,34 +81,21 @@
     return out
 
 
-def pack_kernel(n, nb, me_ref, profile_ref, weight_ref, cot_hbm, amp_hbm, phase_hbm, *refs):
-    early_refs, late_ref = refs[:n], refs[n]
-    cot_ref, amp_ref, phase_ref, sems = refs[n + 1 :]
-    copies = [
-        pltpu.make_async_copy(src, dst, sems.at[i])
-        for i, (src, dst) in enumerate(
-            ((phase_hbm, phase_ref), (amp_hbm, amp_ref), (cot_hbm, cot_ref))
-        )
-    ]
+def pack_early_kernel(n, nb, me_ref, profile_hbm, weight_hbm, amp_hbm, phase_hbm, *refs):
+    early_refs = refs[:n]
+    profile_ref, weight_ref, amp_ref, phase_ref, sems = refs[n:]
+    pairs = (
+        (phase_hbm, phase_ref),
+        (amp_hbm, amp_ref),
+        (profile_hbm, profile_ref),
+        (weight_hbm, weight_ref),
+    )
+    copies = [pltpu.make_async_copy(src, dst, sems.at[i]) for i, (src, dst) in enumerate(pairs)]
     for copy in copies:
         copy.start()
     width = LANES // n
     qp = phase_ref.shape[0] // n
-    qc = cot_ref.shape[0] // n
-    me = me_ref[0]
-    turn = lax.rem(n - me, n) * width
-    rows = early_refs[0].shape[0] - 3 * qp
-    row = lax.broadcasted_iota(jnp.int32, (rows, LANES), 0)
-    extra = jnp.zeros((rows, LANES), F32)
-    for j in range(nb):
-        for k, ref in enumerate((profile_ref, weight_ref)):
-            value = jnp.full((rows, LANES), ref[j], F32)
-            for part in range(3):
-                piece = value.astype(BF16).astype(F32)
-                extra = jnp.where(row == (2 * j + k) * 3 + part, piece, extra)
-                value = value - piece
-    for j in range(n):
-        early_refs[j][3 * qp :, :] = extra.astype(BF16)
+    turn = lax.rem(n - me_ref[0], n) * width
     copies[0].wait()
     for q in range(0, qp, 16):
         parts = [pltpu.roll(phase_ref[a * qp + q : a * qp + q + 16, :], turn, 1) for a in range(n)]
@@ -125,12 +112,38 @@
         for j, block in enumerate(swap_groups(parts, width)):
             early_refs[j][2 * qp + q : 2 * qp + q + 16, :] = block.astype(BF16)
     copies[2].wait()
+    copies[3].wait()
+    rows = early_refs[0].shape[0] - 3 * qp
+    row = lax.broadcasted_iota(jnp.int32, (rows, LANES), 0)
+    extra = jnp.zeros((rows, LANES), F32)
+    for j in range(nb):
+        for k, ref in enumerate((profile_ref, weight_ref)):
+            value = jnp.full((rows, LANES), ref[j], F32)
+            for part in range(3):
+                piece = value.astype(BF16).astype(F32)
+                extra = jnp.where(row == (2 * j + k) * 3 + part, piece, extra)
+                value = value - piece
+    for j in range(n):
+        early_refs[j][3 * qp :, :] = extra.astype(BF16)
+
+
+def pack_late_kernel(n, me_ref, cot_hbm, *refs):
+    late_refs = refs[:n]
+    cot_ref, sem = refs[n:]
+    copy = pltpu.make_async_copy(cot_hbm, cot_ref, sem)
+    copy.start()
+    width = LANES // n
+    qc = cot_ref.shape[0] // n
+    turn = lax.rem(n - me_ref[0], n) * width
+    copy.wait()
 
     def step(i, carry):
         at = pl.multiple_of(i * 16, 16)
-        parts = [cot_ref[pl.ds(a * qc + at, 16), :].astype(F32) for a in range(n)]
-        for d, block in enumerate(swap_groups(parts, width)):
-            late_ref[d, pl.ds(at, 16), :] = block.astype(BF16)
+        parts = [
+            pltpu.roll(cot_ref[pl.ds(a * qc + at, 16), :].astype(F32), turn, 1) for a in range(n)
+        ]
+        for j, block in enumerate(swap_groups(parts, width)):
+            late_refs[j][pl.ds(at, 16), :] = block.astype(BF16)
         return carry
 
     lax.fori_loop(0, qc // 16, step, 0, unroll=4)
@@ -154,16 +167,38 @@
     return sin_v, cos_v
 
 
-def first_kernel(n, nb, pupil, field, me_ref, pos_ref, *refs):
+def first_kernel(n, nb, pupil, field, me_ref, pos_hbm, fwd_hbm, *refs):
     early_refs = refs[:n]
-    fwd_ref, e_s, f_s, aux_ref, phase_s, amp_s = refs[n:]
+    e_s, f_s, aux_ref, phase_s, amp_s, pos_ref, fwd_ref, sems = refs[n:]
+    copies = [
+        pltpu.make_async_copy(pos_hbm, pos_ref, sems.at[0]),
+        pltpu.make_async_copy(fwd_hbm, fwd_ref, sems.at[1]),
+    ]
+    for copy in copies:
+        copy.start()
     width = LANES // n
     nbins = n * nb
     qp = pupil * pupil // (n * n)
     group1 = lane_group((1, LANES), width)
 
+    me = me_ref[0]
+
+    for j in range(n):
+        d = lax.rem(me + n - j, n)
+        for q in range(0, qp, 16):
+            hi = early_refs[j][q : q + 16, :].astype(F32)
+            lo = early_refs[j][qp + q : qp + q + 16, :].astype(F32)
+            am = early_refs[j][2 * qp + q : 2 * qp + q + 16, :].astype(F32)
+            for a, (one, two) in enumerate(
+                zip(spread_groups(hi + lo, n, width), spread_groups(am, n, width))
+            ):
+                at = pl.multiple_of((d * n + a) * qp + q, 16)
+                phase_s[pl.ds(at, 16), :] = one
+                amp_s[pl.ds(at, 16), :] = two
+
+    for copy in copies:
+        copy.wait()
     pos = pos_ref[...]
-    me = me_ref[0]
     near = jnp.zeros_like(pos)
     for d in range(n):
         near = jnp.where(me == d, spread_groups(pos, n, width)[d], near)
@@ -200,19 +235,6 @@
     tilt_x = [kappa[t] * near[0:1, :] for t in range(nb)]
     tilt_y = [kappa[t] * near[1:2, :] for t in range(nb)]
 
-    for j in range(n):
-        d = lax.rem(me + n - j, n)
-        for q in range(0, qp, 16):
-            hi = early_refs[j][q : q + 16, :].astype(F32)
-            lo = early_refs[j][qp + q : qp + q + 16, :].astype(F32)
-            am = early_refs[j][2 * qp + q : 2 * qp + q + 16, :].astype(F32)
-            for a, (one, two) in enumerate(
-                zip(spread_groups(hi + lo, n, width), spread_groups(am, n, width))
-            ):
-                at = pl.multiple_of((d * n + a) * qp + q, 16)
-                phase_s[pl.ds(at, 16), :] = one
-                amp_s[pl.ds(at, 16), :] = two
-
     v_rows = lax.broadcasted_iota(jnp.int32, (pupil, LANES), 0).astype(F32) - (pupil - 1) / 2.0
     swing = [v_rows * tilt_y[t] for t in range(nb)]
     fwd = fwd_ref[...]
@@ -239,9 +261,18 @@
     lax.fori_loop(0, pupil // 4, first, 0)
 
 
-def second_kernel(
-    n, nb, pupil, field, e_s, f_s, aux_in, late_ref, fwd_ref, bwd_ref, grad_ref, stat_ref, g_s, pg_s
-):
+def second_kernel(n, nb, pupil, field, me_ref, fwd_hbm, bwd_hbm, e_s, f_s, aux_in, *refs):
+    late_refs, grad_refs = refs[:n], refs[n : 2 * n]
+    g_s, pg_s, fwd_ref, bwd_ref, sems = refs[2 * n :]
+    copies = [
+        pltpu.make_async_copy(fwd_hbm, fwd_ref, sems.at[0]),
+        pltpu.make_async_copy(bwd_hbm, bwd_ref, sems.at[1]),
+    ]
+    for copy in copies:
+        copy.start()
+    me = me_ref[0]
+    for copy in copies:
+        copy.wait()
     width = LANES // n
     qp = pupil * pupil // (n * n)
     qc = field * field // (n * n)
@@ -251,9 +282,8 @@
 
     per = qc // field
 
-    def middle(i, carry):
-        d, j = i // per, i % per
-        raw = late_ref[d, pl.ds(pl.multiple_of(j * field, field), field), :].astype(F32)
+    def middle(ref, d, j):
+        raw = ref[pl.ds(pl.multiple_of(j * field, field), field), :].astype(F32)
         for a, cot in enumerate(spread_groups(raw, n, width)):
             k1 = (d * n + a) * per + j
             parts = []
@@ -271,9 +301,13 @@
                 g_s[t, pl.ds(pl.multiple_of(k1 * 2 * pupil, 2 * pupil), 2 * pupil), :] = back[
                     :, t * LANES : (t + 1) * LANES
                 ]
-        return carry
-
-    lax.fori_loop(0, n * per, middle, 0)
+
+    for k, ref in enumerate(late_refs):
+        d = lax.rem(me + n - k, n)
+        if per == 1:
+            middle(ref, d, 0)
+        else:
+            lax.fori_loop(0, per, lambda j, carry: middle(ref, d, j) or carry, 0)
 
     def last(i, stats):
         stats = list(stats)
@@ -313,29 +347,38 @@
             stat = stat + roll(stat, step)
             step *= 2
         sums = jnp.where(lane % width == width - 1 - t, roll(stat, -t), sums)
-    for i in range(stat_ref.shape[0]):
-        stat_ref[i] = sums
-
-    def repack(d, carry):
+    group = lane_group((8, LANES), width)
+    for k, ref in enumerate(grad_refs):
+        d = lax.rem(me + k, n)
         for q in range(0, qp, 8):
             out = jnp.zeros((8, LANES), F32)
-            group = lane_group((8, LANES), width)
             for a in range(n):
                 at = pl.multiple_of((d * n + a) * qp + q, 8)
                 out = jnp.where(group == a, pg_s[pl.ds(at, 8), :], out)
-            grad_ref[d, q : q + 8, :] = out
-        return carry
-
-    lax.fori_loop(0, n, repack, 0)
-
-
-def final_kernel(n, nb, nsub_all, me_ref, grad_ref, stat_ref, aux_ref, out_ref, prof_ref):
+            ref[q : q + 8, :] = out
+        ref[qp : qp + 8, :] = jnp.broadcast_to(sums, (8, LANES))
+
+
+def sum_kernel(n, *refs):
+    refs[n][...] = sum(refs[k][...] for k in range(n))
+
+
+def grad_kernel(n, me_ref, *refs):
     width = LANES // n
-    qp = grad_ref.shape[1]
-    for a, block in enumerate(swap_groups([grad_ref[d] for d in range(n)], width)):
-        out_ref[a * qp : (a + 1) * qp, :] = block
+    out_ref = refs[n]
+    qp = out_ref.shape[0] // n
+    turn = me_ref[0] * width
+    for q in range(0, qp, 8):
+        parts = [refs[(n - i) % n][q : q + 8, :] for i in range(n)]
+        for a, block in enumerate(swap_groups(parts, width)):
+            out_ref[a * qp + q : a * qp + q + 8, :] = pltpu.roll(block, turn, 1)
+
+
+def profile_kernel(n, nb, nsub_all, me_ref, aux_ref, *refs):
+    width = LANES // n
+    prof_ref = refs[-1]
     lane = lax.broadcasted_iota(jnp.int32, (1, LANES), 1)
-    stat = jnp.sum(stat_ref[...], axis=0)
+    stat = sum(ref[...] for ref in refs[:-1])[0:1, :]
     aux = aux_ref[...]
     total = jnp.max(aux[3 * nb : 3 * nb + 1, :])
     centre = jnp.zeros((1, LANES), F32)
@@ -365,27 +408,42 @@
     vmem = pl.BlockSpec(memory_space=pltpu.VMEM)
     params = pltpu.CompilerParams(vmem_limit_bytes=VMEM_LIMIT)
 
-    any_space = pl.BlockSpec(memory_space=pl.ANY)
+    hbm = pl.BlockSpec(memory_space=pltpu.HBM)
     early_shape = (3 * qp + extra, LANES)
-    *early, late = pl.pallas_call(
-        functools.partial(pack_kernel, n, nb),
-        out_shape=[jax.ShapeDtypeStruct(early_shape, BF16)] * n
-        + [jax.ShapeDtypeStruct((n, qc, LANES), BF16)],
-        in_specs=[smem, smem, smem, any_space, any_space, any_space],
-        out_specs=[vmem] * (n + 1),
+    n_sub = lax.axis_size("sub")
+
+    def exchange(blocks, axis, size):
+        return [blocks[0]] + [
+            lax.ppermute(blocks[j], axis, [(i, (i + j) % size) for i in range(size)])
+            for j in range(1, size)
+        ]
+
+    early = pl.pallas_call(
+        functools.partial(pack_early_kernel, n, nb),
+        out_shape=[jax.ShapeDtypeStruct(early_shape, BF16)] * n,
+        in_specs=[smem, hbm, hbm, hbm, hbm],
+        out_specs=[vmem] * n,
         scratch_shapes=[
-            pltpu.VMEM(cotangent.shape, BF16),
+            pltpu.SMEM(profile.shape, F32),
+            pltpu.SMEM(alt_weight.shape, F32),
             pltpu.VMEM(amplitude.shape, BF16),
             pltpu.VMEM(phase.shape, F32),
-            pltpu.SemaphoreType.DMA((3,)),
+            pltpu.SemaphoreType.DMA((4,)),
         ],
         compiler_params=params,
-        name="pack",
-    )(me, profile, alt_weight, cotangent, amplitude, phase)
-    early = early[:1] + [
-        lax.ppermute(early[j], "alt", [(i, (i + j) % n) for i in range(n)]) for j in range(1, n)
-    ]
-    late = lax.all_to_all(late, "alt", 0, 0)
+        name="pack_early",
+    )(me, profile, alt_weight, amplitude, phase)
+    early = exchange(early, "alt", n)
+    late = pl.pallas_call(
+        functools.partial(pack_late_kernel, n),
+        out_shape=[jax.ShapeDtypeStruct((qc, LANES), BF16)] * n,
+        in_specs=[smem, hbm],
+        out_specs=[vmem] * n,
+        scratch_shapes=[pltpu.VMEM(cotangent.shape, BF16), pltpu.SemaphoreType.DMA],
+        compiler_params=params,
+        name="pack_late",
+    )(me, cotangent)
+    late = exchange(late, "alt", n)
 
     base = dft_matrix(pupil, field)
     fwd = jnp.asarray(table_three(base))
@@ -398,44 +456,60 @@
             jax.ShapeDtypeStruct((nb, 2 * pupil * field, LANES), F32),
             jax.ShapeDtypeStruct((aux_rows, LANES), F32),
         ),
-        in_specs=[smem, vmem] + [vmem] * n + [vmem],
+        in_specs=[smem, hbm, hbm] + [vmem] * n,
         out_specs=(vmem, vmem, vmem),
         scratch_shapes=[
             pltpu.VMEM((pupil * pupil, LANES), F32),
             pltpu.VMEM((pupil * pupil, LANES), F32),
+            pltpu.VMEM(position.shape, F32),
+            pltpu.VMEM(fwd.shape, BF16),
+            pltpu.SemaphoreType.DMA((2,)),
         ],
         compiler_params=params,
         name="fields",
-    )(me, position, *early, fwd)
-    devices = lax.axis_size("sub") * n
-    grad, stat = pl.pallas_call(
+    )(me, position, fwd, *early)
+    grads = pl.pallas_call(
         functools.partial(second_kernel, n, nb, pupil, field),
-        out_shape=(
-            jax.ShapeDtypeStruct((n, qp, LANES), F32),
-            jax.ShapeDtypeStruct((devices, 1, LANES), F32),
-        ),
-        in_specs=[vmem] * 6,
-        out_specs=(vmem, vmem),
+        out_shape=[jax.ShapeDtypeStruct((qp + 8, LANES), F32)] * n,
+        in_specs=[smem, hbm, hbm] + [vmem] * (3 + n),
+        out_specs=[vmem] * n,
         scratch_shapes=[
             pltpu.VMEM((nb, 2 * pupil * field, LANES), F32),
             pltpu.VMEM((pupil * pupil, LANES), F32),
+            pltpu.VMEM(fwd.shape, BF16),
+            pltpu.VMEM(bwd.shape, BF16),
+            pltpu.SemaphoreType.DMA((2,)),
         ],
         compiler_params=params,
         name="images",
-    )(e, f, aux, late, fwd, bwd)
-    grad = lax.all_to_all(grad, "alt", 0, 0)
-    stat = lax.all_to_all(stat, ("sub", "alt"), 0, 0)
-    phase_grad, profile_grad = pl.pallas_call(
-        functools.partial(final_kernel, n, nb, nsub_all),
-        out_shape=(
-            jax.ShapeDtypeStruct(phase.shape, F32),
-            jax.ShapeDtypeStruct(profile.shape, F32),
-        ),
-        in_specs=[smem, vmem, vmem, vmem],
-        out_specs=(vmem, smem),
-        compiler_params=params,
-        name="unpack",
-    )(me, grad, stat, aux)
+    )(me, fwd, bwd, e, f, aux, *late)
+    grads = exchange(grads, "alt", n)
+    stat = pl.pallas_call(
+        functools.partial(sum_kernel, n),
+        out_shape=jax.ShapeDtypeStruct((8, LANES), F32),
+        grid=(1,),
+        in_specs=[pl.BlockSpec((8, LANES), lambda i: (qp // 8, 0))] * n,
+        out_specs=pl.BlockSpec((8, LANES), lambda i: (0, 0)),
+        compiler_params=params,
+        name="group_sum",
+    )(*grads)
+    stats = exchange([stat] * n_sub, "sub", n_sub)
+    phase_grad = pl.pallas_call(
+        functools.partial(grad_kernel, n),
+        out_shape=jax.ShapeDtypeStruct(phase.shape, F32),
+        in_specs=[smem] + [vmem] * n,
+        out_specs=vmem,
+        compiler_params=params,
+        name="gradient",
+    )(me, *grads)
+    profile_grad = pl.pallas_call(
+        functools.partial(profile_kernel, n, nb, nsub_all),
+        out_shape=jax.ShapeDtypeStruct(profile.shape, F32),
+        in_specs=[smem] + [vmem] * (1 + n_sub),
+        out_specs=smem,
+        compiler_params=params,
+        name="profile",
+    )(me, aux, *stats)
     return phase_grad, profile_grad
 
 

time: 78.2 us -> 65.8 us (0.84)
  blocking collectives: 19.7 us -> 0 us
  starting transfers between devices: 12.2 us -> 20.5 us
  local copies, waits for them, and re-layouts: 11.3 us -> 6.31 us
  waiting for transfers between devices: 7.07 us -> 11.1 us
    all_to_all x2 -> x0, blocking collectives: 19.7 us -> none  [the longest x1 11.2 us: local(): stat = lax.all_to_all(stat, ('sub', 'alt'), 0, 0)]
    ppermute x3 -> x16, starting transfers between devices: 5.85 us -> 20.5 us  [exchange(): lax.ppermute(blocks[j], axis, [(i, (i + j) % size) for i in range(size)])]
    all_to_all x1 -> x0, starting transfers between devices: 6.33 us -> none  [local(): late = lax.all_to_all(late, 'alt', 0, 0)]
    unnamed x22 -> x16, local copies, waits for them, and re-layouts: 11.3 us -> 6.31 us
    ppermute x3 -> x16, waiting for transfers between devices: 7.06 us -> 11.1 us  [exchange(): lax.ppermute(blocks[j], axis, [(i, (i + j) % size) for i in range(size)])]
    pallas_call x2 -> x5, Pallas kernels: 3.58 us -> 3.36 us  [the longest x1 0.97 us: local(): pl.pallas_call(functools.partial(pack_late_kernel, n), out_shape=[jax.Sha...]
  transfers between devices with their start and end apart: 4 -> 16, of which waited for: 2 -> 6; matrix products, arithmetic and copies ran while one was open for 0% -> 0% of each run, Pallas kernels for 6% -> 11%
where the time goes in v3:
time: 65.8 us; the launch traced here: 65.5 us
  Pallas kernels  26.8 us (41%)
  starting transfers between devices  20.5 us (31%)
  waiting for transfers between devices  11.1 us (17%)
  local copies, waits for them, and re-layouts  6.31 us (10%)
  between operations  0.73 us (1%)
    ppermute x16, starting transfers between devices, exchange(): lax.ppermute(blocks[j], axis, [(i, (i + j) % size) for i in range(size)])  20.5 us
    pallas_call x1, Pallas kernels, local(): pl.pallas_call(functools.partial(second_kernel, n, nb, pupil, field), out...  18.2 us
    ppermute x16, waiting for transfers between devices, exchange(): lax.ppermute(blocks[j], axis, [(i, (i + j) % size) for i in range(size)])  11.1 us
    unnamed x16, local copies, waits for them, and re-layouts  6.31 us
    pallas_call x1, Pallas kernels, local(): pl.pallas_call(functools.partial(first_kernel, n, nb, pupil, field), out_...  5.24 us
  transfers between devices with their start and end apart: 16, of which 6 were waited for; matrix products, arithmetic and copies ran while one was open for 0% of the time, Pallas kernels for 11%

profile of v3, /device:TPU:0, one launch (start us, length us, event | category | flops | bytes accessed | tf_op | source)
XLA Modules:
  0.0 65.5 jit_solution(9218795305243989381)
XLA Ops:
  0.6 0.0 copy-start.2
  0.6 0.9 %copy-done.2 = f32[256,128]{1,0:T(8,128)S(1)} copy-done((f32[256,128]{1,0:T(8,128)S(1)}, f32[256,128]{1,0:T(8,128)}, u32[]{:S(2)}) %copy-start.2) | copy-done | bytes 131096
  1.5 0.0 copy-start.3
  1.5 0.8 %copy-done.3 = bf16[256,128]{1,0:T(8,128)(2,1)S(1)} copy-done((bf16[256,128]{1,0:T(8,128)(2,1)S(1)}, bf16[256,128]{1,0:T(8,128)(2,1)}, u32[]{:S(2)}) %copy-start.3) | copy-done | bytes 65560
  2.4 0.0 copy-start.6
  2.4 0.7 copy-done.6
  3.0 0.0 copy-start.7
  3.0 0.7 copy-done.7
  3.7 0.8 %pack_early.1 = (bf16[208,128]{1,0:T(8,128)(2,1)S(1)}, bf16[208,128]{1,0:T(8,128)(2,1)S(1)}, bf16[208,128]{1,0:T(8,128)(2,1)S(1)}, bf16[208,128]{1,0:T(8,128)(2,1)S(1)}) custom-call(s32[1]{0:T(128)} %bitcast.me_ref, f32[2]{0:T(128)S(1)} %copy-done.6, f32[2]{0:T(128)S(1)} %copy-done.7, bf16[256,128]{1,0:T(8,128)(2,1)S(1)} %copy-done.3, f32[256,128]{1,0:T(8,128)S(1)} %copy-done.2), custom_call_target="tpu_custom_call" | custom-call | tf_op jit(solution)/shard_map/pack_early/pallas_call | solution.py:421
  4.5 3.1 %collective-permute-start = (bf16[208,128]{1,0:T(8,128)(2,1)S(1)}, bf16[208,128]{1,0:T(8,128)(2,1)S(1)}, u32[]{:S(2)}, u32[]{:S(2)}) collective-permute-start(bf16[208,128]{1,0:T(8,128)(2,1)S(1)} %get-tuple-element.18), channel_id=1, source_target_pairs={{0,1},{1,2},{2,3},{3,0},{4,5},{5,6},{6,7},{7,4},{8,9},{9,10},{10,1... | collective-permute-start | bytes 159752 | tf_op jit(solution)/shard_map/ppermute | solution.py:417
  7.6 0.0 copy-start.1
  7.6 0.9 %copy-done.1 = bf16[1024,128]{1,0:T(8,128)(2,1)S(1)} copy-done((bf16[1024,128]{1,0:T(8,128)(2,1)S(1)}, bf16[1024,128]{1,0:T(8,128)(2,1)}, u32[]{:S(2)}) %copy-start.1) | copy-done | bytes 262168
  8.5 1.0 %pack_late.1 = (bf16[256,128]{1,0:T(8,128)(2,1)S(1)}, bf16[256,128]{1,0:T(8,128)(2,1)S(1)}, bf16[256,128]{1,0:T(8,128)(2,1)S(1)}, bf16[256,128]{1,0:T(8,128)(2,1)S(1)}) custom-call(s32[1]{0:T(128)} %bitcast.me_ref, bf16[1024,128]{1,0:T(8,128)(2,1)S(1)} %copy-done.1), custom_call_target="tpu_custom_call" | custom-call | tf_op jit(solution)/shard_map/pack_late/pallas_call | solution.py:437
  9.5 1.6 %collective-permute-start.3 = (bf16[256,128]{1,0:T(8,128)(2,1)S(1)}, bf16[256,128]{1,0:T(8,128)(2,1)S(1)}, u32[]{:S(2)}, u32[]{:S(2)}) collective-permute-start(bf16[256,128]{1,0:T(8,128)(2,1)S(1)} %get-tuple-element.25), channel_id=1, source_target_pairs={{0,1},{1,2},{2,3},{3,0},{4,5},{5,6},{6,7},{7,4},{8,9},{9,10},{10,1... | collective-permute-start | bytes 196616 | tf_op jit(solution)/shard_map/ppermute | solution.py:417
  11.2 1.1 %collective-permute-start.4 = (bf16[256,128]{1,0:T(8,128)(2,1)S(1)}, bf16[256,128]{1,0:T(8,128)(2,1)S(1)}, u32[]{:S(2)}, u32[]{:S(2)}) collective-permute-start(bf16[256,128]{1,0:T(8,128)(2,1)S(1)} %get-tuple-element.26), channel_id=1, source_target_pairs={{0,2},{1,3},{2,0},{3,1},{4,6},{5,7},{6,4},{7,5},{8,10},{9,11},{10,... | collective-permute-start | bytes 196616 | tf_op jit(solution)/shard_map/ppermute | solution.py:417
  12.2 2.8 %collective-permute-start.5 = (bf16[256,128]{1,0:T(8,128)(2,1)S(1)}, bf16[256,128]{1,0:T(8,128)(2,1)S(1)}, u32[]{:S(2)}, u32[]{:S(2)}) collective-permute-start(bf16[256,128]{1,0:T(8,128)(2,1)S(1)} %get-tuple-element.27), channel_id=1, source_target_pairs={{0,3},{1,0},{2,1},{3,2},{4,7},{5,4},{6,5},{7,6},{8,11},{9,8},{10,9... | collective-permute-start | bytes 196616 | tf_op jit(solution)/shard_map/ppermute | solution.py:417
  15.1 0.3 collective-permute-start.1
  15.4 0.0 collective-permute-done.refs_1_
  15.4 1.2 %collective-permute-start.2 = (bf16[208,128]{1,0:T(8,128)(2,1)S(1)}, bf16[208,128]{1,0:T(8,128)(2,1)S(1)}, u32[]{:S(2)}, u32[]{:S(2)}) collective-permute-start(bf16[208,128]{1,0:T(8,128)(2,1)S(1)} %get-tuple-element.20), channel_id=1, source_target_pairs={{0,3},{1,0},{2,1},{3,2},{4,7},{5,4},{6,5},{7,6},{8,11},{9,8},{10,9... | collective-permute-start | bytes 159752 | tf_op jit(solution)/shard_map/ppermute | solution.py:417
  16.6 5.4 %collective-permute-done.1.refs_2_ = bf16[208,128]{1,0:T(8,128)(2,1)S(1)} collective-permute-done((bf16[208,128]{1,0:T(8,128)(2,1)S(1)}, bf16[208,128]{1,0:T(8,128)(2,1)S(1)}, u32[]{:S(2)}, u32[]{:S(2)}) %collective-permute-start.1) | collective-permute-done | bytes 53280 | tf_op jit(solution)/shard_map/ppermute | solution.py:417
  22.0 0.0 collective-permute-done.2.refs_3_
  22.0 0.0 copy-start
  22.0 0.8 %copy-done = bf16[128,192]{1,0:T(8,128)(2,1)S(1)} copy-done((bf16[128,192]{1,0:T(8,128)(2,1)S(1)}, bf16[128,192]{1,0:T(8,128)(2,1)}, u32[]{:S(2)}) %copy-start) | copy-done | bytes 49176
  22.8 0.0 copy-start.5
  22.8 0.7 %copy-done.5 = f32[2,128]{1,0:T(2,128)S(1)} copy-done((f32[2,128]{1,0:T(2,128)S(1)}, f32[2,128]{1,0:T(2,128)}, u32[]{:S(2)}) %copy-start.5) | copy-done | bytes 1048
  23.5 5.2 %fields.1 = (f32[2,2048,128]{2,1,0:T(8,128)S(1)}, f32[2,4096,128]{2,1,0:T(8,128)S(1)}, f32[8,128]{1,0:T(8,128)S(1)}) custom-call(s32[1]{0:T(128)} %bitcast.me_ref, f32[2,128]{1,0:T(2,128)S(1)} %copy-done.5, bf16[128,192]{1,0:T(8,128)(2,1)S(1)} %copy-done, bf16[208,128]{1,0:T(8,128)(2,1)S(1)} %get-tuple-element.17.refs_0_, ...), custom_call_target="tpu_custom_call" | custom-call | tf_op jit(solution)/shard_map/fields/pallas_call | solution.py:452
  28.8 0.0 collective-permute-done.3.refs_1_
  28.8 0.0 collective-permute-done.4.refs_2_
  28.8 0.0 collective-permute-done.5.refs_3_
  28.8 0.0 copy-start.4
  28.8 0.8 %copy-done.4 = bf16[64,384]{1,0:T(8,128)(2,1)S(1)} copy-done((bf16[64,384]{1,0:T(8,128)(2,1)S(1)}, bf16[64,384]{1,0:T(8,128)(2,1)}, u32[]{:S(2)}) %copy-start.4) | copy-done | bytes 49176
  29.6 18.2 %images.1 = (f32[72,128]{1,0:T(8,128)S(1)}, f32[72,128]{1,0:T(8,128)S(1)}, f32[72,128]{1,0:T(8,128)S(1)}, f32[72,128]{1,0:T(8,128)S(1)}) custom-call(s32[1]{0:T(128)} %bitcast.me_ref, bf16[128,192]{1,0:T(8,128)(2,1)S(1)} %copy-done, bf16[64,384]{1,0:T(8,128)(2,1)S(1)} %copy-done.4, f32[2,2048,128]{2,1,0:T(8,128)S(1)} %get-tuple-element.21.e_s, ...), custom_call_target="tpu_custom_call" | custom-call | tf_op jit(solution)/shard_map/images/pallas_call | solution.py:471
  47.8 1.2 %collective-permute-start.6 = (f32[72,128]{1,0:T(8,128)S(1)}, f32[72,128]{1,0:T(8,128)S(1)}, u32[]{:S(2)}, u32[]{:S(2)}) collective-permute-start(f32[72,128]{1,0:T(8,128)S(1)} %get-tuple-element.29), channel_id=1, source_target_pairs={{0,1},{1,2},{2,3},{3,0},{4,5},{5,6},{6,7},{7,4},{8,9},{9,10},{10,1... | collective-permute-start | bytes 110600 | tf_op jit(solution)/shard_map/ppermute | solution.py:417
  49.0 1.9 %collective-permute-start.7 = (f32[72,128]{1,0:T(8,128)S(1)}, f32[72,128]{1,0:T(8,128)S(1)}, u32[]{:S(2)}, u32[]{:S(2)}) collective-permute-start(f32[72,128]{1,0:T(8,128)S(1)} %get-tuple-element.30), channel_id=1, source_target_pairs={{0,2},{1,3},{2,0},{3,1},{4,6},{5,7},{6,4},{7,5},{8,10},{9,11},{10,... | collective-permute-start | bytes 110600 | tf_op jit(solution)/shard_map/ppermute | solution.py:417
  50.9 0.8 %collective-permute-start.8 = (f32[72,128]{1,0:T(8,128)S(1)}, f32[72,128]{1,0:T(8,128)S(1)}, u32[]{:S(2)}, u32[]{:S(2)}) collective-permute-start(f32[72,128]{1,0:T(8,128)S(1)} %get-tuple-element.31), channel_id=1, source_target_pairs={{0,3},{1,0},{2,1},{3,2},{4,7},{5,4},{6,5},{7,6},{8,11},{9,8},{10,9... | collective-permute-start | bytes 110600 | tf_op jit(solution)/shard_map/ppermute | solution.py:417
  51.7 1.9 %collective-permute-done.6.refs_1_ = f32[72,128]{1,0:T(8,128)S(1)} collective-permute-done((f32[72,128]{1,0:T(8,128)S(1)}, f32[72,128]{1,0:T(8,128)S(1)}, u32[]{:S(2)}, u32[]{:S(2)}) %collective-permute-start.6) | collective-permute-done | bytes 36896 | tf_op jit(solution)/shard_map/ppermute | solution.py:417
  53.6 0.8 %collective-permute-done.7.refs_2_ = f32[72,128]{1,0:T(8,128)S(1)} collective-permute-done((f32[72,128]{1,0:T(8,128)S(1)}, f32[72,128]{1,0:T(8,128)S(1)}, u32[]{:S(2)}, u32[]{:S(2)}) %collective-permute-start.7) | collective-permute-done | bytes 36896 | tf_op jit(solution)/shard_map/ppermute | solution.py:417
  54.4 0.5 collective-permute-done.8.refs_3_
  54.9 1.5 %collective-permute-start.10 = (f32[8,128]{1,0:T(8,128)S(1)}, f32[8,128]{1,0:T(8,128)S(1)}, u32[]{:S(2)}, u32[]{:S(2)}) collective-permute-start(f32[8,128]{1,0:T(8,128)S(1)} %group_sum.1.refs_0_), channel_id=1, source_target_pairs={{0,8},{4,12},{8,16},{12,20},{16,24},{20,28},{24,0},{28,4},{1,9},{5... | collective-permute-start | bytes 12296 | tf_op jit(solution)/shard_map/ppermute | solution.py:417
  56.4 0.0 collective-permute-start.11
  56.4 1.5 %collective-permute-start.12 = (f32[8,128]{1,0:T(8,128)S(1)}, f32[8,128]{1,0:T(8,128)S(1)}, u32[]{:S(2)}, u32[]{:S(2)}) collective-permute-start(f32[8,128]{1,0:T(8,128)S(1)} %group_sum.1.refs_0_), channel_id=1, source_target_pairs={{0,16},{4,20},{8,24},{12,28},{16,0},{20,4},{24,8},{28,12},{1,17},{... | collective-permute-start | bytes 12296 | tf_op jit(solution)/shard_map/ppermute | solution.py:417
  57.9 1.4 %collective-permute-start.13 = (f32[8,128]{1,0:T(8,128)S(1)}, f32[8,128]{1,0:T(8,128)S(1)}, u32[]{:S(2)}, u32[]{:S(2)}) collective-permute-start(f32[8,128]{1,0:T(8,128)S(1)} %group_sum.1.refs_0_), channel_id=1, source_target_pairs={{0,20},{4,24},{8,28},{12,0},{16,4},{20,8},{24,12},{28,16},{1,21},{... | collective-permute-start | bytes 12296 | tf_op jit(solution)/shard_map/ppermute | solution.py:417
  59.3 1.4 %collective-permute-start.14 = (f32[8,128]{1,0:T(8,128)S(1)}, f32[8,128]{1,0:T(8,128)S(1)}, u32[]{:S(2)}, u32[]{:S(2)}) collective-permute-start(f32[8,128]{1,0:T(8,128)S(1)} %group_sum.1.refs_0_), channel_id=1, source_target_pairs={{0,24},{4,28},{8,0},{12,4},{16,8},{20,12},{24,16},{28,20},{1,25},{... | collective-permute-start | bytes 12296 | tf_op jit(solution)/shard_map/ppermute | solution.py:417
  60.8 0.0 collective-permute-done.10.refs_2_
  60.8 0.0 collective-permute-start.15
  60.8 0.0 collective-permute-done.11.refs_3_
  60.8 0.5 collective-permute-start.9
  61.3 0.9 %gradient.1 = f32[256,128]{1,0:T(8,128)} custom-call(s32[1]{0:T(128)} %bitcast.me_ref, f32[72,128]{1,0:T(8,128)S(1)} %get-tuple-element.28.refs_0_, f32[72,128]{1,0:T(8,128)S(1)} %collective-permute-done.6.refs_1_, f32[72,128]{1,0:T(8,128)S(1)} %collective-permute-done.7.refs_2_, f32[72,128]{1,0:T(8,128)S(1)} %collective-permute-done.8.refs_3_), custom_call_target="tpu_custom_call" | custom-call | tf_op jit(solution)/shard_map/gradient/pallas_call | solution.py:497
  62.2 0.0 collective-permute-done.12.refs_4_
  62.2 0.0 collective-permute-done.13.refs_5_
  62.2 0.8 %collective-permute-done.14.refs_6_ = f32[8,128]{1,0:T(8,128)S(1)} collective-permute-done((f32[8,128]{1,0:T(8,128)S(1)}, f32[8,128]{1,0:T(8,128)S(1)}, u32[]{:S(2)}, u32[]{:S(2)}) %collective-permute-start.14) | collective-permute-done | bytes 4128 | tf_op jit(solution)/shard_map/ppermute | solution.py:417
  63.0 0.0 collective-permute-done.15.refs_7_
  63.0 1.8 %collective-permute-done.9.refs_1_ = f32[8,128]{1,0:T(8,128)S(1)} collective-permute-done((f32[8,128]{1,0:T(8,128)S(1)}, f32[8,128]{1,0:T(8,128)S(1)}, u32[]{:S(2)}, u32[]{:S(2)}) %collective-permute-start.9) | collective-permute-done | bytes 4128 | tf_op jit(solution)/shard_map/ppermute | solution.py:417
  64.8 0.7 %profile.1 = f32[2]{0:T(128)} custom-call(s32[1]{0:T(128)} %bitcast.me_ref, f32[8,128]{1,0:T(8,128)S(1)} %get-tuple-element.23.aux_in.aux_ref, f32[8,128]{1,0:T(8,128)S(1)} %group_sum.1.refs_0_, f32[8,128]{1,0:T(8,128)S(1)} %collective-permute-done.9.refs_1_, f32[8,128]{1,0:T(8,128)S(1)} %collective-permute-done.10.refs_2_, ...), custom_call_target="tpu_custom_call" | custom-call | tf_op jit(solution)/shard_map/profile/pallas_call | solution.py:505
  (1 shorter events, 0.0 us)
Async XLA Ops:
  0.6 0.9 %copy-start.2 = (f32[256,128]{1,0:T(8,128)S(1)}, f32[256,128]{1,0:T(8,128)}, u32[]{:S(2)}) copy-start(f32[256,128]{1,0:T(8,128)} %phase_hbm.1) | copy-start | bytes 393220
  1.5 0.8 %copy-start.3 = (bf16[256,128]{1,0:T(8,128)(2,1)S(1)}, bf16[256,128]{1,0:T(8,128)(2,1)}, u32[]{:S(2)}) copy-start(bf16[256,128]{1,0:T(8,128)(2,1)} %amp_hbm.1) | copy-start | bytes 196612
  2.4 0.7 %copy-start.6 = (f32[2]{0:T(128)S(1)}, f32[2]{0:T(128)}, u32[]{:S(2)}) copy-start(f32[2]{0:T(128)} %profile_hbm.1) | copy-start | bytes 28
  3.0 0.7 %copy-start.7 = (f32[2]{0:T(128)S(1)}, f32[2]{0:T(128)}, u32[]{:S(2)}) copy-start(f32[2]{0:T(128)} %weight_hbm.1) | copy-start | bytes 28
  4.5 10.9 %collective-permute-start = (bf16[208,128]{1,0:T(8,128)(2,1)S(1)}, bf16[208,128]{1,0:T(8,128)(2,1)S(1)}, u32[]{:S(2)}, u32[]{:S(2)}) collective-permute-start(bf16[208,128]{1,0:T(8,128)(2,1)S(1)} %get-tuple-element.18), channel_id=1, source_target_pairs={{0,1},{1,2},{2,3},{3,0},{4,5},{5,6},{6,7},{7,4},{8,9},{9,10},{10,1... | collective-permute-start | bytes 159752 | tf_op jit(solution)/shard_map/ppermute | solution.py:417
  7.6 0.9 %copy-start.1 = (bf16[1024,128]{1,0:T(8,128)(2,1)S(1)}, bf16[1024,128]{1,0:T(8,128)(2,1)}, u32[]{:S(2)}) copy-start(bf16[1024,128]{1,0:T(8,128)(2,1)} %cot_hbm.1) | copy-start | bytes 786436
  9.5 19.3 %collective-permute-start.3 = (bf16[256,128]{1,0:T(8,128)(2,1)S(1)}, bf16[256,128]{1,0:T(8,128)(2,1)S(1)}, u32[]{:S(2)}, u32[]{:S(2)}) collective-permute-start(bf16[256,128]{1,0:T(8,128)(2,1)S(1)} %get-tuple-element.25), channel_id=1, source_target_pairs={{0,1},{1,2},{2,3},{3,0},{4,5},{5,6},{6,7},{7,4},{8,9},{9,10},{10,1... | collective-permute-start | bytes 196616 | tf_op jit(solution)/shard_map/ppermute | solution.py:417
  11.2 17.6 %collective-permute-start.4 = (bf16[256,128]{1,0:T(8,128)(2,1)S(1)}, bf16[256,128]{1,0:T(8,128)(2,1)S(1)}, u32[]{:S(2)}, u32[]{:S(2)}) collective-permute-start(bf16[256,128]{1,0:T(8,128)(2,1)S(1)} %get-tuple-element.26), channel_id=1, source_target_pairs={{0,2},{1,3},{2,0},{3,1},{4,6},{5,7},{6,4},{7,5},{8,10},{9,11},{10,... | collective-permute-start | bytes 196616 | tf_op jit(solution)/shard_map/ppermute | solution.py:417
  12.2 16.6 %collective-permute-start.5 = (bf16[256,128]{1,0:T(8,128)(2,1)S(1)}, bf16[256,128]{1,0:T(8,128)(2,1)S(1)}, u32[]{:S(2)}, u32[]{:S(2)}) collective-permute-start(bf16[256,128]{1,0:T(8,128)(2,1)S(1)} %get-tuple-element.27), channel_id=1, source_target_pairs={{0,3},{1,0},{2,1},{3,2},{4,7},{5,4},{6,5},{7,6},{8,11},{9,8},{10,9... | collective-permute-start | bytes 196616 | tf_op jit(solution)/shard_map/ppermute | solution.py:417
  15.1 6.9 %collective-permute-start.1 = (bf16[208,128]{1,0:T(8,128)(2,1)S(1)}, bf16[208,128]{1,0:T(8,128)(2,1)S(1)}, u32[]{:S(2)}, u32[]{:S(2)}) collective-permute-start(bf16[208,128]{1,0:T(8,128)(2,1)S(1)} %get-tuple-element.19), channel_id=1, source_target_pairs={{0,2},{1,3},{2,0},{3,1},{4,6},{5,7},{6,4},{7,5},{8,10},{9,11},{10,... | collective-permute-start | bytes 159752 | tf_op jit(solution)/shard_map/ppermute | solution.py:417
  15.4 6.6 %collective-permute-start.2 = (bf16[208,128]{1,0:T(8,128)(2,1)S(1)}, bf16[208,128]{1,0:T(8,128)(2,1)S(1)}, u32[]{:S(2)}, u32[]{:S(2)}) collective-permute-start(bf16[208,128]{1,0:T(8,128)(2,1)S(1)} %get-tuple-element.20), channel_id=1, source_target_pairs={{0,3},{1,0},{2,1},{3,2},{4,7},{5,4},{6,5},{7,6},{8,11},{9,8},{10,9... | collective-permute-start | bytes 159752 | tf_op jit(solution)/shard_map/ppermute | solution.py:417
  22.0 0.8 %copy-start = (bf16[128,192]{1,0:T(8,128)(2,1)S(1)}, bf16[128,192]{1,0:T(8,128)(2,1)}, u32[]{:S(2)}) copy-start(bf16[128,192]{1,0:T(8,128)(2,1)} %constant.8.clone.fwd_hbm) | copy-start | bytes 147460
  22.8 0.7 %copy-start.5 = (f32[2,128]{1,0:T(2,128)S(1)}, f32[2,128]{1,0:T(2,128)}, u32[]{:S(2)}) copy-start(f32[2,128]{1,0:T(2,128)} %pos_hbm.1) | copy-start | bytes 3076
  28.8 0.8 %copy-start.4 = (bf16[64,384]{1,0:T(8,128)(2,1)S(1)}, bf16[64,384]{1,0:T(8,128)(2,1)}, u32[]{:S(2)}) copy-start(bf16[64,384]{1,0:T(8,128)(2,1)} %constant.9.clone.bwd_hbm) | copy-start | bytes 147460
  47.8 5.8 %collective-permute-start.6 = (f32[72,128]{1,0:T(8,128)S(1)}, f32[72,128]{1,0:T(8,128)S(1)}, u32[]{:S(2)}, u32[]{:S(2)}) collective-permute-start(f32[72,128]{1,0:T(8,128)S(1)} %get-tuple-element.29), channel_id=1, source_target_pairs={{0,1},{1,2},{2,3},{3,0},{4,5},{5,6},{6,7},{7,4},{8,9},{9,10},{10,1... | collective-permute-start | bytes 110600 | tf_op jit(solution)/shard_map/ppermute | solution.py:417
  49.0 5.4 %collective-permute-start.7 = (f32[72,128]{1,0:T(8,128)S(1)}, f32[72,128]{1,0:T(8,128)S(1)}, u32[]{:S(2)}, u32[]{:S(2)}) collective-permute-start(f32[72,128]{1,0:T(8,128)S(1)} %get-tuple-element.30), channel_id=1, source_target_pairs={{0,2},{1,3},{2,0},{3,1},{4,6},{5,7},{6,4},{7,5},{8,10},{9,11},{10,... | collective-permute-start | bytes 110600 | tf_op jit(solution)/shard_map/ppermute | solution.py:417
  50.9 4.0 %collective-permute-start.8 = (f32[72,128]{1,0:T(8,128)S(1)}, f32[72,128]{1,0:T(8,128)S(1)}, u32[]{:S(2)}, u32[]{:S(2)}) collective-permute-start(f32[72,128]{1,0:T(8,128)S(1)} %get-tuple-element.31), channel_id=1, source_target_pairs={{0,3},{1,0},{2,1},{3,2},{4,7},{5,4},{6,5},{7,6},{8,11},{9,8},{10,9... | collective-permute-start | bytes 110600 | tf_op jit(solution)/shard_map/ppermute | solution.py:417
  54.9 5.9 %collective-permute-start.10 = (f32[8,128]{1,0:T(8,128)S(1)}, f32[8,128]{1,0:T(8,128)S(1)}, u32[]{:S(2)}, u32[]{:S(2)}) collective-permute-start(f32[8,128]{1,0:T(8,128)S(1)} %group_sum.1.refs_0_), channel_id=1, source_target_pairs={{0,8},{4,12},{8,16},{12,20},{16,24},{20,28},{24,0},{28,4},{1,9},{5... | collective-permute-start | bytes 12296 | tf_op jit(solution)/shard_map/ppermute | solution.py:417
  56.4 4.4 %collective-permute-start.11 = (f32[8,128]{1,0:T(8,128)S(1)}, f32[8,128]{1,0:T(8,128)S(1)}, u32[]{:S(2)}, u32[]{:S(2)}) collective-permute-start(f32[8,128]{1,0:T(8,128)S(1)} %group_sum.1.refs_0_), channel_id=1, source_target_pairs={{0,12},{4,16},{8,20},{12,24},{16,28},{20,0},{24,4},{28,8},{1,13},{... | collective-permute-start | bytes 12296 | tf_op jit(solution)/shard_map/ppermute | solution.py:417
  56.4 5.8 %collective-permute-start.12 = (f32[8,128]{1,0:T(8,128)S(1)}, f32[8,128]{1,0:T(8,128)S(1)}, u32[]{:S(2)}, u32[]{:S(2)}) collective-permute-start(f32[8,128]{1,0:T(8,128)S(1)} %group_sum.1.refs_0_), channel_id=1, source_target_pairs={{0,16},{4,20},{8,24},{12,28},{16,0},{20,4},{24,8},{28,12},{1,17},{... | collective-permute-start | bytes 12296 | tf_op jit(solution)/shard_map/ppermute | solution.py:417
  57.9 4.3 %collective-permute-start.13 = (f32[8,128]{1,0:T(8,128)S(1)}, f32[8,128]{1,0:T(8,128)S(1)}, u32[]{:S(2)}, u32[]{:S(2)}) collective-permute-start(f32[8,128]{1,0:T(8,128)S(1)} %group_sum.1.refs_0_), channel_id=1, source_target_pairs={{0,20},{4,24},{8,28},{12,0},{16,4},{20,8},{24,12},{28,16},{1,21},{... | collective-permute-start | bytes 12296 | tf_op jit(solution)/shard_map/ppermute | solution.py:417
  59.3 3.6 %collective-permute-start.14 = (f32[8,128]{1,0:T(8,128)S(1)}, f32[8,128]{1,0:T(8,128)S(1)}, u32[]{:S(2)}, u32[]{:S(2)}) collective-permute-start(f32[8,128]{1,0:T(8,128)S(1)} %group_sum.1.refs_0_), channel_id=1, source_target_pairs={{0,24},{4,28},{8,0},{12,4},{16,8},{20,12},{24,16},{28,20},{1,25},{... | collective-permute-start | bytes 12296 | tf_op jit(solution)/shard_map/ppermute | solution.py:417
  60.8 2.2 %collective-permute-start.15 = (f32[8,128]{1,0:T(8,128)S(1)}, f32[8,128]{1,0:T(8,128)S(1)}, u32[]{:S(2)}, u32[]{:S(2)}) collective-permute-start(f32[8,128]{1,0:T(8,128)S(1)} %group_sum.1.refs_0_), channel_id=1, source_target_pairs={{0,28},{4,0},{8,4},{12,8},{16,12},{20,16},{24,20},{28,24},{1,29},{... | collective-permute-start | bytes 12296 | tf_op jit(solution)/shard_map/ppermute | solution.py:417
  60.8 4.0 %collective-permute-start.9 = (f32[8,128]{1,0:T(8,128)S(1)}, f32[8,128]{1,0:T(8,128)S(1)}, u32[]{:S(2)}, u32[]{:S(2)}) collective-permute-start(f32[8,128]{1,0:T(8,128)S(1)} %group_sum.1.refs_0_), channel_id=1, source_target_pairs={{0,4},{4,8},{8,12},{12,16},{16,20},{20,24},{24,28},{28,0},{1,5},{5... | collective-permute-start | bytes 12296 | tf_op jit(solution)/shard_map/ppermute | solution.py:417

commit v4 on v3

v4 whole, which is shorter than its diff:
```python
import functools
import math

import jax
import jax.numpy as jnp
import ml_dtypes
import numpy as np
from jax import lax
from jax.experimental import pallas as pl
from jax.experimental.pallas import tpu as pltpu
from jax.sharding import PartitionSpec as P

ELONG = 0.75
LANES = 128
VMEM_LIMIT = 44 * 1024 * 1024
F32 = jnp.float32
BF16 = jnp.bfloat16


CHUNK = 512


def halves(pupil, field, fun):
    freq = np.arange(field // 2) + 0.5
    place = (pupil - 1) / 2.0 - np.arange(pupil // 2)
    return fun(2.0 * np.pi / field * np.outer(freq, place))


def hi_lo(matrix):
    hi = matrix.astype(np.float32).astype(ml_dtypes.bfloat16)
    lo = (matrix - hi.astype(np.float64)).astype(np.float32).astype(ml_dtypes.bfloat16)
    return np.concatenate([hi, lo], axis=1)


def tables(pupil, field):
    fun = (np.cos, np.sin)
    fwd, bwd = [], []
    for b in range(2):
        for a in range(2):
            t = np.kron(halves(pupil, field, fun[a]), halves(pupil, field, fun[b]))
            fwd.append(hi_lo(t))
            rows = min(CHUNK, t.shape[0])
            bwd.append(
                np.stack([hi_lo(t[m : m + rows].T) for m in range(0, t.shape[0], rows)])
            )
    return np.stack(fwd), np.stack(bwd)


def split(x):
    hi = x.astype(BF16)
    return hi, (x - hi.astype(F32)).astype(BF16)


def dot_three(table, depth, hi, lo):
    wide = jnp.concatenate([table, table[:, :depth]], axis=1)
    return jnp.dot(wide, jnp.concatenate([hi, hi, lo], axis=0), preferred_element_type=F32)


def lane_group(shape, width):
    return lax.broadcasted_iota(jnp.int32, shape, len(shape) - 1) // width


def roll(x, shift):
    return pltpu.roll(x, shift % LANES, x.ndim - 1)


def swap_groups(blocks, width):
    n = len(blocks)
    blocks = list(blocks)
    group = lane_group(blocks[0].shape, width)
    step = 1
    while step < n:
        low = (group & step) == 0
        for i in range(n):
            if i & step:
                continue
            j = i + step
            a, b = blocks[i], blocks[j]
            blocks[i] = jnp.where(low, a, roll(b, step * width))
            blocks[j] = jnp.where(low, roll(a, -step * width), b)
        step *= 2
    return blocks


def spread_groups(x, n, width):
    group = lane_group(x.shape, width)
    out = [x]
    step = n // 2
    while step >= 1:
        low = (group & step) == 0
        made = []
        for y in out:
            up, down = roll(y, step * width), roll(y, -step * width)
            made.append(jnp.where(low, y, up))
            made.append(jnp.where(low, down, y))
        out = made
        step //= 2
    return out


def reverse_rows(x):
    row = lax.broadcasted_iota(jnp.int32, (8, LANES), 0)
    parts = []
    for i in range(x.shape[0] - 8, -1, -8):
        y = pltpu.roll(x[i : i + 8], 4, 0)
        y = jnp.where((row & 2) == 0, pltpu.roll(y, 6, 0), pltpu.roll(y, 2, 0))
        y = jnp.where((row & 1) == 0, pltpu.roll(y, 7, 0), pltpu.roll(y, 1, 0))
        parts.append(y)
    return jnp.concatenate(parts, axis=0)


def pack_kernel(n, nb, me_ref, profile_hbm, weight_hbm, amp_hbm, phase_hbm, cot_hbm, *refs):
    out_refs = refs[:n]
    profile_ref, weight_ref, amp_ref, phase_ref, cot_ref, sems = refs[n:]
    pairs = (
        (phase_hbm, phase_ref),
        (amp_hbm, amp_ref),
        (profile_hbm, profile_ref),
        (weight_hbm, weight_ref),
        (cot_hbm, cot_ref),
    )
    copies = [pltpu.make_async_copy(src, dst, sems.at[i]) for i, (src, dst) in enumerate(pairs)]
    for copy in copies:
        copy.start()
    width = LANES // n
    qp = phase_ref.shape[0] // n
    qc = cot_ref.shape[0] // n
    turn = lax.rem(n - me_ref[0], n) * width
    for copy in copies:
        copy.wait()
    for q in range(0, qp, 16):
        parts = [pltpu.roll(phase_ref[a * qp + q : a * qp + q + 16, :], turn, 1) for a in range(n)]
        for j, block in enumerate(swap_groups(parts, width)):
            hi, lo = split(block)
            out_refs[j][q : q + 16, :] = hi
            out_refs[j][qp + q : qp + q + 16, :] = lo
    for q in range(0, qp, 16):
        parts = [
            pltpu.roll(amp_ref[a * qp + q : a * qp + q + 16, :].astype(F32), turn, 1)
            for a in range(n)
        ]
        for j, block in enumerate(swap_groups(parts, width)):
            out_refs[j][2 * qp + q : 2 * qp + q + 16, :] = block.astype(BF16)

    def step(i, carry):
        at = pl.multiple_of(i * 16, 16)
        parts = [
            pltpu.roll(cot_ref[pl.ds(a * qc + at, 16), :].astype(F32), turn, 1) for a in range(n)
        ]
        for j, block in enumerate(swap_groups(parts, width)):
            out_refs[j][pl.ds(3 * qp + at, 16), :] = block.astype(BF16)
        return carry

    lax.fori_loop(0, qc // 16, step, 0, unroll=4)
    base = 3 * qp + qc
    rows = out_refs[0].shape[0] - base
    row = lax.broadcasted_iota(jnp.int32, (rows, LANES), 0)
    extra = jnp.zeros((rows, LANES), F32)
    for j in range(nb):
        for k, ref in enumerate((profile_ref, weight_ref)):
            value = jnp.full((rows, LANES), ref[j], F32)
            for part in range(3):
                piece = value.astype(BF16).astype(F32)
                extra = jnp.where(row == (2 * j + k) * 3 + part, piece, extra)
                value = value - piece
    for j in range(n):
        out_refs[j][base:, :] = extra.astype(BF16)


def sincos(x):
    turns = jnp.round(x * (2.0 / math.pi))
    r = x - turns * 1.5703125
    r = r - turns * 4.838267948966e-4
    r2 = r * r
    s = r + r * r2 * (-1.6666654611e-1 + r2 * (8.3321608736e-3 + r2 * -1.9515295891e-4))
    c = (1.0 - 0.5 * r2) + r2 * r2 * (
        4.166664568298827e-2 + r2 * (-1.388731625493765e-3 + r2 * 2.443315711809948e-5)
    )
    quad = turns.astype(jnp.int32)
    odd = (quad & 1) != 0
    sin_v = jnp.where(odd, c, s)
    cos_v = jnp.where(odd, s, c)
    sin_v = jnp.where((quad & 2) != 0, -sin_v, sin_v)
    cos_v = jnp.where(((quad + 1) & 2) != 0, -cos_v, cos_v)
    return sin_v, cos_v


def spots_kernel(n, nb, pupil, field, me_ref, pos_hbm, fwd_hbm, bwd_hbm, *refs):
    in_refs, grad_refs, aux_ref = refs[:n], refs[n : 2 * n], refs[2 * n]
    (
        phase_s, amp_s, cot_s, e_s, x_s, p_s, y_s, g_s, pg_s, pos_ref, fwd_ref, bwd_ref, sems
    ) = refs[2 * n + 1 :]
    copies = [
        pltpu.make_async_copy(pos_hbm, pos_ref, sems.at[0]),
        pltpu.make_async_copy(fwd_hbm, fwd_ref, sems.at[1]),
        pltpu.make_async_copy(bwd_hbm, bwd_ref, sems.at[2]),
    ]
    for copy in copies:
        copy.start()
    width = LANES // n
    nbins = n * nb
    qp = pupil * pupil // (n * n)
    qc = field * field // (n * n)
    half, fhalf = pupil // 2, field // 2
    wide = nb * LANES
    me = me_ref[0]
    group1 = lane_group((1, LANES), width)
    owner = [lax.rem(me + n - j, n) for j in range(n)]

    for j in range(n):
        for q in range(0, qp, 16):
            hi = in_refs[j][q : q + 16, :].astype(F32)
            lo = in_refs[j][qp + q : qp + q + 16, :].astype(F32)
            am = in_refs[j][2 * qp + q : 2 * qp + q + 16, :].astype(F32)
            turned = [(a * qp + q) % pupil >= half for a in range(n)]
            for src, dst in ((hi + lo, phase_s), (am, amp_s)):
                ways = {
                    way: spread_groups(reverse_rows(src) if way else src, n, width)
                    for way in set(turned)
                }
                for a in range(n):
                    line = (a * qp + q) // pupil * pupil + (half if turned[a] else 0)
                    part = (a * qp + q) % half
                    part = half - 16 - part if turned[a] else part
                    at = pl.multiple_of(owner[j] * (n * qp) + line + part, 16)
                    dst[pl.ds(at, 16), :] = ways[turned[a]][a]

    per = qc // field
    for j in range(n):
        low = owner[j] < n // 2
        sign = jnp.where(low, 0, 1)

        def place(i, carry):
            for q in range(0, field, 16):
                at = pl.multiple_of(3 * qp + i * field + q, 16)
                raw = in_refs[j][pl.ds(at, 16), :].astype(F32)
                raw = reverse_rows(raw) if q >= fhalf else raw
                col = field - 16 - q if q >= fhalf else q
                for a, cot in enumerate(spread_groups(raw, n, width)):
                    k1 = (owner[j] * n + a) * per + i
                    line = jnp.where(low, k1, field - 1 - k1)
                    at = pl.multiple_of(line * fhalf + col, 16)
                    cot_s[sign, int(q >= fhalf), pl.ds(at, 16), :] = cot
            return carry

        lax.fori_loop(0, per, place, 0)

    prof, wgt = [], []
    for t in range(nb):
        p_row, w_row = jnp.zeros((1, LANES), F32), jnp.zeros((1, LANES), F32)
        for j in range(n):
            extra = in_refs[j][3 * qp + qc :, :].astype(F32)
            rows = [extra[6 * t + i : 6 * t + i + 1, :] for i in range(6)]
            p_row = jnp.where(group1 == owner[j], rows[0] + rows[1] + rows[2], p_row)
            w_row = jnp.where(group1 == owner[j], rows[3] + rows[4] + rows[5], w_row)
        prof.append(p_row)
        wgt.append(w_row)
    total = sum(prof)
    step = n // 2
    while step >= 1:
        total = total + roll(total, step * width)
        step //= 2
    coef = [2.0 / (pupil * pupil) * prof[t] * wgt[t] / total for t in range(nb)]
    aux = jnp.zeros(aux_ref.shape, F32)
    row = lax.broadcasted_iota(jnp.int32, aux_ref.shape, 0)
    for t in range(nb):
        aux = jnp.where(row == nb + t, prof[t], aux)
        aux = jnp.where(row == 2 * nb + t, wgt[t], aux)
    aux_ref[...] = jnp.where(row == 3 * nb, total, aux)

    copies[0].wait()
    pos = pos_ref[...]
    near = jnp.zeros_like(pos)
    for d, one in enumerate(spread_groups(pos, n, width)):
        near = jnp.where(me == d, one, near)
    shift = math.pi / field
    tilt_x, tilt_y = [], []
    for t in range(nb):
        kappa = ELONG * (2.0 * (group1 * nb + t).astype(F32) / (nbins - 1) - 1.0)
        tilt_x.append(kappa * near[0:1, :] + shift)
        tilt_y.append(kappa * near[1:2, :] + shift)

    row = lax.broadcasted_iota(jnp.int32, (pupil, LANES), 0)
    u_rows = jnp.where(row < half, row, pupil + half - 1 - row).astype(F32) - (pupil - 1) / 2.0
    lean = [u_rows * tilt_x[t] for t in range(nb)]

    def fields(i, carry):
        at16 = pl.multiple_of(i * half, half)
        for t in range(nb):
            found = []
            for r in (i, pupil - 1 - i):
                at = pl.multiple_of(r * pupil, pupil)
                v = r.astype(F32) - (pupil - 1) / 2.0
                am = amp_s[pl.ds(at, pupil), :]
                sin_v, cos_v = sincos(phase_s[pl.ds(at, pupil), :] + (lean[t] + v * tilt_y[t]))
                one = (am * cos_v, am * sin_v)
                for k in range(2):
                    e_s[t, k, pl.ds(at, pupil), :] = one[k]
                found.append(one)
            for k in range(2):
                even, odd = found[1][k] + found[0][k], found[1][k] - found[0][k]
                classes = (
                    even[half:] + even[:half],
                    odd[half:] + odd[:half],
                    even[half:] - even[:half],
                    odd[half:] - odd[:half],
                )
                lanes = pl.ds(k * wide + t * LANES, LANES)
                for c, x in enumerate(classes):
                    hi, lo = split(x)
                    x_s[c, 0, pl.ds(at16, half), lanes] = hi
                    x_s[c, 1, pl.ds(at16, half), lanes] = lo
        return carry

    lax.fori_loop(0, half, fields, 0)

    depth = half * half
    rows_all = fhalf * fhalf
    chunk = min(CHUNK, rows_all)
    copies[1].wait()
    copies[2].wait()

    def images(m, first):
        base = m * chunk
        for c in range(4):
            table = fwd_ref[c, pl.ds(pl.multiple_of(base, chunk), chunk), :]
            for k in range(2):
                lanes = pl.ds(k * wide, wide)
                p_s[c, k] = dot_three(table, depth, x_s[c, 0, :, lanes], x_s[c, 1, :, lanes])

        def weigh(i, carry):
            at = pl.multiple_of(i * 16, 16)
            there = pl.multiple_of(base + i * 16, 16)
            cot = [cot_s[a, b, pl.ds(there, 16), :] for a in range(2) for b in range(2)]
            for t in range(nb):
                lanes = pl.ds(t * LANES, LANES)
                re = [p_s[c, 0, pl.ds(at, 16), lanes] for c in range(4)]
                im = [p_s[c, 1, pl.ds(at, 16), lanes] for c in range(4)]
                s0, s1, s2, s3 = re[0] + im[1], re[0] - im[1], im[2] - re[3], im[2] + re[3]
                y = [cot[0] * (s0 + s2), cot[1] * (s0 - s2), cot[2] * (s1 + s3), cot[3] * (s1 - s3)]
                s0, s1, s2, s3 = im[0] - re[1], im[0] + re[1], re[2] + im[3], re[2] - im[3]
                z = [cot[0] * (s0 - s2), cot[1] * (s0 + s2), cot[2] * (s1 - s3), cot[3] * (s1 + s3)]
                yp, ym, yd, ye = y[0] + y[1], y[2] + y[3], y[0] - y[1], y[2] - y[3]
                zp, zm, zd, ze = z[0] + z[1], z[2] + z[3], z[0] - z[1], z[2] - z[3]
                back = (
                    (yp + ym, zp + zm),
                    (zm - zp, yp - ym),
                    (-ze - zd, yd + ye),
                    (ye - yd, ze - zd),
                )
                for c in range(4):
                    for k in range(2):
                        hi, lo = split(back[c][k])
                        lanes = pl.ds(k * wide + t * LANES, LANES)
                        y_s[c, 0, pl.ds(at, 16), lanes] = hi
                        y_s[c, 1, pl.ds(at, 16), lanes] = lo
            return carry

        lax.fori_loop(0, chunk // 16, weigh, 0, unroll=2)
        for c in range(4):
            table = bwd_ref[c, m]
            for k in range(2):
                lanes = pl.ds(k * wide, wide)
                out = dot_three(table, chunk, y_s[c, 0, :, lanes], y_s[c, 1, :, lanes])
                g_s[c, k] = out if first else g_s[c, k] + out

    images(0, True)
    if rows_all > chunk:
        lax.fori_loop(1, rows_all // chunk, lambda m, carry: images(m, False) or carry, 0)

    def products(i, stats):
        stats = list(stats)
        at16 = pl.multiple_of(i * half, half)
        grads = [jnp.zeros((pupil, LANES), F32) for _ in range(2)]
        spots = [pl.multiple_of(r * pupil, pupil) for r in (i, pupil - 1 - i)]
        for t in range(nb):
            found = []
            for k in range(2):
                g = [g_s[c, k, pl.ds(at16, half), pl.ds(t * LANES, LANES)] for c in range(4)]
                even = jnp.concatenate([g[0] - g[2], g[0] + g[2]], axis=0)
                odd = jnp.concatenate([g[1] - g[3], g[1] + g[3]], axis=0)
                found.append((even - odd, even + odd))
            for which in range(2):
                e_re = e_s[t, 0, pl.ds(spots[which], pupil), :]
                e_im = e_s[t, 1, pl.ds(spots[which], pupil), :]
                g_re, g_im = found[0][which], found[1][which]
                stats[t] = stats[t] + (e_re * g_re + e_im * g_im)
                grads[which] = grads[which] + coef[t] * (e_re * g_im - e_im * g_re)
        for which in range(2):
            grad = grads[which]
            step = n // 2
            while step >= 1:
                grad = grad + roll(grad, step * width)
                step //= 2
            grad = jnp.concatenate([grad[:half], reverse_rows(grad[half:])], axis=0)
            pg_s[pl.ds(spots[which], pupil), :] = grad
        return tuple(stats)

    stats = lax.fori_loop(0, half, products, tuple(jnp.zeros((pupil, LANES), F32) for _ in range(nb)))

    lane = lax.broadcasted_iota(jnp.int32, (1, LANES), 1)
    sums = jnp.zeros((1, LANES), F32)
    for t in range(nb):
        stat = jnp.sum(stats[t], axis=0, keepdims=True) * (1.0 / (pupil * pupil))
        step = 1
        while step < width:
            stat = stat + roll(stat, step)
            step *= 2
        sums = jnp.where(lane % width == width - 1 - t, roll(stat, -t), sums)
    group = lane_group((8, LANES), width)
    for k, ref in enumerate(grad_refs):
        d = lax.rem(me + k, n)
        for q in range(0, qp, 8):
            out = jnp.zeros((8, LANES), F32)
            for a in range(n):
                at = pl.multiple_of((d * n + a) * qp + q, 8)
                out = jnp.where(group == a, pg_s[pl.ds(at, 8), :], out)
            ref[q : q + 8, :] = out
        ref[qp : qp + 8, :] = jnp.broadcast_to(sums, (8, LANES))


def sum_kernel(n, *refs):
    refs[n][...] = jnp.broadcast_to(sum(refs[k][...] for k in range(n))[None], refs[n].shape)


def grad_kernel(n, me_ref, *refs):
    width = LANES // n
    out_ref = refs[n]
    qp = out_ref.shape[0] // n
    turn = me_ref[0] * width
    for q in range(0, qp, 8):
        parts = [refs[(n - i) % n][q : q + 8, :] for i in range(n)]
        for a, block in enumerate(swap_groups(parts, width)):
            out_ref[a * qp + q : a * qp + q + 8, :] = pltpu.roll(block, turn, 1)


def profile_kernel(n, nb, nsub_all, me_ref, aux_ref, stat_ref, prof_ref):
    width = LANES // n
    lane = lax.broadcasted_iota(jnp.int32, (1, LANES), 1)
    stat = jnp.sum(stat_ref[...], axis=0)[0:1, :]
    aux = aux_ref[...]
    total = jnp.max(aux[3 * nb : 3 * nb + 1, :])
    centre = jnp.zeros((1, LANES), F32)
    own = []
    for t in range(nb):
        prof, wgt = aux[nb + t : nb + t + 1], aux[2 * nb + t : 2 * nb + t + 1]
        term = stat * wgt
        centre += jnp.where(lane % width == width - 1 - t, term * prof, 0.0)
        own.append(jnp.sum(jnp.where(lane == (me_ref[0] + 1) * width - 1 - t, term, 0.0)))
    centre = jnp.sum(centre)
    for t in range(nb):
        prof_ref[t] = (own[t] / total - centre / (total * total)) / nsub_all


def local(cotangent, amplitude, phase, position, profile, alt_weight):
    n = lax.axis_size("alt")
    n_sub = lax.axis_size("sub")
    nsub_all = n_sub * phase.shape[1]
    nb = profile.shape[0]
    pupil = math.isqrt(n * phase.shape[0])
    field = math.isqrt(n * cotangent.shape[0])
    qp = phase.shape[0] // n
    qc = cotangent.shape[0] // n
    extra = -(-6 * nb // 16) * 16
    me = lax.axis_index("alt").astype(jnp.int32).reshape(1)
    smem = pl.BlockSpec(memory_space=pltpu.SMEM)
    vmem = pl.BlockSpec(memory_space=pltpu.VMEM)
    hbm = pl.BlockSpec(memory_space=pltpu.HBM)
    params = pltpu.CompilerParams(vmem_limit_bytes=VMEM_LIMIT)

    def keep(*arrays):
        return [pltpu.with_memory_space_constraint(x, pltpu.HBM) for x in arrays]

    def exchange(blocks):
        return [blocks[0]] + [
            lax.ppermute(blocks[j], "alt", [(i, (i + j) % n) for i in range(n)])
            for j in range(1, n)
        ]

    blocks = pl.pallas_call(
        functools.partial(pack_kernel, n, nb),
        out_shape=[jax.ShapeDtypeStruct((3 * qp + qc + extra, LANES), BF16)] * n,
        in_specs=[smem] + [hbm] * 5,
        out_specs=[vmem] * n,
        scratch_shapes=[
            pltpu.SMEM(profile.shape, F32),
            pltpu.SMEM(alt_weight.shape, F32),
            pltpu.VMEM(amplitude.shape, BF16),
            pltpu.VMEM(phase.shape, F32),
            pltpu.VMEM(cotangent.shape, BF16),
            pltpu.SemaphoreType.DMA((5,)),
        ],
        compiler_params=params,
        name="pack",
    )(me, *keep(profile, alt_weight, amplitude, phase, cotangent))
    blocks = exchange(blocks)

    fwd, bwd = (jnp.asarray(x) for x in tables(pupil, field))
    depth = pupil * pupil // 4
    rows_all = field * field // 4
    chunk = min(CHUNK, rows_all)
    wide = nb * LANES
    aux_rows = -(-(3 * nb + 1) // 8) * 8
    *grads, aux = pl.pallas_call(
        functools.partial(spots_kernel, n, nb, pupil, field),
        out_shape=[jax.ShapeDtypeStruct((qp + 8, LANES), F32)] * n
        + [jax.ShapeDtypeStruct((aux_rows, LANES), F32)],
        in_specs=[smem] + [hbm] * 3 + [vmem] * n,
        out_specs=[vmem] * (n + 1),
        scratch_shapes=[
            pltpu.VMEM((pupil * pupil, LANES), F32),
            pltpu.VMEM((pupil * pupil, LANES), F32),
            pltpu.VMEM((2, 2, rows_all, LANES), F32),
            pltpu.VMEM((nb, 2, pupil * pupil, LANES), F32),
            pltpu.VMEM((4, 2, depth, 2 * wide), BF16),
            pltpu.VMEM((4, 2, chunk, wide), F32),
            pltpu.VMEM((4, 2, chunk, 2 * wide), BF16),
            pltpu.VMEM((4, 2, depth, wide), F32),
            pltpu.VMEM((pupil * pupil, LANES), F32),
            pltpu.VMEM(position.shape, F32),
            pltpu.VMEM(fwd.shape, BF16),
            pltpu.VMEM(bwd.shape, BF16),
            pltpu.SemaphoreType.DMA((3,)),
        ],
        compiler_params=params,
        name="spots",
    )(me, *keep(position, fwd, bwd), *blocks)
    grads = exchange(grads)
    stat = pl.pallas_call(
        functools.partial(sum_kernel, n),
        out_shape=jax.ShapeDtypeStruct((n_sub, 8, LANES), F32),
        grid=(1,),
        in_specs=[pl.BlockSpec((8, LANES), lambda i: (qp // 8, 0))] * n,
        out_specs=pl.BlockSpec((n_sub, 8, LANES), lambda i: (0, 0, 0)),
        compiler_params=params,
        name="group_sum",
    )(*grads)
    stat = lax.all_to_all(stat, "sub", 0, 0)
    phase_grad = pl.pallas_call(
        functools.partial(grad_kernel, n),
        out_shape=jax.ShapeDtypeStruct(phase.shape, F32),
        in_specs=[smem] + [vmem] * n,
        out_specs=vmem,
        compiler_params=params,
        name="gradient",
    )(me, *grads)
    profile_grad = pl.pallas_call(
        functools.partial(profile_kernel, n, nb, nsub_all),
        out_shape=jax.ShapeDtypeStruct(profile.shape, F32),
        in_specs=[smem, vmem, vmem],
        out_specs=smem,
        compiler_params=params,
        name="profile",
    )(me, aux, stat)
    return phase_grad, profile_grad


def solution(mesh):
    placed = (P("alt", "sub"), P("alt", "sub"), P("alt", "sub"), P(None, "sub"), P("alt"), P("alt"))
    return jax.shard_map(
        local, mesh=mesh, in_specs=placed, out_specs=(P("alt", "sub"), P("alt")), check_vma=False
    )
```

time: 65.8 us -> 55.1 us (0.84)
  local copies, waits for them, and re-layouts: 6.31 us -> 0 us
  starting transfers between devices: 20.5 us -> 16.2 us
  waiting for transfers between devices: 11.1 us -> 13.6 us
  Pallas kernels: 26.8 us -> 24.4 us
    ppermute x16 -> x6, starting transfers between devices: 20.5 us -> 12.5 us  [exchange(): lax.ppermute(blocks[j], 'alt', [(i, (i + j) % n) for i in range(n)])]
    unnamed x16 -> x0, local copies, waits for them, and re-layouts: 6.31 us -> none
    all_to_all x0 -> x1, waiting for transfers between devices: none -> 3.94 us  [local(): stat = lax.all_to_all(stat, 'sub', 0, 0)]
    all_to_all x0 -> x1, starting transfers between devices: none -> 3.72 us  [local(): stat = lax.all_to_all(stat, 'sub', 0, 0)]
    pallas_call x4 -> x2, Pallas kernels: 25.2 us -> 22.2 us  [the longest x1 19.9 us: local(): pl.pallas_call(functools.partial(spots_kernel, n, nb, pupil, field), out_...]
    ppermute x16 -> x6, waiting for transfers between devices: 11.1 us -> 9.65 us  [exchange(): lax.ppermute(blocks[j], 'alt', [(i, (i + j) % n) for i in range(n)])]
  transfers between devices with their start and end apart: 16 -> 7, of which waited for: 6 -> 6; matrix products, arithmetic and copies ran while one was open for 0% -> 0% of each run, Pallas kernels for 11% -> 2%
where the time goes in v4:
time: 55.1 us; the launch traced here: 54.9 us
  Pallas kernels  24.4 us (44%)
  starting transfers between devices  16.2 us (29%)
  waiting for transfers between devices  13.6 us (25%)
  between operations  0.66 us (1%)
    pallas_call x1, Pallas kernels, local(): pl.pallas_call(functools.partial(spots_kernel, n, nb, pupil, field), out_...  19.9 us
    ppermute x6, starting transfers between devices, exchange(): lax.ppermute(blocks[j], 'alt', [(i, (i + j) % n) for i in range(n)])  12.5 us
    ppermute x6, waiting for transfers between devices, exchange(): lax.ppermute(blocks[j], 'alt', [(i, (i + j) % n) for i in range(n)])  9.65 us
    all_to_all x1, waiting for transfers between devices, local(): stat = lax.all_to_all(stat, 'sub', 0, 0)  3.94 us
    all_to_all x1, starting transfers between devices, local(): stat = lax.all_to_all(stat, 'sub', 0, 0)  3.72 us
    pallas_call x1, Pallas kernels, local(): pl.pallas_call(functools.partial(pack_kernel, n, nb), out_shape=[jax.Shap...  2.37 us
  transfers between devices with their start and end apart: 7, of which 6 were waited for; matrix products, arithmetic and copies ran while one was open for 0% of the time, Pallas kernels for 2%

profile of v4, /device:TPU:0, one launch (start us, length us, event | category | flops | bytes accessed | tf_op | source)
XLA Modules:
  0.0 54.9 jit_solution(6320786665964711618)
XLA Ops:
  0.6 2.4 %pack.1 = (bf16[464,128]{1,0:T(8,128)(2,1)S(1)}, bf16[464,128]{1,0:T(8,128)(2,1)S(1)}, bf16[464,128]{1,0:T(8,128)(2,1)S(1)}, bf16[464,128]{1,0:T(8,128)(2,1)S(1)}) custom-call(s32[1]{0:T(128)} %bitcast.me_ref, f32[2]{0:T(128)} %profile_hbm.1, f32[2]{0:T(128)} %weight_hbm.1, bf16[256,128]{1,0:T(8,128)(2,1)} %amp_hbm.1, f32[256,128]{1,0:T(8,128)} %phase_hbm.1, ...), custom_call_target="tpu_custom_call" | custom-call | tf_op jit(solution)/shard_map/pack/pallas_call | solution.py:480
  3.0 3.1 %collective-permute-start = (bf16[464,128]{1,0:T(8,128)(2,1)S(1)}, bf16[464,128]{1,0:T(8,128)(2,1)S(1)}, u32[]{:S(2)}, u32[]{:S(2)}) collective-permute-start(bf16[464,128]{1,0:T(8,128)(2,1)S(1)} %get-tuple-element.12), channel_id=1, source_target_pairs={{0,1},{1,2},{2,3},{3,0},{4,5},{5,6},{6,7},{7,4},{8,9},{9,10},{10,1... | collective-permute-start | bytes 356360 | tf_op jit(solution)/shard_map/ppermute | solution.py:476
  6.1 2.6 %collective-permute-start.1 = (bf16[464,128]{1,0:T(8,128)(2,1)S(1)}, bf16[464,128]{1,0:T(8,128)(2,1)S(1)}, u32[]{:S(2)}, u32[]{:S(2)}) collective-permute-start(bf16[464,128]{1,0:T(8,128)(2,1)S(1)} %get-tuple-element.13), channel_id=1, source_target_pairs={{0,2},{1,3},{2,0},{3,1},{4,6},{5,7},{6,4},{7,5},{8,10},{9,11},{10,... | collective-permute-start | bytes 356360 | tf_op jit(solution)/shard_map/ppermute | solution.py:476
  8.7 1.3 %collective-permute-start.2 = (bf16[464,128]{1,0:T(8,128)(2,1)S(1)}, bf16[464,128]{1,0:T(8,128)(2,1)S(1)}, u32[]{:S(2)}, u32[]{:S(2)}) collective-permute-start(bf16[464,128]{1,0:T(8,128)(2,1)S(1)} %get-tuple-element.14), channel_id=1, source_target_pairs={{0,3},{1,0},{2,1},{3,2},{4,7},{5,4},{6,5},{7,6},{8,11},{9,8},{10,9... | collective-permute-start | bytes 356360 | tf_op jit(solution)/shard_map/ppermute | solution.py:476
  10.0 2.2 %collective-permute-done.refs_1_ = bf16[464,128]{1,0:T(8,128)(2,1)S(1)} collective-permute-done((bf16[464,128]{1,0:T(8,128)(2,1)S(1)}, bf16[464,128]{1,0:T(8,128)(2,1)S(1)}, u32[]{:S(2)}, u32[]{:S(2)}) %collective-permute-start) | collective-permute-done | bytes 118816 | tf_op jit(solution)/shard_map/ppermute | solution.py:476
  12.3 4.3 %collective-permute-done.1.refs_2_ = bf16[464,128]{1,0:T(8,128)(2,1)S(1)} collective-permute-done((bf16[464,128]{1,0:T(8,128)(2,1)S(1)}, bf16[464,128]{1,0:T(8,128)(2,1)S(1)}, u32[]{:S(2)}, u32[]{:S(2)}) %collective-permute-start.1) | collective-permute-done | bytes 118816 | tf_op jit(solution)/shard_map/ppermute | solution.py:476
  16.5 0.0 collective-permute-done.2.refs_3_
  16.5 19.9 %spots.1 = (f32[72,128]{1,0:T(8,128)S(1)}, f32[72,128]{1,0:T(8,128)S(1)}, f32[72,128]{1,0:T(8,128)S(1)}, f32[72,128]{1,0:T(8,128)S(1)}, f32[8,128]{1,0:T(8,128)S(1)}) custom-call(s32[1]{0:T(128)} %bitcast.me_ref, f32[2,128]{1,0:T(2,128)} %pos_hbm.1, bf16[4,1024,512]{2,1,0:T(8,128)(2,1)} %constant.8.clone.fwd_hbm, ...), custom_call_target="tpu_custom_call" | custom-call | tf_op jit(solution)/shard_map/spots/pallas_call | solution.py:504
  36.4 3.1 %collective-permute-start.3 = (f32[72,128]{1,0:T(8,128)S(1)}, f32[72,128]{1,0:T(8,128)S(1)}, u32[]{:S(2)}, u32[]{:S(2)}) collective-permute-start(f32[72,128]{1,0:T(8,128)S(1)} %get-tuple-element.16), channel_id=1, source_target_pairs={{0,1},{1,2},{2,3},{3,0},{4,5},{5,6},{6,7},{7,4},{8,9},{9,10},{10,1... | collective-permute-start | bytes 110600 | tf_op jit(solution)/shard_map/ppermute | solution.py:476
  39.5 1.6 %collective-permute-start.4 = (f32[72,128]{1,0:T(8,128)S(1)}, f32[72,128]{1,0:T(8,128)S(1)}, u32[]{:S(2)}, u32[]{:S(2)}) collective-permute-start(f32[72,128]{1,0:T(8,128)S(1)} %get-tuple-element.17), channel_id=1, source_target_pairs={{0,2},{1,3},{2,0},{3,1},{4,6},{5,7},{6,4},{7,5},{8,10},{9,11},{10,... | collective-permute-start | bytes 110600 | tf_op jit(solution)/shard_map/ppermute | solution.py:476
  41.1 0.8 %collective-permute-start.5 = (f32[72,128]{1,0:T(8,128)S(1)}, f32[72,128]{1,0:T(8,128)S(1)}, u32[]{:S(2)}, u32[]{:S(2)}) collective-permute-start(f32[72,128]{1,0:T(8,128)S(1)} %get-tuple-element.18), channel_id=1, source_target_pairs={{0,3},{1,0},{2,1},{3,2},{4,7},{5,4},{6,5},{7,6},{8,11},{9,8},{10,9... | collective-permute-start | bytes 110600 | tf_op jit(solution)/shard_map/ppermute | solution.py:476
  41.9 0.6 %collective-permute-done.3.refs_1_ = f32[72,128]{1,0:T(8,128)S(1)} collective-permute-done((f32[72,128]{1,0:T(8,128)S(1)}, f32[72,128]{1,0:T(8,128)S(1)}, u32[]{:S(2)}, u32[]{:S(2)}) %collective-permute-start.3) | collective-permute-done | bytes 36896 | tf_op jit(solution)/shard_map/ppermute | solution.py:476
  42.5 2.0 %collective-permute-done.4.refs_2_ = f32[72,128]{1,0:T(8,128)S(1)} collective-permute-done((f32[72,128]{1,0:T(8,128)S(1)}, f32[72,128]{1,0:T(8,128)S(1)}, u32[]{:S(2)}, u32[]{:S(2)}) %collective-permute-start.4) | collective-permute-done | bytes 36896 | tf_op jit(solution)/shard_map/ppermute | solution.py:476
  44.5 0.6 %collective-permute-done.5.refs_3_ = f32[72,128]{1,0:T(8,128)S(1)} collective-permute-done((f32[72,128]{1,0:T(8,128)S(1)}, f32[72,128]{1,0:T(8,128)S(1)}, u32[]{:S(2)}, u32[]{:S(2)}) %collective-permute-start.5) | collective-permute-done | bytes 36896 | tf_op jit(solution)/shard_map/ppermute | solution.py:476
  45.1 0.6 %group_sum.1 = f32[8,8,128]{2,1,0:T(8,128)} custom-call(f32[72,128]{1,0:T(8,128)S(1)} %get-tuple-element.15.refs_0_, f32[72,128]{1,0:T(8,128)S(1)} %collective-permute-done.3.refs_1_, f32[72,128]{1,0:T(8,128)S(1)} %collective-permute-done.4.refs_2_, f32[72,128]{1,0:T(8,128)S(1)} %collective-permute-done.5.refs_3_), custom_call_target="tpu_custom_call" | custom-call | tf_op jit(solution)/shard_map/group_sum/pallas_call | solution.py:529
  45.7 3.7 %all-to-all-start = ((f32[8,8,128]{2,1,0:T(8,128)}), f32[8,8,128]{2,1,0:T(8,128)S(1)}, u32[]{:S(2)}, u32[]{:S(2)}) async-start(f32[8,8,128]{2,1,0:T(8,128)} %group_sum.1), calls=%async_computation | async-start | bytes 65536 | tf_op jit(solution)/shard_map/all_to_all | solution.py:538
  49.4 0.9 %gradient.1 = f32[256,128]{1,0:T(8,128)} custom-call(s32[1]{0:T(128)} %bitcast.me_ref, f32[72,128]{1,0:T(8,128)S(1)} %get-tuple-element.15.refs_0_, f32[72,128]{1,0:T(8,128)S(1)} %collective-permute-done.3.refs_1_, f32[72,128]{1,0:T(8,128)S(1)} %collective-permute-done.4.refs_2_, f32[72,128]{1,0:T(8,128)S(1)} %collective-permute-done.5.refs_3_), custom_call_target="tpu_custom_call" | custom-call | tf_op jit(solution)/shard_map/gradient/pallas_call | solution.py:539
  50.3 3.9 %all-to-all-done.stat_ref = f32[8,8,128]{2,1,0:T(8,128)S(1)} async-done(((f32[8,8,128]{2,1,0:T(8,128)}), f32[8,8,128]{2,1,0:T(8,128)S(1)}, u32[]{:S(2)}, u32[]{:S(2)}) %all-to-all-start) | async-done | bytes 32800 | tf_op jit(solution)/shard_map/all_to_all | solution.py:538
  54.2 0.7 %profile.1 = f32[2]{0:T(128)} custom-call(s32[1]{0:T(128)} %bitcast.me_ref, f32[8,128]{1,0:T(8,128)S(1)} %get-tuple-element.19.aux_ref, f32[8,8,128]{2,1,0:T(8,128)S(1)} %all-to-all-done.stat_ref), custom_call_target="tpu_custom_call" | custom-call | tf_op jit(solution)/shard_map/profile/pallas_call | solution.py:547
Async XLA Ops:
  3.0 9.3 %collective-permute-start = (bf16[464,128]{1,0:T(8,128)(2,1)S(1)}, bf16[464,128]{1,0:T(8,128)(2,1)S(1)}, u32[]{:S(2)}, u32[]{:S(2)}) collective-permute-start(bf16[464,128]{1,0:T(8,128)(2,1)S(1)} %get-tuple-element.12), channel_id=1, source_target_pairs={{0,1},{1,2},{2,3},{3,0},{4,5},{5,6},{6,7},{7,4},{8,9},{9,10},{10,1... | collective-permute-start | bytes 356360 | tf_op jit(solution)/shard_map/ppermute | solution.py:476
  6.1 10.4 %collective-permute-start.1 = (bf16[464,128]{1,0:T(8,128)(2,1)S(1)}, bf16[464,128]{1,0:T(8,128)(2,1)S(1)}, u32[]{:S(2)}, u32[]{:S(2)}) collective-permute-start(bf16[464,128]{1,0:T(8,128)(2,1)S(1)} %get-tuple-element.13), channel_id=1, source_target_pairs={{0,2},{1,3},{2,0},{3,1},{4,6},{5,7},{6,4},{7,5},{8,10},{9,11},{10,... | collective-permute-start | bytes 356360 | tf_op jit(solution)/shard_map/ppermute | solution.py:476
  8.7 7.9 %collective-permute-start.2 = (bf16[464,128]{1,0:T(8,128)(2,1)S(1)}, bf16[464,128]{1,0:T(8,128)(2,1)S(1)}, u32[]{:S(2)}, u32[]{:S(2)}) collective-permute-start(bf16[464,128]{1,0:T(8,128)(2,1)S(1)} %get-tuple-element.14), channel_id=1, source_target_pairs={{0,3},{1,0},{2,1},{3,2},{4,7},{5,4},{6,5},{7,6},{8,11},{9,8},{10,9... | collective-permute-start | bytes 356360 | tf_op jit(solution)/shard_map/ppermute | solution.py:476
  36.4 6.1 %collective-permute-start.3 = (f32[72,128]{1,0:T(8,128)S(1)}, f32[72,128]{1,0:T(8,128)S(1)}, u32[]{:S(2)}, u32[]{:S(2)}) collective-permute-start(f32[72,128]{1,0:T(8,128)S(1)} %get-tuple-element.16), channel_id=1, source_target_pairs={{0,1},{1,2},{2,3},{3,0},{4,5},{5,6},{6,7},{7,4},{8,9},{9,10},{10,1... | collective-permute-start | bytes 110600 | tf_op jit(solution)/shard_map/ppermute | solution.py:476
  39.5 5.0 %collective-permute-start.4 = (f32[72,128]{1,0:T(8,128)S(1)}, f32[72,128]{1,0:T(8,128)S(1)}, u32[]{:S(2)}, u32[]{:S(2)}) collective-permute-start(f32[72,128]{1,0:T(8,128)S(1)} %get-tuple-element.17), channel_id=1, source_target_pairs={{0,2},{1,3},{2,0},{3,1},{4,6},{5,7},{6,4},{7,5},{8,10},{9,11},{10,... | collective-permute-start | bytes 110600 | tf_op jit(solution)/shard_map/ppermute | solution.py:476
  41.1 4.0 %collective-permute-start.5 = (f32[72,128]{1,0:T(8,128)S(1)}, f32[72,128]{1,0:T(8,128)S(1)}, u32[]{:S(2)}, u32[]{:S(2)}) collective-permute-start(f32[72,128]{1,0:T(8,128)S(1)} %get-tuple-element.18), channel_id=1, source_target_pairs={{0,3},{1,0},{2,1},{3,2},{4,7},{5,4},{6,5},{7,6},{8,11},{9,8},{10,9... | collective-permute-start | bytes 110600 | tf_op jit(solution)/shard_map/ppermute | solution.py:476
  45.7 8.6 %all-to-all-start = ((f32[8,8,128]{2,1,0:T(8,128)}), f32[8,8,128]{2,1,0:T(8,128)S(1)}, u32[]{:S(2)}, u32[]{:S(2)}) async-start(f32[8,8,128]{2,1,0:T(8,128)} %group_sum.1), calls=%async_computation | async-start | bytes 65536 | tf_op jit(solution)/shard_map/all_to_all | solution.py:538

commit v5 on v4

--- a/solution.py
+++ b/solution.py
@@ -17,7 +17,7 @@
 BF16 = jnp.bfloat16
 
 
-CHUNK = 512
+CHUNK = 1024
 
 
 def halves(pupil, field, fun):
@@ -186,10 +186,10 @@
 
 
 def spots_kernel(n, nb, pupil, field, me_ref, pos_hbm, fwd_hbm, bwd_hbm, *refs):
-    in_refs, grad_refs, aux_ref = refs[:n], refs[n : 2 * n], refs[2 * n]
+    in_refs, grad_refs, aux_ref, stat_ref = refs[:n], refs[n : 2 * n], refs[2 * n], refs[2 * n + 1]
     (
         phase_s, amp_s, cot_s, e_s, x_s, p_s, y_s, g_s, pg_s, pos_ref, fwd_ref, bwd_ref, sems
-    ) = refs[2 * n + 1 :]
+    ) = refs[2 * n + 2 :]
     copies = [
         pltpu.make_async_copy(pos_hbm, pos_ref, sems.at[0]),
         pltpu.make_async_copy(fwd_hbm, fwd_ref, sems.at[1]),
@@ -407,6 +407,7 @@
             stat = stat + roll(stat, step)
             step *= 2
         sums = jnp.where(lane % width == width - 1 - t, roll(stat, -t), sums)
+    stat_ref[...] = jnp.broadcast_to(sums, stat_ref.shape)
     group = lane_group((8, LANES), width)
     for k, ref in enumerate(grad_refs):
         d = lax.rem(me + k, n)
@@ -416,28 +417,19 @@
                 at = pl.multiple_of((d * n + a) * qp + q, 8)
                 out = jnp.where(group == a, pg_s[pl.ds(at, 8), :], out)
             ref[q : q + 8, :] = out
-        ref[qp : qp + 8, :] = jnp.broadcast_to(sums, (8, LANES))
-
-
-def sum_kernel(n, *refs):
-    refs[n][...] = jnp.broadcast_to(sum(refs[k][...] for k in range(n))[None], refs[n].shape)
-
-
-def grad_kernel(n, me_ref, *refs):
+
+
+def final_kernel(n, nb, nsub_all, me_ref, aux_ref, stat_ref, *refs):
     width = LANES // n
-    out_ref = refs[n]
+    out_ref, prof_ref = refs[n:]
     qp = out_ref.shape[0] // n
     turn = me_ref[0] * width
     for q in range(0, qp, 8):
         parts = [refs[(n - i) % n][q : q + 8, :] for i in range(n)]
         for a, block in enumerate(swap_groups(parts, width)):
             out_ref[a * qp + q : a * qp + q + 8, :] = pltpu.roll(block, turn, 1)
-
-
-def profile_kernel(n, nb, nsub_all, me_ref, aux_ref, stat_ref, prof_ref):
-    width = LANES // n
     lane = lax.broadcasted_iota(jnp.int32, (1, LANES), 1)
-    stat = jnp.sum(stat_ref[...], axis=0)[0:1, :]
+    stat = jnp.sum(stat_ref[...], axis=0, keepdims=True)
     aux = aux_ref[...]
     total = jnp.max(aux[3 * nb : 3 * nb + 1, :])
     centre = jnp.zeros((1, LANES), F32)
@@ -501,12 +493,12 @@
     chunk = min(CHUNK, rows_all)
     wide = nb * LANES
     aux_rows = -(-(3 * nb + 1) // 8) * 8
-    *grads, aux = pl.pallas_call(
+    *grads, aux, stat = pl.pallas_call(
         functools.partial(spots_kernel, n, nb, pupil, field),
-        out_shape=[jax.ShapeDtypeStruct((qp + 8, LANES), F32)] * n
-        + [jax.ShapeDtypeStruct((aux_rows, LANES), F32)],
+        out_shape=[jax.ShapeDtypeStruct((qp, LANES), F32)] * n
+        + [jax.ShapeDtypeStruct((rows, LANES), F32) for rows in (aux_rows, n_sub * n)],
         in_specs=[smem] + [hbm] * 3 + [vmem] * n,
-        out_specs=[vmem] * (n + 1),
+        out_specs=[vmem] * (n + 2),
         scratch_shapes=[
             pltpu.VMEM((pupil * pupil, LANES), F32),
             pltpu.VMEM((pupil * pupil, LANES), F32),
@@ -525,34 +517,19 @@
         compiler_params=params,
         name="spots",
     )(me, *keep(position, fwd, bwd), *blocks)
+    stat = lax.all_to_all(stat, ("sub", "alt"), 0, 0, tiled=True)
     grads = exchange(grads)
-    stat = pl.pallas_call(
-        functools.partial(sum_kernel, n),
-        out_shape=jax.ShapeDtypeStruct((n_sub, 8, LANES), F32),
-        grid=(1,),
-        in_specs=[pl.BlockSpec((8, LANES), lambda i: (qp // 8, 0))] * n,
-        out_specs=pl.BlockSpec((n_sub, 8, LANES), lambda i: (0, 0, 0)),
+    return pl.pallas_call(
+        functools.partial(final_kernel, n, nb, nsub_all),
+        out_shape=(
+            jax.ShapeDtypeStruct(phase.shape, F32),
+            jax.ShapeDtypeStruct(profile.shape, F32),
+        ),
+        in_specs=[smem, vmem, vmem] + [vmem] * n,
+        out_specs=(vmem, smem),
         compiler_params=params,
-        name="group_sum",
-    )(*grads)
-    stat = lax.all_to_all(stat, "sub", 0, 0)
-    phase_grad = pl.pallas_call(
-        functools.partial(grad_kernel, n),
-        out_shape=jax.ShapeDtypeStruct(phase.shape, F32),
-        in_specs=[smem] + [vmem] * n,
-        out_specs=vmem,
-        compiler_params=params,
-        name="gradient",
-    )(me, *grads)
-    profile_grad = pl.pallas_call(
-        functools.partial(profile_kernel, n, nb, nsub_all),
-        out_shape=jax.ShapeDtypeStruct(profile.shape, F32),
-        in_specs=[smem, vmem, vmem],
-        out_specs=smem,
-        compiler_params=params,
-        name="profile",
-    )(me, aux, stat)
-    return phase_grad, profile_grad
+        name="finish",
+    )(me, aux, stat, *grads)
 
 
 def solution(mesh):

time: 55.1 us -> 54 us (0.980)
  blocking collectives: 0 us -> 11.2 us
  waiting for transfers between devices: 13.6 us -> 6.51 us
  starting transfers between devices: 16.2 us -> 12.5 us
  Pallas kernels: 24.4 us -> 23 us
    all_to_all x0 -> x1, blocking collectives: none -> 11.2 us  [local(): stat = lax.all_to_all(stat, ('sub', 'alt'), 0, 0, tiled=True)]
    all_to_all x1 -> x0, waiting for transfers between devices: 3.94 us -> none  [local(): stat = lax.all_to_all(stat, 'sub', 0, 0)]
    all_to_all x1 -> x0, starting transfers between devices: 3.72 us -> none  [local(): stat = lax.all_to_all(stat, 'sub', 0, 0)]
    ppermute x6, waiting for transfers between devices: 9.65 us -> 6.51 us  [exchange(): lax.ppermute(blocks[j], 'alt', [(i, (i + j) % n) for i in range(n)])]
    pallas_call x3 -> x1, Pallas kernels: 2.19 us -> 0.93 us  [local(): pl.pallas_call(functools.partial(final_kernel, n, nb, nsub_all), out_shap...]
  transfers between devices with their start and end apart: 7 -> 6, of which waited for: 6 -> 2; matrix products, arithmetic and copies ran while one was open for 0% -> 0% of each run, Pallas kernels for 2% -> 0%
where the time goes in v5:
time: 54 us; the launch traced here: 53.9 us
  Pallas kernels  23 us (43%)
  starting transfers between devices  12.5 us (23%)
  blocking collectives  11.2 us (21%)
  waiting for transfers between devices  6.51 us (12%)
  between operations  0.66 us (1%)
    pallas_call x1, Pallas kernels, local(): pl.pallas_call(functools.partial(spots_kernel, n, nb, pupil, field), out_...  19.7 us
    ppermute x6, starting transfers between devices, exchange(): lax.ppermute(blocks[j], 'alt', [(i, (i + j) % n) for i in range(n)])  12.5 us
    all_to_all x1, blocking collectives, local(): stat = lax.all_to_all(stat, ('sub', 'alt'), 0, 0, tiled=True)  11.2 us
    ppermute x6, waiting for transfers between devices, exchange(): lax.ppermute(blocks[j], 'alt', [(i, (i + j) % n) for i in range(n)])  6.51 us
    pallas_call x1, Pallas kernels, local(): pl.pallas_call(functools.partial(pack_kernel, n, nb), out_shape=[jax.Shap...  2.37 us
  transfers between devices with their start and end apart: 6, of which 2 were waited for; matrix products, arithmetic and copies ran while one was open for 0% of the time, Pallas kernels for 0%

profile of v5, /device:TPU:0, one launch (start us, length us, event | category | flops | bytes accessed | tf_op | source)
XLA Modules:
  0.0 53.9 jit_solution(13416216454067758024)
XLA Ops:
  0.6 2.4 %pack.1 = (bf16[464,128]{1,0:T(8,128)(2,1)S(1)}, bf16[464,128]{1,0:T(8,128)(2,1)S(1)}, bf16[464,128]{1,0:T(8,128)(2,1)S(1)}, bf16[464,128]{1,0:T(8,128)(2,1)S(1)}) custom-call(s32[1]{0:T(128)} %bitcast.me_ref, f32[2]{0:T(128)} %profile_hbm.1, f32[2]{0:T(128)} %weight_hbm.1, bf16[256,128]{1,0:T(8,128)(2,1)} %amp_hbm.1, f32[256,128]{1,0:T(8,128)} %phase_hbm.1, ...), custom_call_target="tpu_custom_call" | custom-call | tf_op jit(solution)/shard_map/pack/pallas_call | solution.py:472
  3.0 3.1 %collective-permute-start = (bf16[464,128]{1,0:T(8,128)(2,1)S(1)}, bf16[464,128]{1,0:T(8,128)(2,1)S(1)}, u32[]{:S(2)}, u32[]{:S(2)}) collective-permute-start(bf16[464,128]{1,0:T(8,128)(2,1)S(1)} %get-tuple-element.13), channel_id=1, source_target_pairs={{0,1},{1,2},{2,3},{3,0},{4,5},{5,6},{6,7},{7,4},{8,9},{9,10},{10,1... | collective-permute-start | bytes 356360 | tf_op jit(solution)/shard_map/ppermute | solution.py:468
  6.1 2.6 %collective-permute-start.1 = (bf16[464,128]{1,0:T(8,128)(2,1)S(1)}, bf16[464,128]{1,0:T(8,128)(2,1)S(1)}, u32[]{:S(2)}, u32[]{:S(2)}) collective-permute-start(bf16[464,128]{1,0:T(8,128)(2,1)S(1)} %get-tuple-element.14), channel_id=1, source_target_pairs={{0,2},{1,3},{2,0},{3,1},{4,6},{5,7},{6,4},{7,5},{8,10},{9,11},{10,... | collective-permute-start | bytes 356360 | tf_op jit(solution)/shard_map/ppermute | solution.py:468
  8.7 1.3 %collective-permute-start.2 = (bf16[464,128]{1,0:T(8,128)(2,1)S(1)}, bf16[464,128]{1,0:T(8,128)(2,1)S(1)}, u32[]{:S(2)}, u32[]{:S(2)}) collective-permute-start(bf16[464,128]{1,0:T(8,128)(2,1)S(1)} %get-tuple-element.15), channel_id=1, source_target_pairs={{0,3},{1,0},{2,1},{3,2},{4,7},{5,4},{6,5},{7,6},{8,11},{9,8},{10,9... | collective-permute-start | bytes 356360 | tf_op jit(solution)/shard_map/ppermute | solution.py:468
  10.0 2.2 %collective-permute-done.refs_1_ = bf16[464,128]{1,0:T(8,128)(2,1)S(1)} collective-permute-done((bf16[464,128]{1,0:T(8,128)(2,1)S(1)}, bf16[464,128]{1,0:T(8,128)(2,1)S(1)}, u32[]{:S(2)}, u32[]{:S(2)}) %collective-permute-start) | collective-permute-done | bytes 118816 | tf_op jit(solution)/shard_map/ppermute | solution.py:468
  12.3 4.3 %collective-permute-done.1.refs_2_ = bf16[464,128]{1,0:T(8,128)(2,1)S(1)} collective-permute-done((bf16[464,128]{1,0:T(8,128)(2,1)S(1)}, bf16[464,128]{1,0:T(8,128)(2,1)S(1)}, u32[]{:S(2)}, u32[]{:S(2)}) %collective-permute-start.1) | collective-permute-done | bytes 118816 | tf_op jit(solution)/shard_map/ppermute | solution.py:468
  16.5 0.0 collective-permute-done.2.refs_3_
  16.5 19.7 %spots.1 = (f32[64,128]{1,0:T(8,128)S(1)}, f32[64,128]{1,0:T(8,128)S(1)}, f32[64,128]{1,0:T(8,128)S(1)}, f32[64,128]{1,0:T(8,128)S(1)}, f32[8,128]{1,0:T(8,128)S(1)}, /*index=5*/f32[32,128]{1,0:T(8,128)S(1)}) custom-call(s32[1]{0:T(128)} %bitcast.me_ref, f32[2,128]{1,0:T(2,128)} %pos_hbm.1, bf16[4,1024,512]{2,1,0:T(8,128)(2,1)} %constant.8.clone.fwd_hbm, ...), custom_call_target="tpu_custom_call" | custom-call | tf_op jit(solution)/shard_map/spots/pallas_call | solution.py:496
  36.2 3.1 %collective-permute-start.3 = (f32[64,128]{1,0:T(8,128)S(1)}, f32[64,128]{1,0:T(8,128)S(1)}, u32[]{:S(2)}, u32[]{:S(2)}) collective-permute-start(f32[64,128]{1,0:T(8,128)S(1)} %get-tuple-element.19), channel_id=1, source_target_pairs={{0,1},{1,2},{2,3},{3,0},{4,5},{5,6},{6,7},{7,4},{8,9},{9,10},{10,1... | collective-permute-start | bytes 98312 | tf_op jit(solution)/shard_map/ppermute | solution.py:468
  39.3 1.6 %collective-permute-start.4 = (f32[64,128]{1,0:T(8,128)S(1)}, f32[64,128]{1,0:T(8,128)S(1)}, u32[]{:S(2)}, u32[]{:S(2)}) collective-permute-start(f32[64,128]{1,0:T(8,128)S(1)} %get-tuple-element.20), channel_id=1, source_target_pairs={{0,2},{1,3},{2,0},{3,1},{4,6},{5,7},{6,4},{7,5},{8,10},{9,11},{10,... | collective-permute-start | bytes 98312 | tf_op jit(solution)/shard_map/ppermute | solution.py:468
  40.9 0.8 %collective-permute-start.5 = (f32[64,128]{1,0:T(8,128)S(1)}, f32[64,128]{1,0:T(8,128)S(1)}, u32[]{:S(2)}, u32[]{:S(2)}) collective-permute-start(f32[64,128]{1,0:T(8,128)S(1)} %get-tuple-element.21), channel_id=1, source_target_pairs={{0,3},{1,0},{2,1},{3,2},{4,7},{5,4},{6,5},{7,6},{8,11},{9,8},{10,9... | collective-permute-start | bytes 98312 | tf_op jit(solution)/shard_map/ppermute | solution.py:468
  41.7 11.2 %all_to_all.11 = f32[32,1,128]{2,1,0:T(1,128)S(1)} all-to-all(f32[32,1,128]{2,1,0:T(1,128)S(1)} %bitcast.6), channel_id=1, replica_groups=mesh['sub'=8,'alt'=4] {'sub','alt'}, dimensions={0} | all-to-all | bytes 32768 | tf_op jit(solution)/shard_map/all_to_all | solution.py:520
  52.9 0.0 collective-permute-done.3.refs_1_
  52.9 0.0 collective-permute-done.4.refs_2_
  52.9 0.0 collective-permute-done.5.refs_3_
  52.9 0.9 %finish.1 = (f32[256,128]{1,0:T(8,128)}, f32[2]{0:T(128)}) custom-call(s32[1]{0:T(128)} %bitcast.me_ref, f32[8,128]{1,0:T(8,128)S(1)} %get-tuple-element.16.aux_ref, f32[32,128]{1,0:T(8,128)S(1)} %bitcast.5, f32[64,128]{1,0:T(8,128)S(1)} %get-tuple-element.18.refs_0_, f32[64,128]{1,0:T(8,128)S(1)} %collective-permute-done.3.refs_1_, ...), custom_call_target="tpu_custom_call" | custom-call | tf_op jit(solution)/shard_map/finish/pallas_call | solution.py:522
Async XLA Ops:
  3.0 9.3 %collective-permute-start = (bf16[464,128]{1,0:T(8,128)(2,1)S(1)}, bf16[464,128]{1,0:T(8,128)(2,1)S(1)}, u32[]{:S(2)}, u32[]{:S(2)}) collective-permute-start(bf16[464,128]{1,0:T(8,128)(2,1)S(1)} %get-tuple-element.13), channel_id=1, source_target_pairs={{0,1},{1,2},{2,3},{3,0},{4,5},{5,6},{6,7},{7,4},{8,9},{9,10},{10,1... | collective-permute-start | bytes 356360 | tf_op jit(solution)/shard_map/ppermute | solution.py:468
  6.1 10.4 %collective-permute-start.1 = (bf16[464,128]{1,0:T(8,128)(2,1)S(1)}, bf16[464,128]{1,0:T(8,128)(2,1)S(1)}, u32[]{:S(2)}, u32[]{:S(2)}) collective-permute-start(bf16[464,128]{1,0:T(8,128)(2,1)S(1)} %get-tuple-element.14), channel_id=1, source_target_pairs={{0,2},{1,3},{2,0},{3,1},{4,6},{5,7},{6,4},{7,5},{8,10},{9,11},{10,... | collective-permute-start | bytes 356360 | tf_op jit(solution)/shard_map/ppermute | solution.py:468
  8.7 7.9 %collective-permute-start.2 = (bf16[464,128]{1,0:T(8,128)(2,1)S(1)}, bf16[464,128]{1,0:T(8,128)(2,1)S(1)}, u32[]{:S(2)}, u32[]{:S(2)}) collective-permute-start(bf16[464,128]{1,0:T(8,128)(2,1)S(1)} %get-tuple-element.15), channel_id=1, source_target_pairs={{0,3},{1,0},{2,1},{3,2},{4,7},{5,4},{6,5},{7,6},{8,11},{9,8},{10,9... | collective-permute-start | bytes 356360 | tf_op jit(solution)/shard_map/ppermute | solution.py:468
  36.2 16.7 %collective-permute-start.3 = (f32[64,128]{1,0:T(8,128)S(1)}, f32[64,128]{1,0:T(8,128)S(1)}, u32[]{:S(2)}, u32[]{:S(2)}) collective-permute-start(f32[64,128]{1,0:T(8,128)S(1)} %get-tuple-element.19), channel_id=1, source_target_pairs={{0,1},{1,2},{2,3},{3,0},{4,5},{5,6},{6,7},{7,4},{8,9},{9,10},{10,1... | collective-permute-start | bytes 98312 | tf_op jit(solution)/shard_map/ppermute | solution.py:468
  39.3 13.6 %collective-permute-start.4 = (f32[64,128]{1,0:T(8,128)S(1)}, f32[64,128]{1,0:T(8,128)S(1)}, u32[]{:S(2)}, u32[]{:S(2)}) collective-permute-start(f32[64,128]{1,0:T(8,128)S(1)} %get-tuple-element.20), channel_id=1, source_target_pairs={{0,2},{1,3},{2,0},{3,1},{4,6},{5,7},{6,4},{7,5},{8,10},{9,11},{10,... | collective-permute-start | bytes 98312 | tf_op jit(solution)/shard_map/ppermute | solution.py:468
  40.9 12.0 %collective-permute-start.5 = (f32[64,128]{1,0:T(8,128)S(1)}, f32[64,128]{1,0:T(8,128)S(1)}, u32[]{:S(2)}, u32[]{:S(2)}) collective-permute-start(f32[64,128]{1,0:T(8,128)S(1)} %get-tuple-element.21), channel_id=1, source_target_pairs={{0,3},{1,0},{2,1},{3,2},{4,7},{5,4},{6,5},{7,6},{8,11},{9,8},{10,9... | collective-permute-start | bytes 98312 | tf_op jit(solution)/shard_map/ppermute | solution.py:468

commit v6 on v5

--- a/solution.py
+++ b/solution.py
@@ -12,12 +12,12 @@
 
 ELONG = 0.75
 LANES = 128
-VMEM_LIMIT = 44 * 1024 * 1024
+VMEM_LIMIT = 32 * 1024 * 1024
 F32 = jnp.float32
 BF16 = jnp.bfloat16
 
 
-CHUNK = 1024
+CHUNK = 256
 
 
 def halves(pupil, field, fun):
@@ -109,22 +109,20 @@
     return jnp.concatenate(parts, axis=0)
 
 
-def pack_kernel(n, nb, me_ref, profile_hbm, weight_hbm, amp_hbm, phase_hbm, cot_hbm, *refs):
+def pack_early_kernel(n, nb, me_ref, profile_hbm, weight_hbm, amp_hbm, phase_hbm, *refs):
     out_refs = refs[:n]
-    profile_ref, weight_ref, amp_ref, phase_ref, cot_ref, sems = refs[n:]
+    profile_ref, weight_ref, amp_ref, phase_ref, sems = refs[n:]
     pairs = (
         (phase_hbm, phase_ref),
         (amp_hbm, amp_ref),
         (profile_hbm, profile_ref),
         (weight_hbm, weight_ref),
-        (cot_hbm, cot_ref),
     )
     copies = [pltpu.make_async_copy(src, dst, sems.at[i]) for i, (src, dst) in enumerate(pairs)]
     for copy in copies:
         copy.start()
     width = LANES // n
     qp = phase_ref.shape[0] // n
-    qc = cot_ref.shape[0] // n
     turn = lax.rem(n - me_ref[0], n) * width
     for copy in copies:
         copy.wait()
@@ -142,17 +140,7 @@
         for j, block in enumerate(swap_groups(parts, width)):
             out_refs[j][2 * qp + q : 2 * qp + q + 16, :] = block.astype(BF16)
 
-    def step(i, carry):
-        at = pl.multiple_of(i * 16, 16)
-        parts = [
-            pltpu.roll(cot_ref[pl.ds(a * qc + at, 16), :].astype(F32), turn, 1) for a in range(n)
-        ]
-        for j, block in enumerate(swap_groups(parts, width)):
-            out_refs[j][pl.ds(3 * qp + at, 16), :] = block.astype(BF16)
-        return carry
-
-    lax.fori_loop(0, qc // 16, step, 0, unroll=4)
-    base = 3 * qp + qc
+    base = 3 * qp
     rows = out_refs[0].shape[0] - base
     row = lax.broadcasted_iota(jnp.int32, (rows, LANES), 0)
     extra = jnp.zeros((rows, LANES), F32)
@@ -166,6 +154,27 @@
     for j in range(n):
         out_refs[j][base:, :] = extra.astype(BF16)
 
+
+def pack_late_kernel(n, me_ref, cot_hbm, *refs):
+    out_refs = refs[n - 1 : 2 * n - 1]
+    cot_ref, sem = refs[2 * n - 1 :]
+    copy = pltpu.make_async_copy(cot_hbm, cot_ref, sem)
+    copy.start()
+    width = LANES // n
+    qc = cot_ref.shape[0] // n
+    turn = lax.rem(n - me_ref[0], n) * width
+    copy.wait()
+
+    def step(i, carry):
+        at = pl.multiple_of(i * 16, 16)
+        parts = [
+            pltpu.roll(cot_ref[pl.ds(a * qc + at, 16), :].astype(F32), turn, 1) for a in range(n)
+        ]
+        for j, block in enumerate(swap_groups(parts, width)):
+            out_refs[j][pl.ds(at, 16), :] = block.astype(BF16)
+        return carry
+
+    lax.fori_loop(0, qc // 16, step, 0, unroll=4)
 
 def sincos(x):
     turns = jnp.round(x * (2.0 / math.pi))
@@ -185,23 +194,19 @@
     return sin_v, cos_v
 
 
-def spots_kernel(n, nb, pupil, field, me_ref, pos_hbm, fwd_hbm, bwd_hbm, *refs):
-    in_refs, grad_refs, aux_ref, stat_ref = refs[:n], refs[n : 2 * n], refs[2 * n], refs[2 * n + 1]
-    (
-        phase_s, amp_s, cot_s, e_s, x_s, p_s, y_s, g_s, pg_s, pos_ref, fwd_ref, bwd_ref, sems
-    ) = refs[2 * n + 2 :]
+def fields_kernel(n, nb, pupil, field, me_ref, pos_hbm, fwd_hbm, *refs):
+    in_refs, (e_s, p_s, aux_ref) = refs[:n], refs[n : n + 3]
+    phase_s, amp_s, x_s, pos_ref, fwd_ref, sems = refs[n + 3 :]
     copies = [
         pltpu.make_async_copy(pos_hbm, pos_ref, sems.at[0]),
         pltpu.make_async_copy(fwd_hbm, fwd_ref, sems.at[1]),
-        pltpu.make_async_copy(bwd_hbm, bwd_ref, sems.at[2]),
     ]
     for copy in copies:
         copy.start()
     width = LANES // n
     nbins = n * nb
     qp = pupil * pupil // (n * n)
-    qc = field * field // (n * n)
-    half, fhalf = pupil // 2, field // 2
+    half = pupil // 2
     wide = nb * LANES
     me = me_ref[0]
     group1 = lane_group((1, LANES), width)
@@ -225,31 +230,11 @@
                     at = pl.multiple_of(owner[j] * (n * qp) + line + part, 16)
                     dst[pl.ds(at, 16), :] = ways[turned[a]][a]
 
-    per = qc // field
-    for j in range(n):
-        low = owner[j] < n // 2
-        sign = jnp.where(low, 0, 1)
-
-        def place(i, carry):
-            for q in range(0, field, 16):
-                at = pl.multiple_of(3 * qp + i * field + q, 16)
-                raw = in_refs[j][pl.ds(at, 16), :].astype(F32)
-                raw = reverse_rows(raw) if q >= fhalf else raw
-                col = field - 16 - q if q >= fhalf else q
-                for a, cot in enumerate(spread_groups(raw, n, width)):
-                    k1 = (owner[j] * n + a) * per + i
-                    line = jnp.where(low, k1, field - 1 - k1)
-                    at = pl.multiple_of(line * fhalf + col, 16)
-                    cot_s[sign, int(q >= fhalf), pl.ds(at, 16), :] = cot
-            return carry
-
-        lax.fori_loop(0, per, place, 0)
-
     prof, wgt = [], []
     for t in range(nb):
         p_row, w_row = jnp.zeros((1, LANES), F32), jnp.zeros((1, LANES), F32)
         for j in range(n):
-            extra = in_refs[j][3 * qp + qc :, :].astype(F32)
+            extra = in_refs[j][3 * qp :, :].astype(F32)
             rows = [extra[6 * t + i : 6 * t + i + 1, :] for i in range(6)]
             p_row = jnp.where(group1 == owner[j], rows[0] + rows[1] + rows[2], p_row)
             w_row = jnp.where(group1 == owner[j], rows[3] + rows[4] + rows[5], w_row)
@@ -260,10 +245,10 @@
     while step >= 1:
         total = total + roll(total, step * width)
         step //= 2
-    coef = [2.0 / (pupil * pupil) * prof[t] * wgt[t] / total for t in range(nb)]
     aux = jnp.zeros(aux_ref.shape, F32)
     row = lax.broadcasted_iota(jnp.int32, aux_ref.shape, 0)
     for t in range(nb):
+        aux = jnp.where(row == t, 2.0 / (pupil * pupil) * prof[t] * wgt[t] / total, aux)
         aux = jnp.where(row == nb + t, prof[t], aux)
         aux = jnp.where(row == 2 * nb + t, wgt[t], aux)
     aux_ref[...] = jnp.where(row == 3 * nb, total, aux)
@@ -315,18 +300,53 @@
     lax.fori_loop(0, half, fields, 0)
 
     depth = half * half
+    copies[1].wait()
+    for c in range(4):
+        for k in range(2):
+            lanes = pl.ds(k * wide, wide)
+            p_s[c, k] = dot_three(fwd_ref[c], depth, x_s[c, 0, :, lanes], x_s[c, 1, :, lanes])
+
+
+def images_kernel(n, nb, pupil, field, me_ref, bwd_hbm, e_s, p_s, aux_in, *refs):
+    in_refs, grad_refs, stat_ref = refs[:n], refs[n : 2 * n], refs[2 * n]
+    cot_s, y_s, g_s, pg_s, bwd_ref, sem = refs[2 * n + 1 :]
+    copy = pltpu.make_async_copy(bwd_hbm, bwd_ref, sem)
+    copy.start()
+    width = LANES // n
+    qp = pupil * pupil // (n * n)
+    qc = field * field // (n * n)
+    half, fhalf = pupil // 2, field // 2
+    wide = nb * LANES
+    me = me_ref[0]
+    owner = [lax.rem(me + n - j, n) for j in range(n)]
+    coef = [aux_in[t : t + 1, :] for t in range(nb)]
+
+    per = qc // field
+    for j in range(n):
+        low = owner[j] < n // 2
+        sign = jnp.where(low, 0, 1)
+
+        def place(i, carry):
+            for q in range(0, field, 16):
+                at = pl.multiple_of(i * field + q, 16)
+                raw = in_refs[j][pl.ds(at, 16), :].astype(F32)
+                raw = reverse_rows(raw) if q >= fhalf else raw
+                col = field - 16 - q if q >= fhalf else q
+                for a, cot in enumerate(spread_groups(raw, n, width)):
+                    k1 = (owner[j] * n + a) * per + i
+                    line = jnp.where(low, k1, field - 1 - k1)
+                    at = pl.multiple_of(line * fhalf + col, 16)
+                    cot_s[sign, int(q >= fhalf), pl.ds(at, 16), :] = cot
+            return carry
+
+        lax.fori_loop(0, per, place, 0)
+
     rows_all = fhalf * fhalf
     chunk = min(CHUNK, rows_all)
-    copies[1].wait()
-    copies[2].wait()
+    copy.wait()
 
     def images(m, first):
         base = m * chunk
-        for c in range(4):
-            table = fwd_ref[c, pl.ds(pl.multiple_of(base, chunk), chunk), :]
-            for k in range(2):
-                lanes = pl.ds(k * wide, wide)
-                p_s[c, k] = dot_three(table, depth, x_s[c, 0, :, lanes], x_s[c, 1, :, lanes])
 
         def weigh(i, carry):
             at = pl.multiple_of(i * 16, 16)
@@ -334,8 +354,8 @@
             cot = [cot_s[a, b, pl.ds(there, 16), :] for a in range(2) for b in range(2)]
             for t in range(nb):
                 lanes = pl.ds(t * LANES, LANES)
-                re = [p_s[c, 0, pl.ds(at, 16), lanes] for c in range(4)]
-                im = [p_s[c, 1, pl.ds(at, 16), lanes] for c in range(4)]
+                re = [p_s[c, 0, pl.ds(there, 16), lanes] for c in range(4)]
+                im = [p_s[c, 1, pl.ds(there, 16), lanes] for c in range(4)]
                 s0, s1, s2, s3 = re[0] + im[1], re[0] - im[1], im[2] - re[3], im[2] + re[3]
                 y = [cot[0] * (s0 + s2), cot[1] * (s0 - s2), cot[2] * (s1 + s3), cot[3] * (s1 - s3)]
                 s0, s1, s2, s3 = im[0] - re[1], im[0] + re[1], re[2] + im[3], re[2] - im[3]
@@ -469,23 +489,32 @@
             for j in range(1, n)
         ]
 
-    blocks = pl.pallas_call(
-        functools.partial(pack_kernel, n, nb),
-        out_shape=[jax.ShapeDtypeStruct((3 * qp + qc + extra, LANES), BF16)] * n,
-        in_specs=[smem] + [hbm] * 5,
+    early = pl.pallas_call(
+        functools.partial(pack_early_kernel, n, nb),
+        out_shape=[jax.ShapeDtypeStruct((3 * qp + extra, LANES), BF16)] * n,
+        in_specs=[smem] + [hbm] * 4,
         out_specs=[vmem] * n,
         scratch_shapes=[
             pltpu.SMEM(profile.shape, F32),
             pltpu.SMEM(alt_weight.shape, F32),
             pltpu.VMEM(amplitude.shape, BF16),
             pltpu.VMEM(phase.shape, F32),
-            pltpu.VMEM(cotangent.shape, BF16),
-            pltpu.SemaphoreType.DMA((5,)),
+            pltpu.SemaphoreType.DMA((4,)),
         ],
         compiler_params=params,
-        name="pack",
-    )(me, *keep(profile, alt_weight, amplitude, phase, cotangent))
-    blocks = exchange(blocks)
+        name="pack_early",
+    )(me, *keep(profile, alt_weight, amplitude, phase))
+    early = exchange(early)
+    late = pl.pallas_call(
+        functools.partial(pack_late_kernel, n),
+        out_shape=[jax.ShapeDtypeStruct((qc, LANES), BF16)] * n,
+        in_specs=[smem, hbm] + [vmem] * (n - 1),
+        out_specs=[vmem] * n,
+        scratch_shapes=[pltpu.VMEM(cotangent.shape, BF16), pltpu.SemaphoreType.DMA],
+        compiler_params=params,
+        name="pack_late",
+    )(me, *keep(cotangent), *early[1:])
+    late = exchange(late)
 
     fwd, bwd = (jnp.asarray(x) for x in tables(pupil, field))
     depth = pupil * pupil // 4
@@ -493,30 +522,43 @@
     chunk = min(CHUNK, rows_all)
     wide = nb * LANES
     aux_rows = -(-(3 * nb + 1) // 8) * 8
-    *grads, aux, stat = pl.pallas_call(
-        functools.partial(spots_kernel, n, nb, pupil, field),
-        out_shape=[jax.ShapeDtypeStruct((qp, LANES), F32)] * n
-        + [jax.ShapeDtypeStruct((rows, LANES), F32) for rows in (aux_rows, n_sub * n)],
-        in_specs=[smem] + [hbm] * 3 + [vmem] * n,
-        out_specs=[vmem] * (n + 2),
+    e, p, aux = pl.pallas_call(
+        functools.partial(fields_kernel, n, nb, pupil, field),
+        out_shape=(
+            jax.ShapeDtypeStruct((nb, 2, pupil * pupil, LANES), F32),
+            jax.ShapeDtypeStruct((4, 2, rows_all, wide), F32),
+            jax.ShapeDtypeStruct((aux_rows, LANES), F32),
+        ),
+        in_specs=[smem] + [hbm] * 2 + [vmem] * n,
+        out_specs=(vmem, vmem, vmem),
         scratch_shapes=[
             pltpu.VMEM((pupil * pupil, LANES), F32),
             pltpu.VMEM((pupil * pupil, LANES), F32),
+            pltpu.VMEM((4, 2, depth, 2 * wide), BF16),
+            pltpu.VMEM(position.shape, F32),
+            pltpu.VMEM(fwd.shape, BF16),
+            pltpu.SemaphoreType.DMA((2,)),
+        ],
+        compiler_params=params,
+        name="fields",
+    )(me, *keep(position, fwd), *early)
+    *grads, stat = pl.pallas_call(
+        functools.partial(images_kernel, n, nb, pupil, field),
+        out_shape=[jax.ShapeDtypeStruct((qp, LANES), F32)] * n
+        + [jax.ShapeDtypeStruct((n_sub * n, LANES), F32)],
+        in_specs=[smem, hbm] + [vmem] * (3 + n),
+        out_specs=[vmem] * (n + 1),
+        scratch_shapes=[
             pltpu.VMEM((2, 2, rows_all, LANES), F32),
-            pltpu.VMEM((nb, 2, pupil * pupil, LANES), F32),
-            pltpu.VMEM((4, 2, depth, 2 * wide), BF16),
-            pltpu.VMEM((4, 2, chunk, wide), F32),
             pltpu.VMEM((4, 2, chunk, 2 * wide), BF16),
             pltpu.VMEM((4, 2, depth, wide), F32),
             pltpu.VMEM((pupil * pupil, LANES), F32),
-            pltpu.VMEM(position.shape, F32),
-            pltpu.VMEM(fwd.shape, BF16),
             pltpu.VMEM(bwd.shape, BF16),
-            pltpu.SemaphoreType.DMA((3,)),
+            pltpu.SemaphoreType.DMA,
         ],
         compiler_params=params,
-        name="spots",
-    )(me, *keep(position, fwd, bwd), *blocks)
+        name="images",
+    )(me, *keep(bwd), e, p, aux, *late)
     stat = lax.all_to_all(stat, ("sub", "alt"), 0, 0, tiled=True)
     grads = exchange(grads)
     return pl.pallas_call(

time: 54 us -> 54.7 us (1.013)
  waiting for transfers between devices: 6.51 us -> 2.93 us
  starting transfers between devices: 12.5 us -> 15.9 us
  Pallas kernels: 23 us -> 24.6 us
  blocking collectives: 11.2 us -> 10.4 us
    ppermute x6 -> x9, waiting for transfers between devices: 6.51 us -> 2.93 us  [exchange(): lax.ppermute(blocks[j], 'alt', [(i, (i + j) % n) for i in range(n)])]
    ppermute x6 -> x9, starting transfers between devices: 12.5 us -> 15.9 us  [exchange(): lax.ppermute(blocks[j], 'alt', [(i, (i + j) % n) for i in range(n)])]
    pallas_call x2 -> x4, Pallas kernels: 22.1 us -> 23.7 us  [the longest x1 13 us: local(): pl.pallas_call(functools.partial(images_kernel, n, nb, pupil, field), out...]
    all_to_all x1, blocking collectives: 11.2 us -> 10.4 us  [local(): stat = lax.all_to_all(stat, ('sub', 'alt'), 0, 0, tiled=True)]
  transfers between devices with their start and end apart: 6 -> 9, of which waited for: 2 -> 3; matrix products, arithmetic and copies ran while one was open for 0% -> 0% of each run, Pallas kernels for 0% -> 14%
where the time goes in v6:
time: 54.7 us; the launch traced here: 54.6 us
  Pallas kernels  24.6 us (45%)
  starting transfers between devices  15.9 us (29%)
  blocking collectives  10.4 us (19%)
  waiting for transfers between devices  2.93 us (5%)
  between operations  0.7 us (1%)
    ppermute x9, starting transfers between devices, exchange(): lax.ppermute(blocks[j], 'alt', [(i, (i + j) % n) for i in range(n)])  15.9 us
    pallas_call x1, Pallas kernels, local(): pl.pallas_call(functools.partial(images_kernel, n, nb, pupil, field), out...  13 us
    all_to_all x1, blocking collectives, local(): stat = lax.all_to_all(stat, ('sub', 'alt'), 0, 0, tiled=True)  10.4 us
    pallas_call x1, Pallas kernels, local(): pl.pallas_call(functools.partial(fields_kernel, n, nb, pupil, field), out...  7.49 us
    ppermute x9, waiting for transfers between devices, exchange(): lax.ppermute(blocks[j], 'alt', [(i, (i + j) % n) for i in range(n)])  2.93 us
    pallas_call x1, Pallas kernels, local(): pl.pallas_call(functools.partial(pack_late_kernel, n), out_shape=[jax.Sha...  1.89 us
    pallas_call x1, Pallas kernels, local(): pl.pallas_call(functools.partial(pack_early_kernel, n, nb), out_shape=[ja...  1.29 us
  transfers between devices with their start and end apart: 9, of which 3 were waited for; matrix products, arithmetic and copies ran while one was open for 0% of the time, Pallas kernels for 14%

profile of v6, /device:TPU:0, one launch (start us, length us, event | category | flops | bytes accessed | tf_op | source)
XLA Modules:
  0.0 54.6 jit_solution(2807750544791281637)
XLA Ops:
  0.6 1.3 %pack_early.1 = (bf16[208,128]{1,0:T(8,128)(2,1)S(1)}, bf16[208,128]{1,0:T(8,128)(2,1)S(1)}, bf16[208,128]{1,0:T(8,128)(2,1)S(1)}, bf16[208,128]{1,0:T(8,128)(2,1)S(1)}) custom-call(s32[1]{0:T(128)} %bitcast.me_ref, f32[2]{0:T(128)} %profile_hbm.1, f32[2]{0:T(128)} %weight_hbm.1, bf16[256,128]{1,0:T(8,128)(2,1)} %amp_hbm.1, f32[256,128]{1,0:T(8,128)} %phase_hbm.1), custom_call_target="tpu_custom_call" | custom-call | tf_op jit(solution)/shard_map/pack_early/pallas_call | solution.py:492
  1.9 3.1 %collective-permute-start = (bf16[208,128]{1,0:T(8,128)(2,1)S(1)}, bf16[208,128]{1,0:T(8,128)(2,1)S(1)}, u32[]{:S(2)}, u32[]{:S(2)}) collective-permute-start(bf16[208,128]{1,0:T(8,128)(2,1)S(1)} %get-tuple-element.19), channel_id=1, source_target_pairs={{0,1},{1,2},{2,3},{3,0},{4,5},{5,6},{6,7},{7,4},{8,9},{9,10},{10,1... | collective-permute-start | bytes 159752 | tf_op jit(solution)/shard_map/ppermute | solution.py:488
  5.0 2.6 %collective-permute-start.1 = (bf16[208,128]{1,0:T(8,128)(2,1)S(1)}, bf16[208,128]{1,0:T(8,128)(2,1)S(1)}, u32[]{:S(2)}, u32[]{:S(2)}) collective-permute-start(bf16[208,128]{1,0:T(8,128)(2,1)S(1)} %get-tuple-element.20), channel_id=1, source_target_pairs={{0,2},{1,3},{2,0},{3,1},{4,6},{5,7},{6,4},{7,5},{8,10},{9,11},{10,... | collective-permute-start | bytes 159752 | tf_op jit(solution)/shard_map/ppermute | solution.py:488
  7.6 1.3 %collective-permute-start.2 = (bf16[208,128]{1,0:T(8,128)(2,1)S(1)}, bf16[208,128]{1,0:T(8,128)(2,1)S(1)}, u32[]{:S(2)}, u32[]{:S(2)}) collective-permute-start(bf16[208,128]{1,0:T(8,128)(2,1)S(1)} %get-tuple-element.21), channel_id=1, source_target_pairs={{0,3},{1,0},{2,1},{3,2},{4,7},{5,4},{6,5},{7,6},{8,11},{9,8},{10,9... | collective-permute-start | bytes 159752 | tf_op jit(solution)/shard_map/ppermute | solution.py:488
  8.9 0.3 collective-permute-done.refs_1_.refs_0_
  9.3 2.1 %collective-permute-done.1.refs_2_.refs_1_ = bf16[208,128]{1,0:T(8,128)(2,1)S(1)} collective-permute-done((bf16[208,128]{1,0:T(8,128)(2,1)S(1)}, bf16[208,128]{1,0:T(8,128)(2,1)S(1)}, u32[]{:S(2)}, u32[]{:S(2)}) %collective-permute-start.1) | collective-permute-done | bytes 53280 | tf_op jit(solution)/shard_map/ppermute | solution.py:488
  11.4 0.4 collective-permute-done.2.refs_3_.refs_2_
  11.9 1.9 %pack_late.1 = (bf16[256,128]{1,0:T(8,128)(2,1)S(1)}, bf16[256,128]{1,0:T(8,128)(2,1)S(1)}, bf16[256,128]{1,0:T(8,128)(2,1)S(1)}, bf16[256,128]{1,0:T(8,128)(2,1)S(1)}) custom-call(s32[1]{0:T(128)} %bitcast.me_ref, bf16[1024,128]{1,0:T(8,128)(2,1)} %cot_hbm.1, bf16[208,128]{1,0:T(8,128)(2,1)S(1)} %collective-permute-done.refs_1_.refs_0_, ...), custom_call_target="tpu_custom_call" | custom-call | tf_op jit(solution)/shard_map/pack_late/pallas_call | solution.py:508
  13.8 1.0 %collective-permute-start.3 = (bf16[256,128]{1,0:T(8,128)(2,1)S(1)}, bf16[256,128]{1,0:T(8,128)(2,1)S(1)}, u32[]{:S(2)}, u32[]{:S(2)}) collective-permute-start(bf16[256,128]{1,0:T(8,128)(2,1)S(1)} %get-tuple-element.26), channel_id=1, source_target_pairs={{0,1},{1,2},{2,3},{3,0},{4,5},{5,6},{6,7},{7,4},{8,9},{9,10},{10,1... | collective-permute-start | bytes 196616 | tf_op jit(solution)/shard_map/ppermute | solution.py:488
  14.8 2.6 %collective-permute-start.4 = (bf16[256,128]{1,0:T(8,128)(2,1)S(1)}, bf16[256,128]{1,0:T(8,128)(2,1)S(1)}, u32[]{:S(2)}, u32[]{:S(2)}) collective-permute-start(bf16[256,128]{1,0:T(8,128)(2,1)S(1)} %get-tuple-element.27), channel_id=1, source_target_pairs={{0,2},{1,3},{2,0},{3,1},{4,6},{5,7},{6,4},{7,5},{8,10},{9,11},{10,... | collective-permute-start | bytes 196616 | tf_op jit(solution)/shard_map/ppermute | solution.py:488
  17.4 0.3 collective-permute-start.5
  17.7 7.5 %fields.1 = (f32[2,2,1024,128]{3,2,1,0:T(8,128)S(1)}, f32[4,2,1024,256]{3,2,1,0:T(8,128)S(1)}, f32[8,128]{1,0:T(8,128)S(1)}) custom-call(s32[1]{0:T(128)} %bitcast.me_ref, f32[2,128]{1,0:T(2,128)} %pos_hbm.1, bf16[4,1024,512]{2,1,0:T(8,128)(2,1)} %constant.8.clone.fwd_hbm, bf16[208,128]{1,0:T(8,128)(2,1)S(1)} %get-tuple-element.18.refs_0_, ...), custom_call_target="tpu_custom_call" | custom-call | tf_op jit(solution)/shard_map/fields/pallas_call | solution.py:525
  25.2 0.0 collective-permute-done.3.refs_1_
  25.2 0.0 collective-permute-done.4.refs_2_
  25.3 0.0 collective-permute-done.5.refs_3_
  25.3 13.0 %images.1 = (f32[64,128]{1,0:T(8,128)S(1)}, f32[64,128]{1,0:T(8,128)S(1)}, f32[64,128]{1,0:T(8,128)S(1)}, f32[64,128]{1,0:T(8,128)S(1)}, f32[32,128]{1,0:T(8,128)S(1)}) custom-call(s32[1]{0:T(128)} %bitcast.me_ref, bf16[4,4,256,512]{3,2,1,0:T(8,128)(2,1)} %constant.9.clone.bwd_hbm, f32[2,2,1024,128]{3,2,1,0:T(8,128)S(1)} %get-tuple-element.23.e_s, ...), custom_call_target="tpu_custom_call" | custom-call | tf_op jit(solution)/shard_map/images/pallas_call | solution.py:545
  38.3 1.7 %collective-permute-start.6 = (f32[64,128]{1,0:T(8,128)S(1)}, f32[64,128]{1,0:T(8,128)S(1)}, u32[]{:S(2)}, u32[]{:S(2)}) collective-permute-start(f32[64,128]{1,0:T(8,128)S(1)} %get-tuple-element.31), channel_id=1, source_target_pairs={{0,1},{1,2},{2,3},{3,0},{4,5},{5,6},{6,7},{7,4},{8,9},{9,10},{10,1... | collective-permute-start | bytes 98312 | tf_op jit(solution)/shard_map/ppermute | solution.py:488
  40.0 0.3 collective-permute-start.7
  40.3 2.8 %collective-permute-start.8 = (f32[64,128]{1,0:T(8,128)S(1)}, f32[64,128]{1,0:T(8,128)S(1)}, u32[]{:S(2)}, u32[]{:S(2)}) collective-permute-start(f32[64,128]{1,0:T(8,128)S(1)} %get-tuple-element.33), channel_id=1, source_target_pairs={{0,3},{1,0},{2,1},{3,2},{4,7},{5,4},{6,5},{7,6},{8,11},{9,8},{10,9... | collective-permute-start | bytes 98312 | tf_op jit(solution)/shard_map/ppermute | solution.py:488
  43.2 10.4 %all_to_all.11 = f32[32,1,128]{2,1,0:T(1,128)S(1)} all-to-all(f32[32,1,128]{2,1,0:T(1,128)S(1)} %bitcast.6), channel_id=1, replica_groups=mesh['sub'=8,'alt'=4] {'sub','alt'}, dimensions={0} | all-to-all | bytes 32768 | tf_op jit(solution)/shard_map/all_to_all | solution.py:562
  53.6 0.0 collective-permute-done.6.refs_1_
  53.6 0.0 collective-permute-done.7.refs_2_
  53.6 0.0 collective-permute-done.8.refs_3_
  53.6 0.9 %finish.1 = (f32[256,128]{1,0:T(8,128)}, f32[2]{0:T(128)}) custom-call(s32[1]{0:T(128)} %bitcast.me_ref, f32[8,128]{1,0:T(8,128)S(1)} %get-tuple-element.22.aux_in.aux_ref, f32[32,128]{1,0:T(8,128)S(1)} %bitcast.5, f32[64,128]{1,0:T(8,128)S(1)} %get-tuple-element.30.refs_0_, f32[64,128]{1,0:T(8,128)S(1)} %collective-permute-done.6.refs_1_, ...), custom_call_target="tpu_custom_call" | custom-call | tf_op jit(solution)/shard_map/finish/pallas_call | solution.py:564
Async XLA Ops:
  1.9 7.4 %collective-permute-start = (bf16[208,128]{1,0:T(8,128)(2,1)S(1)}, bf16[208,128]{1,0:T(8,128)(2,1)S(1)}, u32[]{:S(2)}, u32[]{:S(2)}) collective-permute-start(bf16[208,128]{1,0:T(8,128)(2,1)S(1)} %get-tuple-element.19), channel_id=1, source_target_pairs={{0,1},{1,2},{2,3},{3,0},{4,5},{5,6},{6,7},{7,4},{8,9},{9,10},{10,1... | collective-permute-start | bytes 159752 | tf_op jit(solution)/shard_map/ppermute | solution.py:488
  5.0 6.4 %collective-permute-start.1 = (bf16[208,128]{1,0:T(8,128)(2,1)S(1)}, bf16[208,128]{1,0:T(8,128)(2,1)S(1)}, u32[]{:S(2)}, u32[]{:S(2)}) collective-permute-start(bf16[208,128]{1,0:T(8,128)(2,1)S(1)} %get-tuple-element.20), channel_id=1, source_target_pairs={{0,2},{1,3},{2,0},{3,1},{4,6},{5,7},{6,4},{7,5},{8,10},{9,11},{10,... | collective-permute-start | bytes 159752 | tf_op jit(solution)/shard_map/ppermute | solution.py:488
  7.6 4.3 %collective-permute-start.2 = (bf16[208,128]{1,0:T(8,128)(2,1)S(1)}, bf16[208,128]{1,0:T(8,128)(2,1)S(1)}, u32[]{:S(2)}, u32[]{:S(2)}) collective-permute-start(bf16[208,128]{1,0:T(8,128)(2,1)S(1)} %get-tuple-element.21), channel_id=1, source_target_pairs={{0,3},{1,0},{2,1},{3,2},{4,7},{5,4},{6,5},{7,6},{8,11},{9,8},{10,9... | collective-permute-start | bytes 159752 | tf_op jit(solution)/shard_map/ppermute | solution.py:488
  13.8 11.5 %collective-permute-start.3 = (bf16[256,128]{1,0:T(8,128)(2,1)S(1)}, bf16[256,128]{1,0:T(8,128)(2,1)S(1)}, u32[]{:S(2)}, u32[]{:S(2)}) collective-permute-start(bf16[256,128]{1,0:T(8,128)(2,1)S(1)} %get-tuple-element.26), channel_id=1, source_target_pairs={{0,1},{1,2},{2,3},{3,0},{4,5},{5,6},{6,7},{7,4},{8,9},{9,10},{10,1... | collective-permute-start | bytes 196616 | tf_op jit(solution)/shard_map/ppermute | solution.py:488
  14.8 10.4 %collective-permute-start.4 = (bf16[256,128]{1,0:T(8,128)(2,1)S(1)}, bf16[256,128]{1,0:T(8,128)(2,1)S(1)}, u32[]{:S(2)}, u32[]{:S(2)}) collective-permute-start(bf16[256,128]{1,0:T(8,128)(2,1)S(1)} %get-tuple-element.27), channel_id=1, source_target_pairs={{0,2},{1,3},{2,0},{3,1},{4,6},{5,7},{6,4},{7,5},{8,10},{9,11},{10,... | collective-permute-start | bytes 196616 | tf_op jit(solution)/shard_map/ppermute | solution.py:488
  17.4 7.9 %collective-permute-start.5 = (bf16[256,128]{1,0:T(8,128)(2,1)S(1)}, bf16[256,128]{1,0:T(8,128)(2,1)S(1)}, u32[]{:S(2)}, u32[]{:S(2)}) collective-permute-start(bf16[256,128]{1,0:T(8,128)(2,1)S(1)} %get-tuple-element.28), channel_id=1, source_target_pairs={{0,3},{1,0},{2,1},{3,2},{4,7},{5,4},{6,5},{7,6},{8,11},{9,8},{10,9... | collective-permute-start | bytes 196616 | tf_op jit(solution)/shard_map/ppermute | solution.py:488
  38.3 15.3 %collective-permute-start.6 = (f32[64,128]{1,0:T(8,128)S(1)}, f32[64,128]{1,0:T(8,128)S(1)}, u32[]{:S(2)}, u32[]{:S(2)}) collective-permute-start(f32[64,128]{1,0:T(8,128)S(1)} %get-tuple-element.31), channel_id=1, source_target_pairs={{0,1},{1,2},{2,3},{3,0},{4,5},{5,6},{6,7},{7,4},{8,9},{9,10},{10,1... | collective-permute-start | bytes 98312 | tf_op jit(solution)/shard_map/ppermute | solution.py:488
  40.0 13.6 %collective-permute-start.7 = (f32[64,128]{1,0:T(8,128)S(1)}, f32[64,128]{1,0:T(8,128)S(1)}, u32[]{:S(2)}, u32[]{:S(2)}) collective-permute-start(f32[64,128]{1,0:T(8,128)S(1)} %get-tuple-element.32), channel_id=1, source_target_pairs={{0,2},{1,3},{2,0},{3,1},{4,6},{5,7},{6,4},{7,5},{8,10},{9,11},{10,... | collective-permute-start | bytes 98312 | tf_op jit(solution)/shard_map/ppermute | solution.py:488
  40.3 13.3 %collective-permute-start.8 = (f32[64,128]{1,0:T(8,128)S(1)}, f32[64,128]{1,0:T(8,128)S(1)}, u32[]{:S(2)}, u32[]{:S(2)}) collective-permute-start(f32[64,128]{1,0:T(8,128)S(1)} %get-tuple-element.33), channel_id=1, source_target_pairs={{0,3},{1,0},{2,1},{3,2},{4,7},{5,4},{6,5},{7,6},{8,11},{9,8},{10,9... | collective-permute-start | bytes 98312 | tf_op jit(solution)/shard_map/ppermute | solution.py:488

commit v7 on v5

--- a/solution.py
+++ b/solution.py
@@ -12,12 +12,12 @@
 
 ELONG = 0.75
 LANES = 128
-VMEM_LIMIT = 44 * 1024 * 1024
+VMEM_LIMIT = 52 * 1024 * 1024
 F32 = jnp.float32
 BF16 = jnp.bfloat16
 
 
-CHUNK = 1024
+CHUNK = 512
 
 
 def halves(pupil, field, fun):
@@ -39,10 +39,7 @@
         for a in range(2):
             t = np.kron(halves(pupil, field, fun[a]), halves(pupil, field, fun[b]))
             fwd.append(hi_lo(t))
-            rows = min(CHUNK, t.shape[0])
-            bwd.append(
-                np.stack([hi_lo(t[m : m + rows].T) for m in range(0, t.shape[0], rows)])
-            )
+            bwd.append(hi_lo(t.T))
     return np.stack(fwd), np.stack(bwd)
 
 
@@ -185,11 +182,21 @@
     return sin_v, cos_v
 
 
+def multiple(x, m):
+    return x if isinstance(x, int) else pl.multiple_of(x, m)
+
+
+def interleave(dots, pieces):
+    for i, one in enumerate(dots):
+        one()
+        for piece in pieces[i * len(pieces) // len(dots) : (i + 1) * len(pieces) // len(dots)]:
+            piece()
+
+
 def spots_kernel(n, nb, pupil, field, me_ref, pos_hbm, fwd_hbm, bwd_hbm, *refs):
     in_refs, grad_refs, aux_ref, stat_ref = refs[:n], refs[n : 2 * n], refs[2 * n], refs[2 * n + 1]
-    (
-        phase_s, amp_s, cot_s, e_s, x_s, p_s, y_s, g_s, pg_s, pos_ref, fwd_ref, bwd_ref, sems
-    ) = refs[2 * n + 2 :]
+    phase_s, amp_s, cot_s, pg_s, part_s, pos_ref, fwd_ref, bwd_ref, sems, *per_tile = refs[2 * n + 2 :]
+    e_s, x_s, p_s, y_s, g_s = (per_tile[k * nb : (k + 1) * nb] for k in range(5))
     copies = [
         pltpu.make_async_copy(pos_hbm, pos_ref, sems.at[0]),
         pltpu.make_async_copy(fwd_hbm, fwd_ref, sems.at[1]),
@@ -202,7 +209,6 @@
     qp = pupil * pupil // (n * n)
     qc = field * field // (n * n)
     half, fhalf = pupil // 2, field // 2
-    wide = nb * LANES
     me = me_ref[0]
     group1 = lane_group((1, LANES), width)
     owner = [lax.rem(me + n - j, n) for j in range(n)]
@@ -226,24 +232,19 @@
                     dst[pl.ds(at, 16), :] = ways[turned[a]][a]
 
     per = qc // field
-    for j in range(n):
-        low = owner[j] < n // 2
-        sign = jnp.where(low, 0, 1)
-
-        def place(i, carry):
-            for q in range(0, field, 16):
-                at = pl.multiple_of(3 * qp + i * field + q, 16)
-                raw = in_refs[j][pl.ds(at, 16), :].astype(F32)
-                raw = reverse_rows(raw) if q >= fhalf else raw
-                col = field - 16 - q if q >= fhalf else q
-                for a, cot in enumerate(spread_groups(raw, n, width)):
-                    k1 = (owner[j] * n + a) * per + i
-                    line = jnp.where(low, k1, field - 1 - k1)
-                    at = pl.multiple_of(line * fhalf + col, 16)
-                    cot_s[sign, int(q >= fhalf), pl.ds(at, 16), :] = cot
-            return carry
-
-        lax.fori_loop(0, per, place, 0)
+    low = [owner[j] < n // 2 for j in range(n)]
+    sign = [jnp.where(low[j], 0, 1) for j in range(n)]
+
+    def place(j, i, q):
+        at = 3 * qp + i * field + q
+        raw = in_refs[j][at : at + 16, :].astype(F32)
+        raw = reverse_rows(raw) if q >= fhalf else raw
+        col = field - 16 - q if q >= fhalf else q
+        for a, cot in enumerate(spread_groups(raw, n, width)):
+            k1 = (owner[j] * n + a) * per + i
+            line = jnp.where(low[j], k1, field - 1 - k1)
+            at = pl.multiple_of(line * fhalf + col, 16)
+            cot_s[sign[j], int(q >= fhalf), pl.ds(at, 16), :] = cot
 
     prof, wgt = [], []
     for t in range(nb):
@@ -284,119 +285,124 @@
     u_rows = jnp.where(row < half, row, pupil + half - 1 - row).astype(F32) - (pupil - 1) / 2.0
     lean = [u_rows * tilt_x[t] for t in range(nb)]
 
-    def fields(i, carry):
-        at16 = pl.multiple_of(i * half, half)
-        for t in range(nb):
-            found = []
-            for r in (i, pupil - 1 - i):
-                at = pl.multiple_of(r * pupil, pupil)
-                v = r.astype(F32) - (pupil - 1) / 2.0
-                am = amp_s[pl.ds(at, pupil), :]
-                sin_v, cos_v = sincos(phase_s[pl.ds(at, pupil), :] + (lean[t] + v * tilt_y[t]))
-                one = (am * cos_v, am * sin_v)
-                for k in range(2):
-                    e_s[t, k, pl.ds(at, pupil), :] = one[k]
-                found.append(one)
+    def fields(t, i):
+        at16 = multiple(i * half, half)
+        found = []
+        for r in (i, pupil - 1 - i):
+            at = multiple(r * pupil, pupil)
+            v = (float(r) if isinstance(r, int) else r.astype(F32)) - (pupil - 1) / 2.0
+            am = amp_s[pl.ds(at, pupil), :]
+            sin_v, cos_v = sincos(phase_s[pl.ds(at, pupil), :] + (lean[t] + v * tilt_y[t]))
+            one = (am * cos_v, am * sin_v)
             for k in range(2):
-                even, odd = found[1][k] + found[0][k], found[1][k] - found[0][k]
-                classes = (
-                    even[half:] + even[:half],
-                    odd[half:] + odd[:half],
-                    even[half:] - even[:half],
-                    odd[half:] - odd[:half],
-                )
-                lanes = pl.ds(k * wide + t * LANES, LANES)
-                for c, x in enumerate(classes):
-                    hi, lo = split(x)
-                    x_s[c, 0, pl.ds(at16, half), lanes] = hi
-                    x_s[c, 1, pl.ds(at16, half), lanes] = lo
-        return carry
-
-    lax.fori_loop(0, half, fields, 0)
+                e_s[t][k, pl.ds(at, pupil), :] = one[k]
+            found.append(one)
+        for k in range(2):
+            even, odd = found[1][k] + found[0][k], found[1][k] - found[0][k]
+            classes = (
+                even[half:] + even[:half],
+                odd[half:] + odd[:half],
+                even[half:] - even[:half],
+                odd[half:] - odd[:half],
+            )
+            lanes = pl.ds(k * LANES, LANES)
+            for c, x in enumerate(classes):
+                hi, lo = split(x)
+                x_s[t][c, 0, pl.ds(at16, half), lanes] = hi
+                x_s[t][c, 1, pl.ds(at16, half), lanes] = lo
 
     depth = half * half
     rows_all = fhalf * fhalf
     chunk = min(CHUNK, rows_all)
-    copies[1].wait()
-    copies[2].wait()
-
-    def images(m, first):
-        base = m * chunk
+
+    def forward(t, c, m):
+        rows = pl.ds(m * chunk, chunk)
+        p_s[t][c, rows, :] = dot_three(fwd_ref[c, rows, :], depth, x_s[t][c, 0], x_s[t][c, 1])
+
+    def weigh(t, i):
+        rows = pl.ds(i * 16, 16)
+        cot = [cot_s[a, b, rows, :] for a in range(2) for b in range(2)]
+        re = [p_s[t][c, rows, pl.ds(0, LANES)] for c in range(4)]
+        im = [p_s[t][c, rows, pl.ds(LANES, LANES)] for c in range(4)]
+        s0, s1, s2, s3 = re[0] + im[1], re[0] - im[1], im[2] - re[3], im[2] + re[3]
+        y = [cot[0] * (s0 + s2), cot[1] * (s0 - s2), cot[2] * (s1 + s3), cot[3] * (s1 - s3)]
+        s0, s1, s2, s3 = im[0] - re[1], im[0] + re[1], re[2] + im[3], re[2] - im[3]
+        z = [cot[0] * (s0 - s2), cot[1] * (s0 + s2), cot[2] * (s1 - s3), cot[3] * (s1 + s3)]
+        yp, ym, yd, ye = y[0] + y[1], y[2] + y[3], y[0] - y[1], y[2] - y[3]
+        zp, zm, zd, ze = z[0] + z[1], z[2] + z[3], z[0] - z[1], z[2] - z[3]
+        back = (
+            (yp + ym, zp + zm),
+            (zm - zp, yp - ym),
+            (-ze - zd, yd + ye),
+            (ye - yd, ze - zd),
+        )
         for c in range(4):
-            table = fwd_ref[c, pl.ds(pl.multiple_of(base, chunk), chunk), :]
             for k in range(2):
-                lanes = pl.ds(k * wide, wide)
-                p_s[c, k] = dot_three(table, depth, x_s[c, 0, :, lanes], x_s[c, 1, :, lanes])
-
-        def weigh(i, carry):
-            at = pl.multiple_of(i * 16, 16)
-            there = pl.multiple_of(base + i * 16, 16)
-            cot = [cot_s[a, b, pl.ds(there, 16), :] for a in range(2) for b in range(2)]
-            for t in range(nb):
-                lanes = pl.ds(t * LANES, LANES)
-                re = [p_s[c, 0, pl.ds(at, 16), lanes] for c in range(4)]
-                im = [p_s[c, 1, pl.ds(at, 16), lanes] for c in range(4)]
-                s0, s1, s2, s3 = re[0] + im[1], re[0] - im[1], im[2] - re[3], im[2] + re[3]
-                y = [cot[0] * (s0 + s2), cot[1] * (s0 - s2), cot[2] * (s1 + s3), cot[3] * (s1 - s3)]
-                s0, s1, s2, s3 = im[0] - re[1], im[0] + re[1], re[2] + im[3], re[2] - im[3]
-                z = [cot[0] * (s0 - s2), cot[1] * (s0 + s2), cot[2] * (s1 - s3), cot[3] * (s1 + s3)]
-                yp, ym, yd, ye = y[0] + y[1], y[2] + y[3], y[0] - y[1], y[2] - y[3]
-                zp, zm, zd, ze = z[0] + z[1], z[2] + z[3], z[0] - z[1], z[2] - z[3]
-                back = (
-                    (yp + ym, zp + zm),
-                    (zm - zp, yp - ym),
-                    (-ze - zd, yd + ye),
-                    (ye - yd, ze - zd),
-                )
-                for c in range(4):
-                    for k in range(2):
-                        hi, lo = split(back[c][k])
-                        lanes = pl.ds(k * wide + t * LANES, LANES)
-                        y_s[c, 0, pl.ds(at, 16), lanes] = hi
-                        y_s[c, 1, pl.ds(at, 16), lanes] = lo
-            return carry
-
-        lax.fori_loop(0, chunk // 16, weigh, 0, unroll=2)
-        for c in range(4):
-            table = bwd_ref[c, m]
-            for k in range(2):
-                lanes = pl.ds(k * wide, wide)
-                out = dot_three(table, chunk, y_s[c, 0, :, lanes], y_s[c, 1, :, lanes])
-                g_s[c, k] = out if first else g_s[c, k] + out
-
-    images(0, True)
-    if rows_all > chunk:
-        lax.fori_loop(1, rows_all // chunk, lambda m, carry: images(m, False) or carry, 0)
-
-    def products(i, stats):
-        stats = list(stats)
-        at16 = pl.multiple_of(i * half, half)
-        grads = [jnp.zeros((pupil, LANES), F32) for _ in range(2)]
-        spots = [pl.multiple_of(r * pupil, pupil) for r in (i, pupil - 1 - i)]
-        for t in range(nb):
-            found = []
-            for k in range(2):
-                g = [g_s[c, k, pl.ds(at16, half), pl.ds(t * LANES, LANES)] for c in range(4)]
-                even = jnp.concatenate([g[0] - g[2], g[0] + g[2]], axis=0)
-                odd = jnp.concatenate([g[1] - g[3], g[1] + g[3]], axis=0)
-                found.append((even - odd, even + odd))
-            for which in range(2):
-                e_re = e_s[t, 0, pl.ds(spots[which], pupil), :]
-                e_im = e_s[t, 1, pl.ds(spots[which], pupil), :]
-                g_re, g_im = found[0][which], found[1][which]
-                stats[t] = stats[t] + (e_re * g_re + e_im * g_im)
-                grads[which] = grads[which] + coef[t] * (e_re * g_im - e_im * g_re)
-        for which in range(2):
-            grad = grads[which]
+                hi, lo = split(back[c][k])
+                lanes = pl.ds(k * LANES, LANES)
+                y_s[t][c, 0, rows, lanes] = hi
+                y_s[t][c, 1, rows, lanes] = lo
+
+    def backward(t, c):
+        g_s[t][c] = dot_three(bwd_ref[c], rows_all, y_s[t][c, 0], y_s[t][c, 1])
+
+    def products(t, i, stat):
+        at16 = multiple(i * half, half)
+        found = []
+        for k in range(2):
+            g = [g_s[t][c, pl.ds(at16, half), pl.ds(k * LANES, LANES)] for c in range(4)]
+            even = jnp.concatenate([g[0] - g[2], g[0] + g[2]], axis=0)
+            odd = jnp.concatenate([g[1] - g[3], g[1] + g[3]], axis=0)
+            found.append((even - odd, even + odd))
+        for which, r in enumerate((i, pupil - 1 - i)):
+            rows = pl.ds(multiple(r * pupil, pupil), pupil)
+            e_re, e_im = e_s[t][0, rows, :], e_s[t][1, rows, :]
+            g_re, g_im = found[0][which], found[1][which]
+            stat = stat + (e_re * g_re + e_im * g_im)
+            grad = coef[t] * (e_re * g_im - e_im * g_re)
+            if t:
+                grad = grad + part_s[rows, :]
+            if t < nb - 1:
+                part_s[rows, :] = grad
+                continue
             step = n // 2
             while step >= 1:
                 grad = grad + roll(grad, step * width)
                 step //= 2
-            grad = jnp.concatenate([grad[:half], reverse_rows(grad[half:])], axis=0)
-            pg_s[pl.ds(spots[which], pupil), :] = grad
-        return tuple(stats)
-
-    stats = lax.fori_loop(0, half, products, tuple(jnp.zeros((pupil, LANES), F32) for _ in range(nb)))
+            pg_s[rows, :] = jnp.concatenate([grad[:half], reverse_rows(grad[half:])], axis=0)
+        return stat
+
+    stats = [jnp.zeros((pupil, LANES), F32) for _ in range(nb)]
+
+    def early_products(t, i):
+        stats[t] = products(t, i, stats[t])
+
+    work = functools.partial
+    places = [
+        work(place, j, i, q) for j in range(n) for i in range(per) for q in range(0, field, 16)
+    ]
+    lax.fori_loop(0, half, lambda i, carry: fields(0, i) or carry, 0)
+    copies[1].wait()
+    for t in range(nb):
+        pieces = places if t == 0 else []
+        if t < nb - 1:
+            pieces = [work(fields, t + 1, i) for i in range(half)] + pieces
+        elif nb > 1:
+            pieces = [work(weigh, 0, i) for i in range(rows_all // 16)] + pieces
+        interleave(
+            [work(forward, t, c, m) for c in range(4) for m in range(rows_all // chunk)], pieces
+        )
+    if nb == 1:
+        for i in range(rows_all // 16):
+            weigh(0, i)
+    copies[2].wait()
+    for t in range(nb):
+        if t < nb - 1:
+            pieces = [work(weigh, t + 1, i) for i in range(rows_all // 16)]
+        else:
+            pieces = [work(early_products, b, i) for b in range(nb - 1) for i in range(half)]
+        interleave([work(backward, t, c) for c in range(4)], pieces)
+    stats[-1] = lax.fori_loop(0, half, lambda i, stat: products(nb - 1, i, stat), stats[-1])
 
     lane = lax.broadcasted_iota(jnp.int32, (1, LANES), 1)
     sums = jnp.zeros((1, LANES), F32)
@@ -490,8 +496,6 @@
     fwd, bwd = (jnp.asarray(x) for x in tables(pupil, field))
     depth = pupil * pupil // 4
     rows_all = field * field // 4
-    chunk = min(CHUNK, rows_all)
-    wide = nb * LANES
     aux_rows = -(-(3 * nb + 1) // 8) * 8
     *grads, aux, stat = pl.pallas_call(
         functools.partial(spots_kernel, n, nb, pupil, field),
@@ -503,17 +507,18 @@
             pltpu.VMEM((pupil * pupil, LANES), F32),
             pltpu.VMEM((pupil * pupil, LANES), F32),
             pltpu.VMEM((2, 2, rows_all, LANES), F32),
-            pltpu.VMEM((nb, 2, pupil * pupil, LANES), F32),
-            pltpu.VMEM((4, 2, depth, 2 * wide), BF16),
-            pltpu.VMEM((4, 2, chunk, wide), F32),
-            pltpu.VMEM((4, 2, chunk, 2 * wide), BF16),
-            pltpu.VMEM((4, 2, depth, wide), F32),
+            pltpu.VMEM((pupil * pupil, LANES), F32),
             pltpu.VMEM((pupil * pupil, LANES), F32),
             pltpu.VMEM(position.shape, F32),
             pltpu.VMEM(fwd.shape, BF16),
             pltpu.VMEM(bwd.shape, BF16),
             pltpu.SemaphoreType.DMA((3,)),
-        ],
+        ]
+        + [pltpu.VMEM((2, pupil * pupil, LANES), F32)] * nb
+        + [pltpu.VMEM((4, 2, depth, 2 * LANES), BF16)] * nb
+        + [pltpu.VMEM((4, rows_all, 2 * LANES), F32)] * nb
+        + [pltpu.VMEM((4, 2, rows_all, 2 * LANES), BF16)] * nb
+        + [pltpu.VMEM((4, depth, 2 * LANES), F32)] * nb,
         compiler_params=params,
         name="spots",
     )(me, *keep(position, fwd, bwd), *blocks)

time: 54 us -> 50.7 us (0.939)
  Pallas kernels: 23 us -> 19.7 us
    pallas_call x1, Pallas kernels: 19.7 us -> 16.3 us  [local(): pl.pallas_call(functools.partial(spots_kernel, n, nb, pupil, field), out_...]
where the time goes in v7:
time: 50.7 us; the launch traced here: 50.5 us
  Pallas kernels  19.7 us (39%)
  starting transfers between devices  12.5 us (25%)
  blocking collectives  11.2 us (22%)
  waiting for transfers between devices  6.51 us (13%)
  between operations  0.66 us (1%)
    pallas_call x1, Pallas kernels, local(): pl.pallas_call(functools.partial(spots_kernel, n, nb, pupil, field), out_...  16.3 us
    ppermute x6, starting transfers between devices, exchange(): lax.ppermute(blocks[j], 'alt', [(i, (i + j) % n) for i in range(n)])  12.5 us
    all_to_all x1, blocking collectives, local(): stat = lax.all_to_all(stat, ('sub', 'alt'), 0, 0, tiled=True)  11.2 us
    ppermute x6, waiting for transfers between devices, exchange(): lax.ppermute(blocks[j], 'alt', [(i, (i + j) % n) for i in range(n)])  6.51 us
    pallas_call x1, Pallas kernels, local(): pl.pallas_call(functools.partial(pack_kernel, n, nb), out_shape=[jax.Shap...  2.37 us
  transfers between devices with their start and end apart: 6, of which 2 were waited for; matrix products, arithmetic and copies ran while one was open for 0% of the time, Pallas kernels for 0%

profile of v7, /device:TPU:0, one launch (start us, length us, event | category | flops | bytes accessed | tf_op | source)
XLA Modules:
  0.0 50.5 jit_solution(2506831812652814856)
XLA Ops:
  0.6 2.4 %pack.1 = (bf16[464,128]{1,0:T(8,128)(2,1)S(1)}, bf16[464,128]{1,0:T(8,128)(2,1)S(1)}, bf16[464,128]{1,0:T(8,128)(2,1)S(1)}, bf16[464,128]{1,0:T(8,128)(2,1)S(1)}) custom-call(s32[1]{0:T(128)} %bitcast.me_ref, f32[2]{0:T(128)} %profile_hbm.1, f32[2]{0:T(128)} %weight_hbm.1, bf16[256,128]{1,0:T(8,128)(2,1)} %amp_hbm.1, f32[256,128]{1,0:T(8,128)} %phase_hbm.1, ...), custom_call_target="tpu_custom_call" | custom-call | tf_op jit(solution)/shard_map/pack/pallas_call | solution.py:478
  3.0 3.1 %collective-permute-start = (bf16[464,128]{1,0:T(8,128)(2,1)S(1)}, bf16[464,128]{1,0:T(8,128)(2,1)S(1)}, u32[]{:S(2)}, u32[]{:S(2)}) collective-permute-start(bf16[464,128]{1,0:T(8,128)(2,1)S(1)} %get-tuple-element.13), channel_id=1, source_target_pairs={{0,1},{1,2},{2,3},{3,0},{4,5},{5,6},{6,7},{7,4},{8,9},{9,10},{10,1... | collective-permute-start | bytes 356360 | tf_op jit(solution)/shard_map/ppermute | solution.py:474
  6.1 2.6 %collective-permute-start.1 = (bf16[464,128]{1,0:T(8,128)(2,1)S(1)}, bf16[464,128]{1,0:T(8,128)(2,1)S(1)}, u32[]{:S(2)}, u32[]{:S(2)}) collective-permute-start(bf16[464,128]{1,0:T(8,128)(2,1)S(1)} %get-tuple-element.14), channel_id=1, source_target_pairs={{0,2},{1,3},{2,0},{3,1},{4,6},{5,7},{6,4},{7,5},{8,10},{9,11},{10,... | collective-permute-start | bytes 356360 | tf_op jit(solution)/shard_map/ppermute | solution.py:474
  8.7 1.3 %collective-permute-start.2 = (bf16[464,128]{1,0:T(8,128)(2,1)S(1)}, bf16[464,128]{1,0:T(8,128)(2,1)S(1)}, u32[]{:S(2)}, u32[]{:S(2)}) collective-permute-start(bf16[464,128]{1,0:T(8,128)(2,1)S(1)} %get-tuple-element.15), channel_id=1, source_target_pairs={{0,3},{1,0},{2,1},{3,2},{4,7},{5,4},{6,5},{7,6},{8,11},{9,8},{10,9... | collective-permute-start | bytes 356360 | tf_op jit(solution)/shard_map/ppermute | solution.py:474
  10.0 2.2 %collective-permute-done.refs_1_ = bf16[464,128]{1,0:T(8,128)(2,1)S(1)} collective-permute-done((bf16[464,128]{1,0:T(8,128)(2,1)S(1)}, bf16[464,128]{1,0:T(8,128)(2,1)S(1)}, u32[]{:S(2)}, u32[]{:S(2)}) %collective-permute-start) | collective-permute-done | bytes 118816 | tf_op jit(solution)/shard_map/ppermute | solution.py:474
  12.3 4.3 %collective-permute-done.1.refs_2_ = bf16[464,128]{1,0:T(8,128)(2,1)S(1)} collective-permute-done((bf16[464,128]{1,0:T(8,128)(2,1)S(1)}, bf16[464,128]{1,0:T(8,128)(2,1)S(1)}, u32[]{:S(2)}, u32[]{:S(2)}) %collective-permute-start.1) | collective-permute-done | bytes 118816 | tf_op jit(solution)/shard_map/ppermute | solution.py:474
  16.5 0.0 collective-permute-done.2.refs_3_
  16.5 16.3 %spots.1 = (f32[64,128]{1,0:T(8,128)S(1)}, f32[64,128]{1,0:T(8,128)S(1)}, f32[64,128]{1,0:T(8,128)S(1)}, f32[64,128]{1,0:T(8,128)S(1)}, f32[8,128]{1,0:T(8,128)S(1)}, /*index=5*/f32[32,128]{1,0:T(8,128)S(1)}) custom-call(s32[1]{0:T(128)} %bitcast.me_ref, f32[2,128]{1,0:T(2,128)} %pos_hbm.1, bf16[4,1024,512]{2,1,0:T(8,128)(2,1)} %constant.8.clone.fwd_hbm, ...), custom_call_target="tpu_custom_call" | custom-call | tf_op jit(solution)/shard_map/spots/pallas_call | solution.py:500
  32.9 3.1 %collective-permute-start.3 = (f32[64,128]{1,0:T(8,128)S(1)}, f32[64,128]{1,0:T(8,128)S(1)}, u32[]{:S(2)}, u32[]{:S(2)}) collective-permute-start(f32[64,128]{1,0:T(8,128)S(1)} %get-tuple-element.19), channel_id=1, source_target_pairs={{0,1},{1,2},{2,3},{3,0},{4,5},{5,6},{6,7},{7,4},{8,9},{9,10},{10,1... | collective-permute-start | bytes 98312 | tf_op jit(solution)/shard_map/ppermute | solution.py:474
  36.0 1.6 %collective-permute-start.4 = (f32[64,128]{1,0:T(8,128)S(1)}, f32[64,128]{1,0:T(8,128)S(1)}, u32[]{:S(2)}, u32[]{:S(2)}) collective-permute-start(f32[64,128]{1,0:T(8,128)S(1)} %get-tuple-element.20), channel_id=1, source_target_pairs={{0,2},{1,3},{2,0},{3,1},{4,6},{5,7},{6,4},{7,5},{8,10},{9,11},{10,... | collective-permute-start | bytes 98312 | tf_op jit(solution)/shard_map/ppermute | solution.py:474
  37.6 0.8 %collective-permute-start.5 = (f32[64,128]{1,0:T(8,128)S(1)}, f32[64,128]{1,0:T(8,128)S(1)}, u32[]{:S(2)}, u32[]{:S(2)}) collective-permute-start(f32[64,128]{1,0:T(8,128)S(1)} %get-tuple-element.21), channel_id=1, source_target_pairs={{0,3},{1,0},{2,1},{3,2},{4,7},{5,4},{6,5},{7,6},{8,11},{9,8},{10,9... | collective-permute-start | bytes 98312 | tf_op jit(solution)/shard_map/ppermute | solution.py:474
  38.4 11.2 %all_to_all.11 = f32[32,1,128]{2,1,0:T(1,128)S(1)} all-to-all(f32[32,1,128]{2,1,0:T(1,128)S(1)} %bitcast.6), channel_id=1, replica_groups=mesh['sub'=8,'alt'=4] {'sub','alt'}, dimensions={0} | all-to-all | bytes 32768 | tf_op jit(solution)/shard_map/all_to_all | solution.py:525
  49.6 0.0 collective-permute-done.3.refs_1_
  49.6 0.0 collective-permute-done.4.refs_2_
  49.6 0.0 collective-permute-done.5.refs_3_
  49.6 0.9 %finish.1 = (f32[256,128]{1,0:T(8,128)}, f32[2]{0:T(128)}) custom-call(s32[1]{0:T(128)} %bitcast.me_ref, f32[8,128]{1,0:T(8,128)S(1)} %get-tuple-element.16.aux_ref, f32[32,128]{1,0:T(8,128)S(1)} %bitcast.5, f32[64,128]{1,0:T(8,128)S(1)} %get-tuple-element.18.refs_0_, f32[64,128]{1,0:T(8,128)S(1)} %collective-permute-done.3.refs_1_, ...), custom_call_target="tpu_custom_call" | custom-call | tf_op jit(solution)/shard_map/finish/pallas_call | solution.py:527
Async XLA Ops:
  3.0 9.3 %collective-permute-start = (bf16[464,128]{1,0:T(8,128)(2,1)S(1)}, bf16[464,128]{1,0:T(8,128)(2,1)S(1)}, u32[]{:S(2)}, u32[]{:S(2)}) collective-permute-start(bf16[464,128]{1,0:T(8,128)(2,1)S(1)} %get-tuple-element.13), channel_id=1, source_target_pairs={{0,1},{1,2},{2,3},{3,0},{4,5},{5,6},{6,7},{7,4},{8,9},{9,10},{10,1... | collective-permute-start | bytes 356360 | tf_op jit(solution)/shard_map/ppermute | solution.py:474
  6.1 10.4 %collective-permute-start.1 = (bf16[464,128]{1,0:T(8,128)(2,1)S(1)}, bf16[464,128]{1,0:T(8,128)(2,1)S(1)}, u32[]{:S(2)}, u32[]{:S(2)}) collective-permute-start(bf16[464,128]{1,0:T(8,128)(2,1)S(1)} %get-tuple-element.14), channel_id=1, source_target_pairs={{0,2},{1,3},{2,0},{3,1},{4,6},{5,7},{6,4},{7,5},{8,10},{9,11},{10,... | collective-permute-start | bytes 356360 | tf_op jit(solution)/shard_map/ppermute | solution.py:474
  8.7 7.9 %collective-permute-start.2 = (bf16[464,128]{1,0:T(8,128)(2,1)S(1)}, bf16[464,128]{1,0:T(8,128)(2,1)S(1)}, u32[]{:S(2)}, u32[]{:S(2)}) collective-permute-start(bf16[464,128]{1,0:T(8,128)(2,1)S(1)} %get-tuple-element.15), channel_id=1, source_target_pairs={{0,3},{1,0},{2,1},{3,2},{4,7},{5,4},{6,5},{7,6},{8,11},{9,8},{10,9... | collective-permute-start | bytes 356360 | tf_op jit(solution)/shard_map/ppermute | solution.py:474
  32.9 16.7 %collective-permute-start.3 = (f32[64,128]{1,0:T(8,128)S(1)}, f32[64,128]{1,0:T(8,128)S(1)}, u32[]{:S(2)}, u32[]{:S(2)}) collective-permute-start(f32[64,128]{1,0:T(8,128)S(1)} %get-tuple-element.19), channel_id=1, source_target_pairs={{0,1},{1,2},{2,3},{3,0},{4,5},{5,6},{6,7},{7,4},{8,9},{9,10},{10,1... | collective-permute-start | bytes 98312 | tf_op jit(solution)/shard_map/ppermute | solution.py:474
  36.0 13.6 %collective-permute-start.4 = (f32[64,128]{1,0:T(8,128)S(1)}, f32[64,128]{1,0:T(8,128)S(1)}, u32[]{:S(2)}, u32[]{:S(2)}) collective-permute-start(f32[64,128]{1,0:T(8,128)S(1)} %get-tuple-element.20), channel_id=1, source_target_pairs={{0,2},{1,3},{2,0},{3,1},{4,6},{5,7},{6,4},{7,5},{8,10},{9,11},{10,... | collective-permute-start | bytes 98312 | tf_op jit(solution)/shard_map/ppermute | solution.py:474
  37.6 12.0 %collective-permute-start.5 = (f32[64,128]{1,0:T(8,128)S(1)}, f32[64,128]{1,0:T(8,128)S(1)}, u32[]{:S(2)}, u32[]{:S(2)}) collective-permute-start(f32[64,128]{1,0:T(8,128)S(1)} %get-tuple-element.21), channel_id=1, source_target_pairs={{0,3},{1,0},{2,1},{3,2},{4,7},{5,4},{6,5},{7,6},{8,11},{9,8},{10,9... | collective-permute-start | bytes 98312 | tf_op jit(solution)/shard_map/ppermute | solution.py:474

commit v8 on v7

--- a/solution.py
+++ b/solution.py
@@ -39,7 +39,7 @@
         for a in range(2):
             t = np.kron(halves(pupil, field, fun[a]), halves(pupil, field, fun[b]))
             fwd.append(hi_lo(t))
-            bwd.append(hi_lo(t.T))
+            bwd.append(np.concatenate(np.split(hi_lo(t.T), 2, axis=1), axis=0))
     return np.stack(fwd), np.stack(bwd)
 
 
@@ -344,7 +344,9 @@
                 y_s[t][c, 1, rows, lanes] = lo
 
     def backward(t, c):
-        g_s[t][c] = dot_three(bwd_ref[c], rows_all, y_s[t][c, 0], y_s[t][c, 1])
+        high = jnp.dot(bwd_ref[c], y_s[t][c, 0], preferred_element_type=F32)
+        low = jnp.dot(bwd_ref[c, :depth, :], y_s[t][c, 1], preferred_element_type=F32)
+        g_s[t][c] = high[:depth] + (high[depth:] + low)
 
     def products(t, i, stat):
         at16 = multiple(i * half, half)
@@ -425,15 +427,19 @@
             ref[q : q + 8, :] = out
 
 
-def final_kernel(n, nb, nsub_all, me_ref, aux_ref, stat_ref, *refs):
+def gradient_kernel(n, me_ref, *refs):
     width = LANES // n
-    out_ref, prof_ref = refs[n:]
+    out_ref = refs[n]
     qp = out_ref.shape[0] // n
     turn = me_ref[0] * width
     for q in range(0, qp, 8):
         parts = [refs[(n - i) % n][q : q + 8, :] for i in range(n)]
         for a, block in enumerate(swap_groups(parts, width)):
             out_ref[a * qp + q : a * qp + q + 8, :] = pltpu.roll(block, turn, 1)
+
+
+def profile_kernel(n, nb, nsub_all, me_ref, aux_ref, stat_ref, prof_ref):
+    width = LANES // n
     lane = lax.broadcasted_iota(jnp.int32, (1, LANES), 1)
     stat = jnp.sum(stat_ref[...], axis=0, keepdims=True)
     aux = aux_ref[...]
@@ -524,17 +530,23 @@
     )(me, *keep(position, fwd, bwd), *blocks)
     stat = lax.all_to_all(stat, ("sub", "alt"), 0, 0, tiled=True)
     grads = exchange(grads)
-    return pl.pallas_call(
-        functools.partial(final_kernel, n, nb, nsub_all),
-        out_shape=(
-            jax.ShapeDtypeStruct(phase.shape, F32),
-            jax.ShapeDtypeStruct(profile.shape, F32),
-        ),
-        in_specs=[smem, vmem, vmem] + [vmem] * n,
-        out_specs=(vmem, smem),
+    phase_grad = pl.pallas_call(
+        functools.partial(gradient_kernel, n),
+        out_shape=jax.ShapeDtypeStruct(phase.shape, F32),
+        in_specs=[smem] + [vmem] * n,
+        out_specs=vmem,
         compiler_params=params,
-        name="finish",
-    )(me, aux, stat, *grads)
+        name="gradient",
+    )(me, *grads)
+    profile_grad = pl.pallas_call(
+        functools.partial(profile_kernel, n, nb, nsub_all),
+        out_shape=jax.ShapeDtypeStruct(profile.shape, F32),
+        in_specs=[smem, vmem, vmem],
+        out_specs=smem,
+        compiler_params=params,
+        name="profile",
+    )(me, aux, stat)
+    return phase_grad, profile_grad
 
 
 def solution(mesh):

time: 50.7 us -> 51.2 us (level)
    pallas_call x1 -> x2, Pallas kernels: 0.93 us -> 1.58 us  [the longest x1 0.9 us: local(): pl.pallas_call(functools.partial(gradient_kernel, n), out_shape=jax.Shape...]
  transfers between devices with their start and end apart: 6 -> 6, of which waited for: 2 -> 2; matrix products, arithmetic and copies ran while one was open for 0% -> 0% of each run, Pallas kernels for 0% -> 1%
where the time goes in v8:
time: 51.2 us; the launch traced here: 51 us
  Pallas kernels  20.1 us (39%)
  starting transfers between devices  12.5 us (24%)
  blocking collectives  11.2 us (22%)
  waiting for transfers between devices  6.51 us (13%)
  between operations  0.69 us (1%)
    pallas_call x1, Pallas kernels, local(): pl.pallas_call(functools.partial(spots_kernel, n, nb, pupil, field), out_...  16.2 us
    ppermute x6, starting transfers between devices, exchange(): lax.ppermute(blocks[j], 'alt', [(i, (i + j) % n) for i in range(n)])  12.5 us
    all_to_all x1, blocking collectives, local(): stat = lax.all_to_all(stat, ('sub', 'alt'), 0, 0, tiled=True)  11.2 us
    ppermute x6, waiting for transfers between devices, exchange(): lax.ppermute(blocks[j], 'alt', [(i, (i + j) % n) for i in range(n)])  6.51 us
    pallas_call x1, Pallas kernels, local(): pl.pallas_call(functools.partial(pack_kernel, n, nb), out_shape=[jax.Shap...  2.37 us
  transfers between devices with their start and end apart: 6, of which 2 were waited for; matrix products, arithmetic and copies ran while one was open for 0% of the time, Pallas kernels for 1%

profile of v8, /device:TPU:0, one launch (start us, length us, event | category | flops | bytes accessed | tf_op | source)
XLA Modules:
  0.0 51.0 jit_solution(5405110520177913033)
XLA Ops:
  0.6 2.4 %pack.1 = (bf16[464,128]{1,0:T(8,128)(2,1)S(1)}, bf16[464,128]{1,0:T(8,128)(2,1)S(1)}, bf16[464,128]{1,0:T(8,128)(2,1)S(1)}, bf16[464,128]{1,0:T(8,128)(2,1)S(1)}) custom-call(s32[1]{0:T(128)} %bitcast.me_ref, f32[2]{0:T(128)} %profile_hbm.1, f32[2]{0:T(128)} %weight_hbm.1, bf16[256,128]{1,0:T(8,128)(2,1)} %amp_hbm.1, f32[256,128]{1,0:T(8,128)} %phase_hbm.1, ...), custom_call_target="tpu_custom_call" | custom-call | tf_op jit(solution)/shard_map/pack/pallas_call | solution.py:484
  3.0 3.1 %collective-permute-start = (bf16[464,128]{1,0:T(8,128)(2,1)S(1)}, bf16[464,128]{1,0:T(8,128)(2,1)S(1)}, u32[]{:S(2)}, u32[]{:S(2)}) collective-permute-start(bf16[464,128]{1,0:T(8,128)(2,1)S(1)} %get-tuple-element.13), channel_id=1, source_target_pairs={{0,1},{1,2},{2,3},{3,0},{4,5},{5,6},{6,7},{7,4},{8,9},{9,10},{10,1... | collective-permute-start | bytes 356360 | tf_op jit(solution)/shard_map/ppermute | solution.py:480
  6.1 2.6 %collective-permute-start.1 = (bf16[464,128]{1,0:T(8,128)(2,1)S(1)}, bf16[464,128]{1,0:T(8,128)(2,1)S(1)}, u32[]{:S(2)}, u32[]{:S(2)}) collective-permute-start(bf16[464,128]{1,0:T(8,128)(2,1)S(1)} %get-tuple-element.14), channel_id=1, source_target_pairs={{0,2},{1,3},{2,0},{3,1},{4,6},{5,7},{6,4},{7,5},{8,10},{9,11},{10,... | collective-permute-start | bytes 356360 | tf_op jit(solution)/shard_map/ppermute | solution.py:480
  8.7 1.3 %collective-permute-start.2 = (bf16[464,128]{1,0:T(8,128)(2,1)S(1)}, bf16[464,128]{1,0:T(8,128)(2,1)S(1)}, u32[]{:S(2)}, u32[]{:S(2)}) collective-permute-start(bf16[464,128]{1,0:T(8,128)(2,1)S(1)} %get-tuple-element.15), channel_id=1, source_target_pairs={{0,3},{1,0},{2,1},{3,2},{4,7},{5,4},{6,5},{7,6},{8,11},{9,8},{10,9... | collective-permute-start | bytes 356360 | tf_op jit(solution)/shard_map/ppermute | solution.py:480
  10.0 2.2 %collective-permute-done.refs_1_ = bf16[464,128]{1,0:T(8,128)(2,1)S(1)} collective-permute-done((bf16[464,128]{1,0:T(8,128)(2,1)S(1)}, bf16[464,128]{1,0:T(8,128)(2,1)S(1)}, u32[]{:S(2)}, u32[]{:S(2)}) %collective-permute-start) | collective-permute-done | bytes 118816 | tf_op jit(solution)/shard_map/ppermute | solution.py:480
  12.3 4.3 %collective-permute-done.1.refs_2_ = bf16[464,128]{1,0:T(8,128)(2,1)S(1)} collective-permute-done((bf16[464,128]{1,0:T(8,128)(2,1)S(1)}, bf16[464,128]{1,0:T(8,128)(2,1)S(1)}, u32[]{:S(2)}, u32[]{:S(2)}) %collective-permute-start.1) | collective-permute-done | bytes 118816 | tf_op jit(solution)/shard_map/ppermute | solution.py:480
  16.5 0.0 collective-permute-done.2.refs_3_
  16.5 16.2 %spots.1 = (f32[64,128]{1,0:T(8,128)S(1)}, f32[64,128]{1,0:T(8,128)S(1)}, f32[64,128]{1,0:T(8,128)S(1)}, f32[64,128]{1,0:T(8,128)S(1)}, f32[8,128]{1,0:T(8,128)S(1)}, /*index=5*/f32[32,128]{1,0:T(8,128)S(1)}) custom-call(s32[1]{0:T(128)} %bitcast.me_ref, f32[2,128]{1,0:T(2,128)} %pos_hbm.1, bf16[4,1024,512]{2,1,0:T(8,128)(2,1)} %constant.8.clone.fwd_hbm, ...), custom_call_target="tpu_custom_call" | custom-call | tf_op jit(solution)/shard_map/spots/pallas_call | solution.py:506
  32.7 3.1 %collective-permute-start.3 = (f32[64,128]{1,0:T(8,128)S(1)}, f32[64,128]{1,0:T(8,128)S(1)}, u32[]{:S(2)}, u32[]{:S(2)}) collective-permute-start(f32[64,128]{1,0:T(8,128)S(1)} %get-tuple-element.17), channel_id=1, source_target_pairs={{0,1},{1,2},{2,3},{3,0},{4,5},{5,6},{6,7},{7,4},{8,9},{9,10},{10,1... | collective-permute-start | bytes 98312 | tf_op jit(solution)/shard_map/ppermute | solution.py:480
  35.8 1.6 %collective-permute-start.4 = (f32[64,128]{1,0:T(8,128)S(1)}, f32[64,128]{1,0:T(8,128)S(1)}, u32[]{:S(2)}, u32[]{:S(2)}) collective-permute-start(f32[64,128]{1,0:T(8,128)S(1)} %get-tuple-element.18), channel_id=1, source_target_pairs={{0,2},{1,3},{2,0},{3,1},{4,6},{5,7},{6,4},{7,5},{8,10},{9,11},{10,... | collective-permute-start | bytes 98312 | tf_op jit(solution)/shard_map/ppermute | solution.py:480
  37.4 0.8 %collective-permute-start.5 = (f32[64,128]{1,0:T(8,128)S(1)}, f32[64,128]{1,0:T(8,128)S(1)}, u32[]{:S(2)}, u32[]{:S(2)}) collective-permute-start(f32[64,128]{1,0:T(8,128)S(1)} %get-tuple-element.19), channel_id=1, source_target_pairs={{0,3},{1,0},{2,1},{3,2},{4,7},{5,4},{6,5},{7,6},{8,11},{9,8},{10,9... | collective-permute-start | bytes 98312 | tf_op jit(solution)/shard_map/ppermute | solution.py:480
  38.2 11.2 %all_to_all.11 = f32[32,1,128]{2,1,0:T(1,128)S(1)} all-to-all(f32[32,1,128]{2,1,0:T(1,128)S(1)} %bitcast.6), channel_id=1, replica_groups=mesh['sub'=8,'alt'=4] {'sub','alt'}, dimensions={0} | all-to-all | bytes 32768 | tf_op jit(solution)/shard_map/all_to_all | solution.py:531
  49.4 0.7 %profile.1 = f32[2]{0:T(128)} custom-call(s32[1]{0:T(128)} %bitcast.me_ref, f32[8,128]{1,0:T(8,128)S(1)} %get-tuple-element.20.aux_ref, f32[32,128]{1,0:T(8,128)S(1)} %bitcast.5), custom_call_target="tpu_custom_call" | custom-call | tf_op jit(solution)/shard_map/profile/pallas_call | solution.py:541
  50.1 0.0 collective-permute-done.3.refs_1_
  50.1 0.0 collective-permute-done.4.refs_2_
  50.1 0.0 collective-permute-done.5.refs_3_
  50.1 0.9 %gradient.1 = f32[256,128]{1,0:T(8,128)} custom-call(s32[1]{0:T(128)} %bitcast.me_ref, f32[64,128]{1,0:T(8,128)S(1)} %get-tuple-element.16.refs_0_, f32[64,128]{1,0:T(8,128)S(1)} %collective-permute-done.3.refs_1_, f32[64,128]{1,0:T(8,128)S(1)} %collective-permute-done.4.refs_2_, f32[64,128]{1,0:T(8,128)S(1)} %collective-permute-done.5.refs_3_), custom_call_target="tpu_custom_call" | custom-call | tf_op jit(solution)/shard_map/gradient/pallas_call | solution.py:533
Async XLA Ops:
  3.0 9.3 %collective-permute-start = (bf16[464,128]{1,0:T(8,128)(2,1)S(1)}, bf16[464,128]{1,0:T(8,128)(2,1)S(1)}, u32[]{:S(2)}, u32[]{:S(2)}) collective-permute-start(bf16[464,128]{1,0:T(8,128)(2,1)S(1)} %get-tuple-element.13), channel_id=1, source_target_pairs={{0,1},{1,2},{2,3},{3,0},{4,5},{5,6},{6,7},{7,4},{8,9},{9,10},{10,1... | collective-permute-start | bytes 356360 | tf_op jit(solution)/shard_map/ppermute | solution.py:480
  6.1 10.4 %collective-permute-start.1 = (bf16[464,128]{1,0:T(8,128)(2,1)S(1)}, bf16[464,128]{1,0:T(8,128)(2,1)S(1)}, u32[]{:S(2)}, u32[]{:S(2)}) collective-permute-start(bf16[464,128]{1,0:T(8,128)(2,1)S(1)} %get-tuple-element.14), channel_id=1, source_target_pairs={{0,2},{1,3},{2,0},{3,1},{4,6},{5,7},{6,4},{7,5},{8,10},{9,11},{10,... | collective-permute-start | bytes 356360 | tf_op jit(solution)/shard_map/ppermute | solution.py:480
  8.7 7.9 %collective-permute-start.2 = (bf16[464,128]{1,0:T(8,128)(2,1)S(1)}, bf16[464,128]{1,0:T(8,128)(2,1)S(1)}, u32[]{:S(2)}, u32[]{:S(2)}) collective-permute-start(bf16[464,128]{1,0:T(8,128)(2,1)S(1)} %get-tuple-element.15), channel_id=1, source_target_pairs={{0,3},{1,0},{2,1},{3,2},{4,7},{5,4},{6,5},{7,6},{8,11},{9,8},{10,9... | collective-permute-start | bytes 356360 | tf_op jit(solution)/shard_map/ppermute | solution.py:480
  32.7 17.4 %collective-permute-start.3 = (f32[64,128]{1,0:T(8,128)S(1)}, f32[64,128]{1,0:T(8,128)S(1)}, u32[]{:S(2)}, u32[]{:S(2)}) collective-permute-start(f32[64,128]{1,0:T(8,128)S(1)} %get-tuple-element.17), channel_id=1, source_target_pairs={{0,1},{1,2},{2,3},{3,0},{4,5},{5,6},{6,7},{7,4},{8,9},{9,10},{10,1... | collective-permute-start | bytes 98312 | tf_op jit(solution)/shard_map/ppermute | solution.py:480
  35.8 14.3 %collective-permute-start.4 = (f32[64,128]{1,0:T(8,128)S(1)}, f32[64,128]{1,0:T(8,128)S(1)}, u32[]{:S(2)}, u32[]{:S(2)}) collective-permute-start(f32[64,128]{1,0:T(8,128)S(1)} %get-tuple-element.18), channel_id=1, source_target_pairs={{0,2},{1,3},{2,0},{3,1},{4,6},{5,7},{6,4},{7,5},{8,10},{9,11},{10,... | collective-permute-start | bytes 98312 | tf_op jit(solution)/shard_map/ppermute | solution.py:480
  37.4 12.7 %collective-permute-start.5 = (f32[64,128]{1,0:T(8,128)S(1)}, f32[64,128]{1,0:T(8,128)S(1)}, u32[]{:S(2)}, u32[]{:S(2)}) collective-permute-start(f32[64,128]{1,0:T(8,128)S(1)} %get-tuple-element.19), channel_id=1, source_target_pairs={{0,3},{1,0},{2,1},{3,2},{4,7},{5,4},{6,5},{7,6},{8,11},{9,8},{10,9... | collective-permute-start | bytes 98312 | tf_op jit(solution)/shard_map/ppermute | solution.py:480

commit v9 on v7

--- a/solution.py
+++ b/solution.py
@@ -17,7 +17,7 @@
 BF16 = jnp.bfloat16
 
 
-CHUNK = 512
+CHUNK = 1024
 
 
 def halves(pupil, field, fun):
@@ -39,7 +39,7 @@
         for a in range(2):
             t = np.kron(halves(pupil, field, fun[a]), halves(pupil, field, fun[b]))
             fwd.append(hi_lo(t))
-            bwd.append(hi_lo(t.T))
+            bwd.append(np.concatenate(np.split(hi_lo(t.T), 2, axis=1), axis=0))
     return np.stack(fwd), np.stack(bwd)
 
 
@@ -344,7 +344,9 @@
                 y_s[t][c, 1, rows, lanes] = lo
 
     def backward(t, c):
-        g_s[t][c] = dot_three(bwd_ref[c], rows_all, y_s[t][c, 0], y_s[t][c, 1])
+        high = jnp.dot(bwd_ref[c], y_s[t][c, 0], preferred_element_type=F32)
+        low = jnp.dot(bwd_ref[c, :depth, :], y_s[t][c, 1], preferred_element_type=F32)
+        g_s[t][c] = high[:depth] + (high[depth:] + low)
 
     def products(t, i, stat):
         at16 = multiple(i * half, half)
@@ -381,7 +383,7 @@
     places = [
         work(place, j, i, q) for j in range(n) for i in range(per) for q in range(0, field, 16)
     ]
-    lax.fori_loop(0, half, lambda i, carry: fields(0, i) or carry, 0)
+    lax.fori_loop(0, half, lambda i, carry: fields(0, i) or carry, 0, unroll=2)
     copies[1].wait()
     for t in range(nb):
         pieces = places if t == 0 else []
@@ -402,7 +404,9 @@
         else:
             pieces = [work(early_products, b, i) for b in range(nb - 1) for i in range(half)]
         interleave([work(backward, t, c) for c in range(4)], pieces)
-    stats[-1] = lax.fori_loop(0, half, lambda i, stat: products(nb - 1, i, stat), stats[-1])
+    stats[-1] = lax.fori_loop(
+        0, half, lambda i, stat: products(nb - 1, i, stat), stats[-1], unroll=2
+    )
 
     lane = lax.broadcasted_iota(jnp.int32, (1, LANES), 1)
     sums = jnp.zeros((1, LANES), F32)

time: 50.7 us -> 49.4 us (0.974)
  Pallas kernels: 19.7 us -> 18.3 us
    pallas_call x1, Pallas kernels: 16.3 us -> 15 us  [local(): pl.pallas_call(functools.partial(spots_kernel, n, nb, pupil, field), out_...]
where the time goes in v9:
time: 49.4 us; the launch traced here: 49.2 us
  Pallas kernels  18.3 us (37%)
  starting transfers between devices  12.5 us (25%)
  blocking collectives  11.2 us (23%)
  waiting for transfers between devices  6.51 us (13%)
  between operations  0.66 us (1%)
    pallas_call x1, Pallas kernels, local(): pl.pallas_call(functools.partial(spots_kernel, n, nb, pupil, field), out_...  15 us
    ppermute x6, starting transfers between devices, exchange(): lax.ppermute(blocks[j], 'alt', [(i, (i + j) % n) for i in range(n)])  12.5 us
    all_to_all x1, blocking collectives, local(): stat = lax.all_to_all(stat, ('sub', 'alt'), 0, 0, tiled=True)  11.2 us
    ppermute x6, waiting for transfers between devices, exchange(): lax.ppermute(blocks[j], 'alt', [(i, (i + j) % n) for i in range(n)])  6.51 us
    pallas_call x1, Pallas kernels, local(): pl.pallas_call(functools.partial(pack_kernel, n, nb), out_shape=[jax.Shap...  2.37 us
  transfers between devices with their start and end apart: 6, of which 2 were waited for; matrix products, arithmetic and copies ran while one was open for 0% of the time, Pallas kernels for 0%

profile of v9, /device:TPU:0, one launch (start us, length us, event | category | flops | bytes accessed | tf_op | source)
XLA Modules:
  0.0 49.2 jit_solution(7761386234106727632)
XLA Ops:
  0.6 2.4 %pack.1 = (bf16[464,128]{1,0:T(8,128)(2,1)S(1)}, bf16[464,128]{1,0:T(8,128)(2,1)S(1)}, bf16[464,128]{1,0:T(8,128)(2,1)S(1)}, bf16[464,128]{1,0:T(8,128)(2,1)S(1)}) custom-call(s32[1]{0:T(128)} %bitcast.me_ref, f32[2]{0:T(128)} %profile_hbm.1, f32[2]{0:T(128)} %weight_hbm.1, bf16[256,128]{1,0:T(8,128)(2,1)} %amp_hbm.1, f32[256,128]{1,0:T(8,128)} %phase_hbm.1, ...), custom_call_target="tpu_custom_call" | custom-call | tf_op jit(solution)/shard_map/pack/pallas_call | solution.py:482
  3.0 3.1 %collective-permute-start = (bf16[464,128]{1,0:T(8,128)(2,1)S(1)}, bf16[464,128]{1,0:T(8,128)(2,1)S(1)}, u32[]{:S(2)}, u32[]{:S(2)}) collective-permute-start(bf16[464,128]{1,0:T(8,128)(2,1)S(1)} %get-tuple-element.13), channel_id=1, source_target_pairs={{0,1},{1,2},{2,3},{3,0},{4,5},{5,6},{6,7},{7,4},{8,9},{9,10},{10,1... | collective-permute-start | bytes 356360 | tf_op jit(solution)/shard_map/ppermute | solution.py:478
  6.1 2.6 %collective-permute-start.1 = (bf16[464,128]{1,0:T(8,128)(2,1)S(1)}, bf16[464,128]{1,0:T(8,128)(2,1)S(1)}, u32[]{:S(2)}, u32[]{:S(2)}) collective-permute-start(bf16[464,128]{1,0:T(8,128)(2,1)S(1)} %get-tuple-element.14), channel_id=1, source_target_pairs={{0,2},{1,3},{2,0},{3,1},{4,6},{5,7},{6,4},{7,5},{8,10},{9,11},{10,... | collective-permute-start | bytes 356360 | tf_op jit(solution)/shard_map/ppermute | solution.py:478
  8.7 1.3 %collective-permute-start.2 = (bf16[464,128]{1,0:T(8,128)(2,1)S(1)}, bf16[464,128]{1,0:T(8,128)(2,1)S(1)}, u32[]{:S(2)}, u32[]{:S(2)}) collective-permute-start(bf16[464,128]{1,0:T(8,128)(2,1)S(1)} %get-tuple-element.15), channel_id=1, source_target_pairs={{0,3},{1,0},{2,1},{3,2},{4,7},{5,4},{6,5},{7,6},{8,11},{9,8},{10,9... | collective-permute-start | bytes 356360 | tf_op jit(solution)/shard_map/ppermute | solution.py:478
  10.0 2.2 %collective-permute-done.refs_1_ = bf16[464,128]{1,0:T(8,128)(2,1)S(1)} collective-permute-done((bf16[464,128]{1,0:T(8,128)(2,1)S(1)}, bf16[464,128]{1,0:T(8,128)(2,1)S(1)}, u32[]{:S(2)}, u32[]{:S(2)}) %collective-permute-start) | collective-permute-done | bytes 118816 | tf_op jit(solution)/shard_map/ppermute | solution.py:478
  12.3 4.3 %collective-permute-done.1.refs_2_ = bf16[464,128]{1,0:T(8,128)(2,1)S(1)} collective-permute-done((bf16[464,128]{1,0:T(8,128)(2,1)S(1)}, bf16[464,128]{1,0:T(8,128)(2,1)S(1)}, u32[]{:S(2)}, u32[]{:S(2)}) %collective-permute-start.1) | collective-permute-done | bytes 118816 | tf_op jit(solution)/shard_map/ppermute | solution.py:478
  16.5 0.0 collective-permute-done.2.refs_3_
  16.5 15.0 %spots.1 = (f32[64,128]{1,0:T(8,128)S(1)}, f32[64,128]{1,0:T(8,128)S(1)}, f32[64,128]{1,0:T(8,128)S(1)}, f32[64,128]{1,0:T(8,128)S(1)}, f32[8,128]{1,0:T(8,128)S(1)}, /*index=5*/f32[32,128]{1,0:T(8,128)S(1)}) custom-call(s32[1]{0:T(128)} %bitcast.me_ref, f32[2,128]{1,0:T(2,128)} %pos_hbm.1, bf16[4,1024,512]{2,1,0:T(8,128)(2,1)} %constant.8.clone.fwd_hbm, ...), custom_call_target="tpu_custom_call" | custom-call | tf_op jit(solution)/shard_map/spots/pallas_call | solution.py:504
  31.6 3.1 %collective-permute-start.3 = (f32[64,128]{1,0:T(8,128)S(1)}, f32[64,128]{1,0:T(8,128)S(1)}, u32[]{:S(2)}, u32[]{:S(2)}) collective-permute-start(f32[64,128]{1,0:T(8,128)S(1)} %get-tuple-element.19), channel_id=1, source_target_pairs={{0,1},{1,2},{2,3},{3,0},{4,5},{5,6},{6,7},{7,4},{8,9},{9,10},{10,1... | collective-permute-start | bytes 98312 | tf_op jit(solution)/shard_map/ppermute | solution.py:478
  34.6 1.6 %collective-permute-start.4 = (f32[64,128]{1,0:T(8,128)S(1)}, f32[64,128]{1,0:T(8,128)S(1)}, u32[]{:S(2)}, u32[]{:S(2)}) collective-permute-start(f32[64,128]{1,0:T(8,128)S(1)} %get-tuple-element.20), channel_id=1, source_target_pairs={{0,2},{1,3},{2,0},{3,1},{4,6},{5,7},{6,4},{7,5},{8,10},{9,11},{10,... | collective-permute-start | bytes 98312 | tf_op jit(solution)/shard_map/ppermute | solution.py:478
  36.3 0.8 %collective-permute-start.5 = (f32[64,128]{1,0:T(8,128)S(1)}, f32[64,128]{1,0:T(8,128)S(1)}, u32[]{:S(2)}, u32[]{:S(2)}) collective-permute-start(f32[64,128]{1,0:T(8,128)S(1)} %get-tuple-element.21), channel_id=1, source_target_pairs={{0,3},{1,0},{2,1},{3,2},{4,7},{5,4},{6,5},{7,6},{8,11},{9,8},{10,9... | collective-permute-start | bytes 98312 | tf_op jit(solution)/shard_map/ppermute | solution.py:478
  37.1 11.2 %all_to_all.11 = f32[32,1,128]{2,1,0:T(1,128)S(1)} all-to-all(f32[32,1,128]{2,1,0:T(1,128)S(1)} %bitcast.6), channel_id=1, replica_groups=mesh['sub'=8,'alt'=4] {'sub','alt'}, dimensions={0} | all-to-all | bytes 32768 | tf_op jit(solution)/shard_map/all_to_all | solution.py:529
  48.3 0.0 collective-permute-done.3.refs_1_
  48.3 0.0 collective-permute-done.4.refs_2_
  48.3 0.0 collective-permute-done.5.refs_3_
  48.3 0.9 %finish.1 = (f32[256,128]{1,0:T(8,128)}, f32[2]{0:T(128)}) custom-call(s32[1]{0:T(128)} %bitcast.me_ref, f32[8,128]{1,0:T(8,128)S(1)} %get-tuple-element.16.aux_ref, f32[32,128]{1,0:T(8,128)S(1)} %bitcast.5, f32[64,128]{1,0:T(8,128)S(1)} %get-tuple-element.18.refs_0_, f32[64,128]{1,0:T(8,128)S(1)} %collective-permute-done.3.refs_1_, ...), custom_call_target="tpu_custom_call" | custom-call | tf_op jit(solution)/shard_map/finish/pallas_call | solution.py:531
Async XLA Ops:
  3.0 9.3 %collective-permute-start = (bf16[464,128]{1,0:T(8,128)(2,1)S(1)}, bf16[464,128]{1,0:T(8,128)(2,1)S(1)}, u32[]{:S(2)}, u32[]{:S(2)}) collective-permute-start(bf16[464,128]{1,0:T(8,128)(2,1)S(1)} %get-tuple-element.13), channel_id=1, source_target_pairs={{0,1},{1,2},{2,3},{3,0},{4,5},{5,6},{6,7},{7,4},{8,9},{9,10},{10,1... | collective-permute-start | bytes 356360 | tf_op jit(solution)/shard_map/ppermute | solution.py:478
  6.1 10.4 %collective-permute-start.1 = (bf16[464,128]{1,0:T(8,128)(2,1)S(1)}, bf16[464,128]{1,0:T(8,128)(2,1)S(1)}, u32[]{:S(2)}, u32[]{:S(2)}) collective-permute-start(bf16[464,128]{1,0:T(8,128)(2,1)S(1)} %get-tuple-element.14), channel_id=1, source_target_pairs={{0,2},{1,3},{2,0},{3,1},{4,6},{5,7},{6,4},{7,5},{8,10},{9,11},{10,... | collective-permute-start | bytes 356360 | tf_op jit(solution)/shard_map/ppermute | solution.py:478
  8.7 7.9 %collective-permute-start.2 = (bf16[464,128]{1,0:T(8,128)(2,1)S(1)}, bf16[464,128]{1,0:T(8,128)(2,1)S(1)}, u32[]{:S(2)}, u32[]{:S(2)}) collective-permute-start(bf16[464,128]{1,0:T(8,128)(2,1)S(1)} %get-tuple-element.15), channel_id=1, source_target_pairs={{0,3},{1,0},{2,1},{3,2},{4,7},{5,4},{6,5},{7,6},{8,11},{9,8},{10,9... | collective-permute-start | bytes 356360 | tf_op jit(solution)/shard_map/ppermute | solution.py:478
  31.6 16.7 %collective-permute-start.3 = (f32[64,128]{1,0:T(8,128)S(1)}, f32[64,128]{1,0:T(8,128)S(1)}, u32[]{:S(2)}, u32[]{:S(2)}) collective-permute-start(f32[64,128]{1,0:T(8,128)S(1)} %get-tuple-element.19), channel_id=1, source_target_pairs={{0,1},{1,2},{2,3},{3,0},{4,5},{5,6},{6,7},{7,4},{8,9},{9,10},{10,1... | collective-permute-start | bytes 98312 | tf_op jit(solution)/shard_map/ppermute | solution.py:478
  34.6 13.6 %collective-permute-start.4 = (f32[64,128]{1,0:T(8,128)S(1)}, f32[64,128]{1,0:T(8,128)S(1)}, u32[]{:S(2)}, u32[]{:S(2)}) collective-permute-start(f32[64,128]{1,0:T(8,128)S(1)} %get-tuple-element.20), channel_id=1, source_target_pairs={{0,2},{1,3},{2,0},{3,1},{4,6},{5,7},{6,4},{7,5},{8,10},{9,11},{10,... | collective-permute-start | bytes 98312 | tf_op jit(solution)/shard_map/ppermute | solution.py:478
  36.3 12.0 %collective-permute-start.5 = (f32[64,128]{1,0:T(8,128)S(1)}, f32[64,128]{1,0:T(8,128)S(1)}, u32[]{:S(2)}, u32[]{:S(2)}) collective-permute-start(f32[64,128]{1,0:T(8,128)S(1)} %get-tuple-element.21), channel_id=1, source_target_pairs={{0,3},{1,0},{2,1},{3,2},{4,7},{5,4},{6,5},{7,6},{8,11},{9,8},{10,9... | collective-permute-start | bytes 98312 | tf_op jit(solution)/shard_map/ppermute | solution.py:478
